TPU v7x, 512 devices: a whole 4x4x16 slice. The times are simulated.
512 devices in a mesh: ctx: 32 (over z, x_hi), tp: 16 (over x_lo, y, core).
Axes of the slice: x: 4 (x_hi: 2, x_lo: 2; x = x_hi * 2 + x_lo), y: 4, z: 16, core: 2. Of those that a mesh axis runs over, the one named last changes fastest.
Arguments:
- token_ids: int32 [2, 16384], P(None, 'ctx'), may hold values from 0 to 511
- lengths: int32 [2], replicated, may hold values from 8192 to 16384, as said below
- embedding: bfloat16 [512, 8192], P(None, 'tp'), may hold values from -6 to 6
- query_act: bfloat16 [2, 16384, 8192], P(None, 'ctx', 'tp'), may hold values from -11 to 11
- key_act: bfloat16 [2, 16384, 8192], P(None, 'ctx', 'tp'), may hold values from -6 to 6
- value_act: bfloat16 [2, 16384, 8192], P(None, 'ctx', 'tp'), may hold values from -6 to 6
- short_filter: bfloat16 [512, 128], P('tp'), may hold values from -0.5 to 0.5
- decay_rates: float32 [512, 16], P('tp'), may hold values from 0 to 1
- residues: float32 [512, 16], P('tp'), may hold values from -1 to 1
- skip_gain: float32 [8192], P('tp'), may hold values from 0.5 to 1.5
- norm_gain: float32 [8192], P('tp'), may hold values from 0.25 to 1.75
Outputs:
- scored: bfloat16 [2, 16384, 8192], P(None, 'ctx', 'tp')
Inputs may be any that keep to these rules, and one draw needn't show every extreme that they name: `lengths`: one sample has the full length 16384.
All inputs are finite; a program needn't handle non-finite values.
Results may differ from a plain program's by a relative error of at most 0.0065.
Values may be sent and summed in bfloat16 or wider, within the bound.
No kernel may reach another device: no remote copies, remote signals or barrier semaphores. Data moves between devices by JAX's collectives and lax.ppermute only.
A program may use at most 64 MiB of HBM per device.

v0:
```python
import jax
import jax.numpy as jnp
from jax import lax
from jax.sharding import PartitionSpec as P

D = 8192
GROUP = 16


def shifted(shard, axis, by):
    size = lax.axis_size(axis)
    pairs = [(i, i + by) for i in range(size) if 0 <= i + by < size]
    return lax.ppermute(shard, axis, pairs)


def to_lanes(blocks):
    samples_here, block_count, taps, groups_here, members = blocks.shape
    moved = jnp.transpose(blocks, (3, 2, 0, 1, 4))
    return moved.reshape(groups_here, taps, samples_here * block_count * members)


def from_lanes(flat, samples_here, block_count, members):
    groups_here, taps, _ = flat.shape
    shaped = flat.reshape(groups_here, taps, samples_here, block_count, members)
    return jnp.transpose(shaped, (2, 3, 1, 0, 4))


def split_product(form, weights, signal):
    upper = weights.astype(jnp.bfloat16)
    lower = (weights - upper.astype(jnp.float32)).astype(jnp.bfloat16)
    first = jnp.einsum(form, upper, signal, preferred_element_type=jnp.float32)
    return first + jnp.einsum(form, lower, signal, preferred_element_type=jnp.float32)


def lag_table(taps, shift_by, dtype):
    offset = jnp.arange(taps)[:, None] - jnp.arange(taps)[None, :] + shift_by
    lags = jnp.arange(taps)
    return (offset[None, :, :] == lags[:, None, None]).astype(dtype)


def short_conv(extended, short_filter):
    samples_here, total_rows, width = extended.shape
    taps = short_filter.shape[1]
    groups_here = short_filter.shape[0]
    members = width // groups_here
    blocks = extended.reshape(samples_here, total_rows // taps, taps, groups_here, members)
    current = jnp.einsum(
        "gl,lij->gij",
        short_filter,
        lag_table(taps, 0, jnp.bfloat16),
        preferred_element_type=jnp.float32,
    ).astype(jnp.bfloat16)
    earlier = jnp.einsum(
        "gl,lij->gij",
        short_filter,
        lag_table(taps, taps, jnp.bfloat16),
        preferred_element_type=jnp.float32,
    ).astype(jnp.bfloat16)
    block_count = total_rows // taps - 1
    result = jnp.einsum(
        "gij,gjx->gix", current, to_lanes(blocks[:, 1:]), preferred_element_type=jnp.float32
    )
    result = result + jnp.einsum(
        "gij,gjx->gix", earlier, to_lanes(blocks[:, :-1]), preferred_element_type=jnp.float32
    )
    return from_lanes(result, samples_here, block_count, members).reshape(
        samples_here, total_rows - taps, width
    )


def modal_conv(blocks, rate_part, residue_part):
    samples_here, block_count, block_rows, groups_here, members = blocks.shape
    highest = lax.Precision.HIGHEST
    lag_values = jnp.arange(block_rows).astype(jnp.float32)
    decay_table = jnp.exp(-rate_part[:, :, None] * lag_values)
    kernel_head = jnp.einsum("gm,gml->gl", residue_part, decay_table, precision=highest)
    toeplitz = jnp.einsum(
        "gl,lij->gij", kernel_head, lag_table(block_rows, 0, jnp.float32), precision=highest
    )
    signal = to_lanes(blocks)
    inner = split_product("gij,gjx->gix", toeplitz, signal)
    inner = from_lanes(inner, samples_here, block_count, members)
    end_weights = jnp.exp(-rate_part[:, :, None] * (block_rows - 1.0 - lag_values))
    states = split_product("gmj,gjx->gmx", end_weights, signal)
    states = states.reshape(groups_here, rate_part.shape[1], samples_here, block_count, members)
    block_ids = jnp.arange(block_count)
    block_gap = block_ids[:, None] - 1 - block_ids[None, :]
    gap_rows = (block_rows * jnp.maximum(block_gap, 0)).astype(jnp.float32)
    across = jnp.where(block_gap >= 0, jnp.exp(-rate_part[:, :, None, None] * gap_rows), 0.0)
    carried = jnp.einsum("gmnk,gmskc->gmsnc", across, states, precision=highest)
    start_weights = jnp.exp(-rate_part[:, :, None] * (lag_values + 1.0)) * residue_part[:, :, None]
    outer = jnp.einsum("gmi,gmsnc->snigc", start_weights, carried, precision=highest)
    remaining = (block_rows * (block_count - 1 - block_ids)).astype(jnp.float32)
    tail_weights = jnp.exp(-rate_part[:, :, None] * remaining)
    ending = jnp.einsum("gmn,gmsnc->sgmc", tail_weights, states, precision=highest)
    return (inner + outer, start_weights, ending)


def per_device(
    token_ids,
    lengths,
    embedding,
    query_act,
    key_act,
    value_act,
    short_filter,
    decay_rates,
    residues,
    skip_gain,
    norm_gain,
):
    samples_here, rows_here, width = query_act.shape
    taps = short_filter.shape[1]
    product = (key_act.astype(jnp.float32) * value_act.astype(jnp.float32)).astype(jnp.bfloat16)
    border = shifted(product[:, rows_here - taps :, :], "ctx", 1)
    mixed = short_conv(jnp.concatenate([border, product], axis=1), short_filter).astype(
        jnp.bfloat16
    )
    received = lax.all_to_all(mixed, "ctx", split_axis=2, concat_axis=1, tiled=True)
    count_here, full_rows, columns = received.shape
    local_groups = columns // GROUP
    group_start = lax.axis_index("ctx") * local_groups
    rate_part = lax.dynamic_slice_in_dim(decay_rates, group_start, local_groups, 0)
    residue_part = lax.dynamic_slice_in_dim(residues, group_start, local_groups, 0)
    blocks = received.reshape(count_here, full_rows // taps, taps, local_groups, GROUP)
    convolved, start_weights, ending = modal_conv(blocks, rate_part, residue_part)
    returned = convolved.reshape(count_here, full_rows, columns).astype(jnp.bfloat16)
    filtered = lax.all_to_all(returned, "ctx", split_axis=1, concat_axis=2, tiled=True)
    gated = query_act.astype(jnp.float32) * (
        filtered.astype(jnp.float32) + skip_gain * mixed.astype(jnp.float32)
    )
    square_total = lax.psum(jnp.sum(gated * gated, axis=2), "tp")
    inverse_rms = lax.rsqrt(square_total / D + 1e-06)
    normed = gated * inverse_rms[:, :, None] * norm_gain
    one_hot = (token_ids[:, :, None] == jnp.arange(embedding.shape[0])[None, None, :]).astype(
        jnp.bfloat16
    )
    embedded = jnp.einsum("stv,vd->std", one_hot, embedding, preferred_element_type=jnp.float32)
    position = lax.axis_index("ctx") * rows_here + jnp.arange(rows_here)
    valid = position[None, :] < lengths[:, None]
    return jnp.where(valid[:, :, None], embedded + normed, 0.0).astype(jnp.bfloat16)


def solution(mesh):
    placed = (
        P(None, "ctx"),
        P(),
        P(None, "tp"),
        P(None, "ctx", "tp"),
        P(None, "ctx", "tp"),
        P(None, "ctx", "tp"),
        P("tp", None),
        P("tp", None),
        P("tp", None),
        P("tp"),
        P("tp"),
    )
    return jax.shard_map(
        per_device, mesh=mesh, in_specs=placed, out_specs=P(None, "ctx", "tp"), check_vma=False
    )
```

profile of v0, /device:TPU:1, one launch (start us, length us, event | category | flops | bytes accessed | tf_op | source)
XLA Modules:
  0.0 260.9 jit_solution(10494251787485676510)
XLA Ops:
  0.0 0.0 copy-start
  0.0 1.9 multiply_convert_fusion
  1.9 5.5 %collective-permute-start = (bf16[2,128,512]{2,1,0:T(8,128)(2,1)S(1)}, bf16[2,128,512]{2,1,0:T(8,128)(2,1)S(1)}, u32[]{:S(2)}, u32[]{:S(2)}) collective-permute-start(bf16[2,128,512]{2,1,0:T(8,128)(2,1)S(1)} %slice.12), channel_id=1, source_target_pairs={{0,16},{16,32},{32,48},{48,64},{64,80},{80,96},{96,112},{112,128},... | collective-permute-start | bytes 786440 | tf_op jit(solution)/shard_map/ppermute | solution.py:13
  7.5 0.0 copy-done.8
  7.5 2.8 %fusion.10 = bf16[32,128,128]{2,0,1:T(8,128)(2,1)} fusion(s32[128,128]{1,0:T(8,128)S(1)} %iota_subtract_fusion.1, bf16[32,128]{1,0:T(8,128)(2,1)S(1)} %copy-done.8), kind=kOutput, calls=%fused_computation.21 | convolution fusion | flops 136839168 | bytes 1122304 | tf_op jit(solution)/shard_map/gl,lij->gij/dot_general | solution.py:47
  10.2 2.8 %fusion.11 = bf16[32,128,128]{2,0,1:T(8,128)(2,1)} fusion(s32[128,128]{1,0:T(8,128)S(1)} %broadcast_add_fusion, bf16[32,128]{1,0:T(8,128)(2,1)S(1)} %copy-done.8), kind=kOutput, calls=%fused_computation.22 | convolution fusion | flops 136839168 | bytes 1122304 | tf_op jit(solution)/shard_map/gl,lij->gij/dot_general | solution.py:53
  13.0 0.0 collective-permute-done
  13.0 0.1 pad_maximum_fusion
  13.1 1.5 copy.50
  14.5 3.1 %reshape.500 = bf16[2,5,128,32,16]{2,1,4,3,0:T(8,128)(2,1)S(1)} reshape(bf16[2,640,512]{1,2,0:T(8,128)(2,1)} %copy.50) | data formatting | bytes 2621440 | tf_op jit(solution)/shard_map/reshape | solution.py:46
  17.6 1.2 slice_bitcast_fusion
  18.8 0.0 copy-start.3
  18.9 0.3 copy.51
  19.1 0.3 copy.53
  19.4 0.7 copy-done.3
  20.1 0.9 fusion.14
  21.0 0.3 copy-done.2
  21.3 0.9 add_convert_fusion
  22.2 0.5 copy.83
  22.7 0.4 convert_element_type.186
  23.1 0.0 copy-start.4
  23.2 0.0 copy-start.5
  23.2 2.0 copy.56
  25.2 18.2 %all-to-all-start = ((bf16[2,512,512]{1,0,2:T(2,128)(2,1)}), bf16[2,512,512]{1,0,2:T(2,128)(2,1)S(1)}, u32[]{:S(2)}, u32[]{:S(2)}) async-start(bf16[2,512,512]{1,0,2:T(2,128)(2,1)} %copy.56), calls=%async_computation | async-start | bytes 2097152 | tf_op jit(solution)/shard_map/all_to_all | solution.py:119
  43.4 0.0 copy-done.4
  43.4 0.0 copy-done.5
  43.4 0.2 negate_reduce_fusion
  43.7 0.2 convolution_bitcast_fusion.1
  43.9 0.1 fusion.26
  44.0 0.1 multiply_convert_fusion.1
  44.0 2.7 %fusion.1 = f32[1,128,128]{2,0,1:T(1,128)S(1)} fusion(f32[128,1,1]{0,1,2:T(1,128)S(1)} %convolution_bitcast_fusion.1, s32[128,128]{1,0:T(8,128)S(1)} %iota_subtract_fusion.1), kind=kOutput, calls=%fused_computation.3 | convolution fusion | flops 27262976 | bytes 131584 | tf_op jit(solution)/shard_map/gl,lij->gij/dot_general | solution.py:77
  46.7 48.3 %all-to-all-done = bf16[2,512,512]{1,0,2:T(2,128)(2,1)S(1)} async-done(((bf16[2,512,512]{1,0,2:T(2,128)(2,1)}), bf16[2,512,512]{1,0,2:T(2,128)(2,1)S(1)}, u32[]{:S(2)}, u32[]{:S(2)}) %all-to-all-start) | async-done | bytes 1048608 | tf_op jit(solution)/shard_map/all_to_all | solution.py:119
  95.1 0.2 copy.57
  95.2 0.6 copy.58
  95.8 1.4 reshape.503
  97.3 1.9 copy.59
  99.2 0.4 fusion.28
  99.6 1.8 convolution_add_fusion
  101.4 2.9 %copy.60 = f32[128,4096]{0,1:T(8,128)} copy(f32[128,4096]{1,0:T(8,128)} %convolution_add_fusion) | data formatting | bytes 4194304 | tf_op jit(solution)/shard_map/add | solution.py:32
  104.3 0.4 fusion.43
  104.7 0.4 convolution_add_fusion.1
  105.2 2.1 reshape.506
  107.2 5.2 %convolution_bitcast_fusion = f32[16,2,128,16]{2,3,1,0:T(8,128)S(1)} fusion(f32[16,2,128,16]{3,2,1,0:T(8,128)} %reshape.506, f32[128,128]{1,0:T(8,128)S(1)} %multiply_convert_fusion.1, f32[16]{0:T(128)S(1)} %get-tuple-element.7, pred[128,128]{1,0:T(8,128)(4,1)S(1)} %fusion.26), kind=kOutput, calls=%fused_computation.24 | convolution fusion | flops 101187584 | bytes 606272 | tf_op jit(solution)/shard_map/gmnk,gmskc->gmsnc/dot_general | solution.py:90
  112.4 0.0 copy-done.1
  112.4 4.0 %fusion.6 = bf16[2,128,128,1,16]{2,1,4,0,3:T(8,128)(2,1)S(1)} fusion(f32[1,128,2,128,16]{1,4,3,2,0:T(8,128)S(1)} %bitcast.106, f32[16,2,128,16]{2,3,1,0:T(8,128)S(1)} %convolution_bitcast_fusion, f32[16]{0:T(128)S(1)} %get-tuple-element.8, f32[128]{0:T(128)S(1)} %broadcast_add_fusion.1, f32[16]{0:T(128)S(1)} %get-tuple-element.7), kind=kOutput, calls=%fused_computation.11 | convolution fusion | flops 101715968 | bytes 3408512 | tf_op jit(solution)/shard_map/gmi,gmsnc->snigc/dot_general | solution.py:92
  116.4 9.2 %copy.73 = bf16[2,128,128,1,16]{4,0,2,1,3:T(2,128)(2,1)} copy(bf16[2,128,128,1,16]{2,1,4,0,3:T(8,128)(2,1)S(1)} %fusion.6) | data formatting | bytes 2097152 | tf_op jit(solution)/shard_map/convert_element_type | solution.py:127
  125.5 11.2 %reshape.522 = bf16[32,2,8192]{2,1,0:T(2,128)(2,1)} reshape(bf16[16384,2,16]{2,1,0:T(2,128)(2,1)} %bitcast.100) | data formatting | bytes 2097152
  136.7 8.7 %all-to-all-start.1 = ((bf16[32,2,8192]{2,1,0:T(2,128)(2,1)}), bf16[32,2,8192]{2,1,0:T(2,128)(2,1)S(1)}, u32[]{:S(2)}, u32[]{:S(2)}) async-start(bf16[32,2,8192]{2,1,0:T(2,128)(2,1)} %reshape.522), calls=%async_computation.1 | async-start | bytes 2097152 | tf_op jit(solution)/shard_map/all_to_all | solution.py:128
  145.5 0.0 copy-done.7
  145.5 0.1 broadcast_compare_fusion
  145.5 1.4 copy.67
  146.9 51.4 %all-to-all-done.1 = bf16[32,2,8192]{2,1,0:T(2,128)(2,1)S(1)} async-done(((bf16[32,2,8192]{2,1,0:T(2,128)(2,1)}), bf16[32,2,8192]{2,1,0:T(2,128)(2,1)S(1)}, u32[]{:S(2)}, u32[]{:S(2)}) %all-to-all-start.1) | async-done | bytes 1048608 | tf_op jit(solution)/shard_map/all_to_all | solution.py:128
  198.3 7.5 %reshape.523 = bf16[16384,2,16]{2,1,0:T(2,128)(2,1)} reshape(bf16[32,2,8192]{2,1,0:T(2,128)(2,1)S(1)} %all-to-all-done.1) | data formatting | bytes 2097152
  205.8 15.4 %copy.65 = bf16[2,16384,16]{1,2,0:T(8,128)(2,1)S(1)} copy(bf16[2,16384,16]{2,0,1:T(2,128)(2,1)} %bitcast.101) | data formatting | bytes 2097152 | tf_op jit(solution)/shard_map/all_to_all | solution.py:128
  221.2 0.1 convert_element_type.205
  221.4 1.2 copy.74
  222.6 2.6 copy.66
  225.2 1.9 copy.68
  227.1 0.0 copy-done.6
  227.1 0.0 copy-start.9
  227.1 0.0 copy-start.10
  227.2 2.1 multiply_reduce_fusion
  229.3 28.2 %psum.7 = f32[2,512]{1,0:T(2,128)S(1)} all-reduce(f32[2,512]{1,0:T(2,128)S(1)} %multiply_reduce_fusion), channel_id=1, replica_groups=mesh['ctx'=32,'tp'=16] {'tp'}, use_global_device_ids=true, to_apply=%region_1.2 | all-reduce | flops 1024 | bytes 8192 | tf_op jit(solution)/shard_map/psum | solution.py:132
  257.5 3.4 %select_convert_fusion = bf16[2,512,512]{2,1,0:T(8,128)(2,1)} fusion(f32[512]{0:T(512)S(1)} %copy-done.10, f32[2,512]{1,0:T(2,128)S(1)} %add_rsqrt_fusion, s32[2,512]{1,0:T(2,128)S(1)} %copy-done.9, pred[2,512]{1,0:T(4,128)(4,1)S(1)} %broadcast_compare_fusion, f32[2,512,512]{2,1,0:T(8,128)S(1)} %copy.68, bf16[2,512,512]{2,1,0:T(8,128)(2,1)} %copy.67, ...), kind=kOutput, calls=%fused_computation.12 | convolution fusion | flops 542638080 | bytes 5780480 | tf_op jit(solution)/shard_map/stv,vd->std/dot_general | solution.py:138
  (17 shorter events, 0.1 us)
Async XLA Ops:
  0.0 257.5 %copy-start = (bf16[512,512]{1,0:T(8,128)(2,1)S(1)}, bf16[512,512]{1,0:T(8,128)(2,1)}, u32[]{:S(2)}) copy-start(bf16[512,512]{1,0:T(8,128)(2,1)} %param.13) | copy-start | bytes 1572868
  0.0 7.4 %copy-start.8 = (bf16[32,128]{1,0:T(8,128)(2,1)S(1)}, bf16[32,128]{1,0:T(8,128)(2,1)}, u32[]{:S(2)}) copy-start(bf16[32,128]{1,0:T(8,128)(2,1)} %param.17) | copy-start | bytes 24580
  1.9 11.1 %collective-permute-start = (bf16[2,128,512]{2,1,0:T(8,128)(2,1)S(1)}, bf16[2,128,512]{2,1,0:T(8,128)(2,1)S(1)}, u32[]{:S(2)}, u32[]{:S(2)}) collective-permute-start(bf16[2,128,512]{2,1,0:T(8,128)(2,1)S(1)} %slice.12), channel_id=1, source_target_pairs={{0,16},{16,32},{32,48},{48,64},{64,80},{80,96},{96,112},{112,128},... | collective-permute-start | bytes 786440 | tf_op jit(solution)/shard_map/ppermute | solution.py:13
  18.8 1.2 copy-start.3
  20.1 1.2 copy-start.2
  23.1 20.3 %copy-start.4 = (f32[32,16]{0,1:T(8,128)S(1)}, f32[32,16]{0,1:T(8,128)}, u32[]{:S(2)}) copy-start(f32[32,16]{0,1:T(8,128)} %param.18) | copy-start | bytes 6148
  23.2 20.3 %copy-start.5 = (f32[32,16]{0,1:T(8,128)S(1)}, f32[32,16]{0,1:T(8,128)}, u32[]{:S(2)}) copy-start(f32[32,16]{0,1:T(8,128)} %param.19) | copy-start | bytes 6148
  25.2 69.8 %all-to-all-start = ((bf16[2,512,512]{1,0,2:T(2,128)(2,1)}), bf16[2,512,512]{1,0,2:T(2,128)(2,1)S(1)}, u32[]{:S(2)}, u32[]{:S(2)}) async-start(bf16[2,512,512]{1,0,2:T(2,128)(2,1)} %copy.56), calls=%async_computation | async-start | bytes 2097152 | tf_op jit(solution)/shard_map/all_to_all | solution.py:119
  107.2 5.2 %copy-start.1 = (f32[128,4096]{0,1:T(8,128)S(1)}, f32[128,4096]{0,1:T(8,128)}, u32[]{:S(2)}) copy-start(f32[128,4096]{0,1:T(8,128)} %copy.60) | copy-start | bytes 6291460
  136.7 8.7 %copy-start.7 = (s32[2]{0:T(128)S(1)}, s32[2]{0:T(128)}, u32[]{:S(2)}) copy-start(s32[2]{0:T(128)} %param.12) | copy-start | bytes 28
  136.7 61.5 %all-to-all-start.1 = ((bf16[32,2,8192]{2,1,0:T(2,128)(2,1)}), bf16[32,2,8192]{2,1,0:T(2,128)(2,1)S(1)}, u32[]{:S(2)}, u32[]{:S(2)}) async-start(bf16[32,2,8192]{2,1,0:T(2,128)(2,1)} %reshape.522), calls=%async_computation.1 | async-start | bytes 2097152 | tf_op jit(solution)/shard_map/all_to_all | solution.py:128
  225.2 1.9 copy-start.6
  227.1 30.4 %copy-start.9 = (s32[2,512]{1,0:T(2,128)S(1)}, s32[2,512]{1,0:T(2,128)}, u32[]{:S(2)}) copy-start(s32[2,512]{1,0:T(2,128)} %param.11) | copy-start | bytes 12292
  227.1 30.4 %copy-start.10 = (f32[512]{0:T(512)S(1)}, f32[512]{0:T(512)}, u32[]{:S(2)}) copy-start(f32[512]{0:T(512)} %param.21) | copy-start | bytes 6148
where the time goes:
time: 264 us; the launch traced here: 261 us
  waiting for transfers between devices  99.7 us (38%)
  local copies, waits for them, and re-layouts  69.8 us (26%)
  starting transfers between devices  32.4 us (12%)
  blocking collectives  28.2 us (11%)
  matrix products  25.7 us (10%)
  other arithmetic  4.71 us (2%)
    all_to_all x1, waiting for transfers between devices, per_device(): lax.all_to_all(returned, 'ctx', split_axis=1, concat_axis=2, tiled=True)  51.4 us
    all_to_all x1, waiting for transfers between devices, per_device(): lax.all_to_all(mixed, 'ctx', split_axis=2, concat_axis=1, tiled=True)  48.3 us
    psum x1, blocking collectives, per_device(): square_total = lax.psum(jnp.sum(gated * gated, axis=2), 'tp')  28.2 us
    unnamed x25, local copies, waits for them, and re-layouts  21 us
    all_to_all x1, starting transfers between devices, per_device(): lax.all_to_all(mixed, 'ctx', split_axis=2, concat_axis=1, tiled=True)  18.2 us
    all_to_all x1, local copies, waits for them, and re-layouts, per_device(): lax.all_to_all(returned, 'ctx', split_axis=1, concat_axis=2, tiled=True)  15.4 us
    convert_element_type x1, local copies, waits for them, and re-layouts, per_device(): convolved.reshape(count_here, full_rows, columns).astype(jnp.bfloat16)  9.16 us
    all_to_all x1, starting transfers between devices, per_device(): lax.all_to_all(returned, 'ctx', split_axis=1, concat_axis=2, tiled=True)  8.69 us
  transfers between devices with their start and end apart: 3, of which 2 were waited for; matrix products, arithmetic and copies ran while one was open for 4% of the time, Pallas kernels for 0%

commit v1 on v0

v1 whole, which is shorter than its diff:
```python
import jax
import jax.numpy as jnp
from jax import lax
from jax.experimental import pallas as pl
from jax.experimental.pallas import tpu as pltpu
from jax.sharding import PartitionSpec as P

GROUP = 16
LANES = 128
TILE_GROUPS = LANES // GROUP
F32 = jnp.float32
BF16 = jnp.bfloat16


def iota(shape, dim, dtype=jnp.int32):
    return lax.broadcasted_iota(jnp.int32, shape, dim).astype(dtype)


def column(values):
    groups, modes = values.shape
    spread = jnp.broadcast_to(values[:, None, :], (groups, modes, modes))
    same = iota(spread.shape, 1) == iota(spread.shape, 2)
    picked = jnp.sum(jnp.where(same, spread, 0.0), axis=2, keepdims=True)
    return picked.reshape(groups * modes, 1)


def own_group(stacked, rows):
    lane_group = iota((rows, LANES), 1) // GROUP
    picked = stacked[:rows]
    for g in range(1, TILE_GROUPS):
        picked = jnp.where(lane_group == g, stacked[g * rows : (g + 1) * rows], picked)
    return picked


def halves(values):
    upper = values.astype(BF16)
    return upper, (values - upper.astype(F32)).astype(BF16)


def dot(a, b):
    return jnp.dot(a, b, preferred_element_type=F32)


def states_kernel(key_ref, value_ref, rate_ref, product_ref, state_ref, border_ref):
    samples, rows, _ = key_ref.shape
    taps = 128
    modes = rate_ref.shape[1]
    rate = column(rate_ref[...])
    weights = jnp.exp(-rate * (rows - 1.0 - iota((1, rows), 1, F32)))
    weights = jnp.concatenate(halves(weights), axis=0)
    half = weights.shape[0] // 2
    for s in range(samples):
        product = (key_ref[s].astype(F32) * value_ref[s].astype(F32)).astype(BF16)
        product_ref[s] = product
        full = dot(weights, product)
        state_ref[s * modes : (s + 1) * modes, :] = own_group(full[:half] + full[half:], modes)
        early = dot(weights[:, taps:], product[: rows - taps])
        upper, lower = halves(own_group(early[:half] + early[half:], modes))
        border_ref[s * taps : (s + 1) * taps, :] = product[rows - taps :]
        first = samples * taps + s * modes
        border_ref[first : first + modes, :] = upper
        border_ref[first + samples * modes : first + (samples + 1) * modes, :] = lower


def scan_kernel(first_ref, rate_ref, state_ref, out_ref, *, chunks, rows):
    total, width = state_ref.shape
    each = total // chunks
    groups, modes = rate_ref.shape
    rates = rate_ref[...]
    for r in range(each):
        mode = lax.rem(first_ref[0] * each + r, modes)
        picked = jnp.sum(
            jnp.where(iota(rates.shape, 1) == mode, rates, 0.0), axis=1, keepdims=True
        )
        at_group = iota((groups, width), 0) == iota((groups, width), 1) // GROUP
        rate = jnp.sum(jnp.where(at_group, picked, 0.0), axis=0, keepdims=True)
        decay = jnp.exp(-rate * float(rows))
        held = jnp.zeros((1, width), F32)
        out_ref[r : r + 1, :] = held
        for n in range(1, chunks):
            out_ref[n * each + r : n * each + r + 1, :] = held
            held = decay * held + state_ref[(n - 1) * each + r : (n - 1) * each + r + 1, :]


def local_kernel(
    product_ref,
    border_ref,
    filter_ref,
    rate_ref,
    residue_ref,
    mixed_ref,
    local_ref,
    upper_ref,
    lower_ref,
    factor_ref,
    short_table,
    long_table,
    product_window,
    mixed_window,
):
    samples, rows, _ = product_ref.shape
    modes = rate_ref.shape[1]
    taps = 128
    span = rows + taps
    blocks = rows // taps
    rate = column(rate_ref[...])
    residue = column(residue_ref[...])
    filters = filter_ref[...]

    reverse = (iota((taps, 2 * taps), 0) + iota((taps, 2 * taps), 1) == taps).astype(BF16)
    short_base = dot(filters, reverse)
    wide = span + taps
    place = iota((1, wide), 1)
    lag = jnp.where(place <= rows, rows - place, rows + wide - place)
    zero = jnp.logical_and(place > rows, place <= rows + taps)
    modal = residue * jnp.exp(-rate * lag.astype(F32))
    modal = jnp.where(zero, 0.0, modal)
    long_base = jnp.sum(modal.reshape(TILE_GROUPS, modes, wide), axis=1)
    for g in range(TILE_GROUPS):
        spread = jnp.broadcast_to(short_base[g : g + 1], (taps, 2 * taps))
        rolled = pltpu.roll(spread, 0, 1, stride=1, stride_axis=0)
        short_table[g * taps : (g + 1) * taps, :] = rolled.astype(BF16)
        spread = jnp.broadcast_to(long_base[g : g + 1], (taps, wide))
        rolled = pltpu.roll(spread, 0, 1, stride=1, stride_axis=0)
        long_table[g * taps : (g + 1) * taps, :] = rolled[:, :span].astype(BF16)

    for s in range(samples):
        product_window[s, 0:taps, :] = jnp.zeros((taps, LANES), BF16)
        product_window[s, taps : 2 * taps, :] = border_ref[s * taps : (s + 1) * taps, :]
        product_window[s, 2 * taps :, :] = product_ref[s]

    def short_step(step, _):
        s = step // (blocks + 1)
        first = pl.multiple_of(lax.rem(step, blocks + 1) * taps, taps)
        full = dot(short_table[...], product_window[s, pl.ds(first, 2 * taps), :])
        mixed_window[s, pl.ds(first, taps), :] = own_group(full, taps).astype(BF16)
        return _

    lax.fori_loop(0, samples * (blocks + 1), short_step, 0)

    def long_step(s, _):
        mixed_ref[s] = mixed_window[s, taps:, :]
        for b in range(1, blocks + 1):
            full = dot(long_table[:, (blocks - b) * taps :], mixed_window[s, : (b + 1) * taps, :])
            local_ref[s, (b - 1) * taps : b * taps, :] = own_group(full, taps)
        return _

    lax.fori_loop(0, samples, long_step, 0)

    after = jnp.exp(-rate * (1.0 + iota((1, rows), 1, F32)))
    upper, lower = halves(after.T)
    upper_ref[...] = upper
    lower_ref[...] = lower
    tap_weights = jnp.exp(-rate * (taps - iota((1, taps), 1, F32)))
    spread = jnp.broadcast_to(
        filters.astype(F32)[:, None, :], (TILE_GROUPS, modes, taps)
    ).reshape(TILE_GROUPS * modes, taps)
    gain = residue * jnp.sum(spread * tap_weights, axis=1, keepdims=True)
    square = (TILE_GROUPS * modes, LANES)
    factor_ref[:modes, :] = own_group(
        jnp.broadcast_to(jnp.exp(-rate * float(rows - taps)), square), modes
    )
    factor_ref[modes:, :] = own_group(jnp.broadcast_to(gain, square), modes)


def embed_kernel(token_ref, table_ref, out_ref):
    samples, rows = token_ref.shape
    vocab = table_ref.shape[0]
    for s in range(samples):
        ids = jnp.broadcast_to(token_ref[s : s + 1, :].astype(F32), (8, rows)).T[:, :1]
        one_hot = (ids == iota((rows, vocab), 1, F32)).astype(BF16)
        out_ref[s] = dot(one_hot, table_ref[...]).astype(BF16)


def gate_kernel(
    carried_ref,
    early_ref,
    factor_ref,
    upper_ref,
    lower_ref,
    local_ref,
    mixed_ref,
    query_ref,
    skip_ref,
    gated_ref,
    sum_ref,
    squares,
):
    samples, rows, _ = local_ref.shape
    modes = factor_ref.shape[0] // 2
    copies = sum_ref.shape[0]
    step = pl.program_id(0)
    own = iota((LANES, LANES), 0) // modes == iota((LANES, LANES), 1) // GROUP
    early = early_ref[...].astype(F32)
    early = early[: samples * modes] + early[samples * modes :]
    skip = skip_ref[...]
    for s in range(samples):
        part = slice(s * modes, (s + 1) * modes)
        state = factor_ref[:modes, :] * carried_ref[part, :] + early[part]
        state = state * factor_ref[modes:, :]
        spread = jnp.concatenate([state] * TILE_GROUPS, axis=0)
        upper, lower = halves(jnp.where(own, spread, 0.0))
        carry = (
            dot(upper_ref[...], upper) + dot(upper_ref[...], lower) + dot(lower_ref[...], upper)
        )
        filtered = (local_ref[s] + carry).astype(BF16).astype(F32)
        gated = query_ref[s].astype(F32) * (filtered + skip * mixed_ref[s].astype(F32))
        gated_ref[s] = gated
        square = gated * gated

        @pl.when(step == 0)
        def _():
            squares[s] = square

        @pl.when(step > 0)
        def _():
            squares[s] = squares[s] + square

    @pl.when(step == pl.num_programs(0) - 1)
    def _():
        for s in range(samples):
            total = jnp.sum(squares[s].T, axis=0, keepdims=True)
            sum_ref[:, s * rows : (s + 1) * rows] = jnp.broadcast_to(total, (copies, rows))


def norm_kernel(length_ref, index_ref, sum_ref, gated_ref, embed_ref, gain_ref, out_ref, *, full, rows):
    _, here, _ = gated_ref.shape
    s = pl.program_id(0)
    total = jnp.sum(sum_ref[...], axis=0, keepdims=True)
    scale = lax.rsqrt(total / full + 1e-06)
    scale = jnp.broadcast_to(scale, (8, here)).T[:, :1]
    start = index_ref[0] * rows + pl.program_id(1) * here
    valid = start + iota((here, 1), 0) < length_ref[s]
    value = gated_ref[0] * scale * gain_ref[...] + embed_ref[0].astype(F32)
    out_ref[0] = jnp.where(valid, value, 0.0).astype(BF16)


def params(mebibytes):
    return pltpu.CompilerParams(vmem_limit_bytes=mebibytes << 20)


def per_device(
    token_ids,
    lengths,
    embedding,
    query_act,
    key_act,
    value_act,
    short_filter,
    decay_rates,
    residues,
    skip_gain,
    norm_gain,
):
    samples, rows, width = query_act.shape
    taps = short_filter.shape[1]
    groups, modes = decay_rates.shape
    vocab = embedding.shape[0]
    chunks = lax.axis_size("ctx")
    columns = lax.axis_size("tp")
    index = lax.axis_index("ctx").reshape(1)
    tiles = width // LANES
    smem = pl.BlockSpec(memory_space=pltpu.SMEM)

    def cube():
        return pl.BlockSpec((samples, rows, LANES), lambda i: (0, 0, i))

    def flat(height):
        return pl.BlockSpec((height, LANES), lambda i: (0, i))

    def grouped(cols):
        return pl.BlockSpec((TILE_GROUPS, cols), lambda i: (i, 0))

    state_rows = samples * modes
    border_rows = samples * taps + 2 * state_rows
    shape = jax.ShapeDtypeStruct

    product, states, border = pl.pallas_call(
        states_kernel,
        grid=(tiles,),
        in_specs=[cube(), cube(), grouped(modes)],
        out_specs=[cube(), flat(state_rows), flat(border_rows)],
        out_shape=[
            shape((samples, rows, width), BF16),
            shape((state_rows, width), F32),
            shape((border_rows, width), BF16),
        ],
        compiler_params=params(16),
        name="states",
    )(key_act, value_act, decay_rates)

    gathered = lax.all_to_all(states, "ctx", split_axis=0, concat_axis=0, tiled=True)
    before = lax.ppermute(border, "ctx", [(i, i + 1) for i in range(chunks - 1)])

    embedded = pl.pallas_call(
        embed_kernel,
        out_shape=shape((samples, rows, width), BF16),
        cost_estimate=pl.CostEstimate(
            flops=2 * samples * rows * width * vocab, bytes_accessed=4 << 20, transcendentals=0
        ),
        compiler_params=params(16),
        name="embed",
    )(token_ids, embedding)

    mixed, local, upper, lower, factors = pl.pallas_call(
        local_kernel,
        grid=(tiles,),
        in_specs=[cube(), flat(border_rows), grouped(taps), grouped(modes), grouped(modes)],
        out_specs=[cube(), cube(), flat(rows), flat(rows), flat(2 * modes)],
        out_shape=[
            shape((samples, rows, width), BF16),
            shape((samples, rows, width), F32),
            shape((rows, width), BF16),
            shape((rows, width), BF16),
            shape((2 * modes, width), F32),
        ],
        scratch_shapes=[
            pltpu.VMEM((TILE_GROUPS * taps, 2 * taps), BF16),
            pltpu.VMEM((TILE_GROUPS * taps, rows + taps), BF16),
            pltpu.VMEM((samples, rows + 2 * taps, LANES), BF16),
            pltpu.VMEM((samples, rows + taps, LANES), BF16),
        ],
        cost_estimate=pl.CostEstimate(
            flops=12_000_000_000, bytes_accessed=8 << 20, transcendentals=1 << 20
        ),
        compiler_params=params(32),
        name="local",
    )(product, before, short_filter, decay_rates, residues)

    def scan(first_ref, rate_ref, state_ref, out_ref):
        scan_kernel(first_ref, rate_ref, state_ref, out_ref, chunks=chunks, rows=rows)

    entering = pl.pallas_call(
        scan,
        in_specs=[smem, pl.BlockSpec(), pl.BlockSpec()],
        out_shape=shape((state_rows, width), F32),
        compiler_params=params(8),
        name="scan",
    )(index, decay_rates, gathered)
    carried = lax.all_to_all(entering, "ctx", split_axis=0, concat_axis=0, tiled=True)

    early_at = samples * taps // (2 * state_rows)
    gated, sums = pl.pallas_call(
        gate_kernel,
        grid=(tiles,),
        in_specs=[
            flat(state_rows),
            pl.BlockSpec((2 * state_rows, LANES), lambda i: (early_at, i)),
            flat(2 * modes),
            flat(rows),
            flat(rows),
            cube(),
            cube(),
            cube(),
            flat(1),
        ],
        out_specs=[cube(), pl.BlockSpec((columns, samples * rows), lambda i: (0, 0))],
        out_shape=[shape((samples, rows, width), F32), shape((columns, samples * rows), F32)],
        scratch_shapes=[pltpu.VMEM((samples, rows, LANES), F32)],
        compiler_params=params(16),
        name="gate",
    )(
        carried,
        before,
        factors,
        upper,
        lower,
        local,
        mixed,
        query_act,
        skip_gain.reshape(1, width),
    )
    shares = lax.all_to_all(sums, "tp", split_axis=0, concat_axis=0, tiled=True)

    parts = 2
    here = rows // parts

    def norm(length_ref, index_ref, sum_ref, gated_ref, embed_ref, gain_ref, out_ref):
        norm_kernel(
            length_ref,
            index_ref,
            sum_ref,
            gated_ref,
            embed_ref,
            gain_ref,
            out_ref,
            full=float(columns * width),
            rows=rows,
        )

    block = pl.BlockSpec((1, here, width), lambda s, i: (s, i, 0))
    return pl.pallas_call(
        norm,
        grid=(samples, parts),
        in_specs=[
            smem,
            smem,
            pl.BlockSpec((columns, here), lambda s, i: (0, s * parts + i)),
            block,
            block,
            pl.BlockSpec((1, width), lambda s, i: (0, 0)),
        ],
        out_specs=block,
        out_shape=shape((samples, rows, width), BF16),
        compiler_params=params(16),
        name="norm",
    )(lengths, index, shares, gated, embedded, norm_gain.reshape(1, width))


def solution(mesh):
    placed = (
        P(None, "ctx"),
        P(),
        P(None, "tp"),
        P(None, "ctx", "tp"),
        P(None, "ctx", "tp"),
        P(None, "ctx", "tp"),
        P("tp", None),
        P("tp", None),
        P("tp", None),
        P("tp"),
        P("tp"),
    )
    return jax.shard_map(
        per_device, mesh=mesh, in_specs=placed, out_specs=P(None, "ctx", "tp"), check_vma=False
    )
```

time: 264 us -> 104 us (0.39)
  waiting for transfers between devices: 99.7 us -> 17.7 us
  local copies, waits for them, and re-layouts: 69.8 us -> 15.3 us
  Pallas kernels: 0 us -> 37.3 us
  blocking collectives: 28.2 us -> 0 us
  matrix products: 25.7 us -> 0 us
  other arithmetic: 4.71 us -> 0 us
    all_to_all x2 -> x3, waiting for transfers between devices: 99.7 us -> 17.7 us  [the longest x1 14 us: per_device(): lax.all_to_all(states, 'ctx', split_axis=0, concat_axis=0, tiled=True)]
    pallas_call x0 -> x6, Pallas kernels: none -> 37.3 us  [the longest x1 26.1 us: per_device(): pl.pallas_call(local_kernel, grid=(tiles,), in_specs=[cube(), flat(border...]
    psum x1 -> x0, blocking collectives: 28.2 us -> none  [per_device(): square_total = lax.psum(jnp.sum(gated * gated, axis=2), 'tp')]
    dot_general x13 -> x0, matrix products: 25.7 us -> none  [the longest x1 5.16 us: modal_conv(): carried = jnp.einsum('gmnk,gmskc->gmsnc', across, states, precision=highest)]
    convert_element_type x7 -> x0, local copies, waits for them, and re-layouts: 18 us -> none  [the longest x1 9.16 us: per_device(): convolved.reshape(count_here, full_rows, columns).astype(jnp.bfloat16)]
    all_to_all x3, local copies, waits for them, and re-layouts: 16.2 us -> 2.08 us  [the longest x1 0.7 us: per_device(): shares = lax.all_to_all(sums, 'tp', split_axis=0, concat_axis=0, tiled=True)]
    unnamed x25 -> x41, local copies, waits for them, and re-layouts: 21 us -> 13.2 us
    reshape x2 -> x0, local copies, waits for them, and re-layouts: 4.54 us -> none  [the longest x1 3.09 us: short_conv(): extended.reshape(samples_here, total_rows // taps, taps, groups_here, mem...]
  transfers between devices with their start and end apart: 3 -> 4, of which waited for: 2 -> 2; matrix products, arithmetic and copies ran while one was open for 4% -> 1% of each run, Pallas kernels for 0% -> 27%
where the time goes in v1:
time: 104 us; the launch traced here: 103 us
  Pallas kernels  37.3 us (36%)
  starting transfers between devices  32.8 us (32%)
  waiting for transfers between devices  17.7 us (17%)
  local copies, waits for them, and re-layouts  15.3 us (15%)
    pallas_call x1, Pallas kernels, per_device(): pl.pallas_call(local_kernel, grid=(tiles,), in_specs=[cube(), flat(border...  26.1 us
    all_to_all x1, starting transfers between devices, per_device(): lax.all_to_all(states, 'ctx', split_axis=0, concat_axis=0, tiled=True)  15.6 us
    all_to_all x1, waiting for transfers between devices, per_device(): lax.all_to_all(states, 'ctx', split_axis=0, concat_axis=0, tiled=True)  14 us
    unnamed x41, local copies, waits for them, and re-layouts  13.2 us
    all_to_all x1, starting transfers between devices, per_device(): shares = lax.all_to_all(sums, 'tp', split_axis=0, concat_axis=0, tiled=True)  7.85 us
    ppermute x1, starting transfers between devices, per_device(): lax.ppermute(border, 'ctx', [(i, i + 1) for i in range(chunks - 1)])  5.5 us
    pallas_call x1, Pallas kernels, per_device(): pl.pallas_call(gate_kernel, grid=(tiles,), in_specs=[flat(state_rows), pl...  4.37 us
    all_to_all x1, starting transfers between devices, per_device(): lax.all_to_all(entering, 'ctx', split_axis=0, concat_axis=0, tiled=True)  3.84 us
  transfers between devices with their start and end apart: 4, of which 2 were waited for; matrix products, arithmetic and copies ran while one was open for 1% of the time, Pallas kernels for 27%

profile of v1, /device:TPU:1, one launch (start us, length us, event | category | flops | bytes accessed | tf_op | source)
XLA Modules:
  0.0 103.2 jit_solution(17917388924393208825)
XLA Ops:
  0.0 0.0 copy-start.17
  0.0 0.0 copy-start.15
  0.0 0.8 copy.18.rate_ref
  0.8 0.0 copy-start.2
  0.8 1.2 %copy-done.2 = bf16[2,512,512]{2,1,0:T(8,128)(2,1)S(1)} copy-done((bf16[2,512,512]{2,1,0:T(8,128)(2,1)S(1)}, bf16[2,512,512]{2,1,0:T(8,128)(2,1)}, u32[]{:S(2)}) %copy-start.2) | copy-done | bytes 1048600
  2.0 0.0 copy-start.3
  2.0 1.2 %copy-done.3 = bf16[2,512,512]{2,1,0:T(8,128)(2,1)S(1)} copy-done((bf16[2,512,512]{2,1,0:T(8,128)(2,1)S(1)}, bf16[2,512,512]{2,1,0:T(8,128)(2,1)}, u32[]{:S(2)}) %copy-start.3) | copy-done | bytes 1048600
  3.3 2.6 %states.1 = (bf16[2,512,512]{2,1,0:T(8,128)(2,1)S(1)}, f32[32,512]{1,0:T(8,128)S(1)}, bf16[320,512]{1,0:T(8,128)(2,1)S(1)}) custom-call(bf16[2,512,512]{2,1,0:T(8,128)(2,1)S(1)} %copy-done.2, bf16[2,512,512]{2,1,0:T(8,128)(2,1)S(1)} %copy-done.3, f32[32,16]{1,0:T(8,128)S(1)} %copy.18.rate_ref), custom_call_target="tpu_custom_call" | custom-call | tf_op jit(solution)/shard_map/states/pallas_call | solution.py:278
  5.8 5.5 %collective-permute-start = (bf16[320,512]{1,0:T(8,128)(2,1)S(1)}, bf16[320,512]{1,0:T(8,128)(2,1)S(1)}, u32[]{:S(2)}, u32[]{:S(2)}) collective-permute-start(bf16[320,512]{1,0:T(8,128)(2,1)S(1)} %get-tuple-element.16), channel_id=1, source_target_pairs={{0,16},{16,32},{32,48},{48,64},{64,80},{80,96},{96,112},{112,128},... | collective-permute-start | bytes 983048 | tf_op jit(solution)/shard_map/ppermute | solution.py:293
  11.3 0.7 copy.17
  12.0 15.6 %all-to-all-start = ((f32[32,1,512]{2,1,0:T(1,128)}), f32[32,1,512]{2,1,0:T(1,128)S(1)}, u32[]{:S(2)}, u32[]{:S(2)}) async-start(f32[32,1,512]{2,1,0:T(1,128)} %copy.17), calls=%async_computation | async-start | bytes 131072 | tf_op jit(solution)/shard_map/all_to_all | solution.py:292
  27.6 0.0 copy-done.17
  27.6 0.1 copy.21.residue_ref
  27.7 14.0 %all-to-all-done = f32[32,1,512]{2,1,0:T(1,128)S(1)} async-done(((f32[32,1,512]{2,1,0:T(1,128)}), f32[32,1,512]{2,1,0:T(1,128)S(1)}, u32[]{:S(2)}, u32[]{:S(2)}) %all-to-all-start) | async-done | bytes 65568 | tf_op jit(solution)/shard_map/all_to_all | solution.py:292
  41.7 0.2 scan.1
  41.9 0.7 copy.19
  42.6 3.8 %all-to-all-start.1 = ((f32[32,1,512]{2,1,0:T(1,128)}), f32[32,1,512]{2,1,0:T(1,128)S(1)}, u32[]{:S(2)}, u32[]{:S(2)}) async-start(f32[32,1,512]{2,1,0:T(1,128)} %copy.19), calls=%async_computation.1 | async-start | bytes 131072 | tf_op jit(solution)/shard_map/all_to_all | solution.py:340
  46.4 0.0 collective-permute-done.border_ref.early_ref
  46.4 0.0 copy-done.15
  46.4 0.0 copy-start.4
  46.4 0.0 copy-start.11
  46.4 26.1 %local.1 = (bf16[2,512,512]{2,1,0:T(8,128)(2,1)S(1)}, f32[2,512,512]{2,1,0:T(8,128)S(1)}, bf16[512,512]{1,0:T(8,128)(2,1)S(1)}, bf16[512,512]{1,0:T(8,128)(2,1)S(1)}, f32[32,512]{1,0:T(8,128)S(1)}) custom-call(bf16[2,512,512]{2,1,0:T(8,128)(2,1)S(1)} %get-tuple-element.17.product_ref, bf16[320,512]{1,0:T(8,128)(2,1)S(1)} %collective-permute-done.border_ref.early_ref, ...), custom_call_target="tpu_custom_call" | custom-call | flops 12000000000 | bytes 8388608 | tf_op jit(solution)/shard_map/local/pallas_call | solution.py:305
  72.6 0.0 copy-start
  72.6 1.3 %copy-done = f32[2,512,512]{2,1,0:T(8,128)} copy-done((f32[2,512,512]{2,1,0:T(8,128)}, f32[2,512,512]{2,1,0:T(8,128)S(1)}, u32[]{:S(2)}) %copy-start) | copy-done | bytes 2097176
  73.9 0.0 copy-start.5
  73.9 1.0 copy-done.5
  74.9 0.0 copy-start.7
  74.9 0.8 copy-done.7
  75.7 0.0 copy-start.9
  75.7 0.8 copy-done.9
  76.5 0.0 all-to-all-done.1
  76.5 0.0 copy-done.4
  76.5 0.0 copy-done.11
  76.5 0.0 copy-start.1
  76.5 1.6 %copy-done.1 = f32[2,512,512]{2,1,0:T(8,128)S(1)} copy-done((f32[2,512,512]{2,1,0:T(8,128)S(1)}, f32[2,512,512]{2,1,0:T(8,128)}, u32[]{:S(2)}) %copy-start.1) | copy-done | bytes 2097176
  78.1 0.0 copy-start.6
  78.1 1.2 %copy-done.6 = bf16[2,512,512]{2,1,0:T(8,128)(2,1)S(1)} copy-done((bf16[2,512,512]{2,1,0:T(8,128)(2,1)S(1)}, bf16[2,512,512]{2,1,0:T(8,128)(2,1)}, u32[]{:S(2)}) %copy-start.6) | copy-done | bytes 1048600
  79.3 0.0 copy-start.8
  79.3 1.0 %copy-done.8 = bf16[512,512]{1,0:T(8,128)(2,1)S(1)} copy-done((bf16[512,512]{1,0:T(8,128)(2,1)S(1)}, bf16[512,512]{1,0:T(8,128)(2,1)}, u32[]{:S(2)}) %copy-start.8) | copy-done | bytes 524312
  80.4 0.0 copy-start.10
  80.4 1.0 %copy-done.10 = bf16[512,512]{1,0:T(8,128)(2,1)S(1)} copy-done((bf16[512,512]{1,0:T(8,128)(2,1)S(1)}, bf16[512,512]{1,0:T(8,128)(2,1)}, u32[]{:S(2)}) %copy-start.10) | copy-done | bytes 524312
  81.4 0.0 copy-start.16
  81.4 4.4 %gate.1 = (f32[2,512,512]{2,1,0:T(8,128)S(1)}, f32[16,1024]{1,0:T(8,128)S(1)}) custom-call(f32[32,512]{1,0:T(8,128)S(1)} %bitcast.18, bf16[320,512]{1,0:T(8,128)(2,1)S(1)} %collective-permute-done.border_ref.early_ref, f32[32,512]{1,0:T(8,128)S(1)} %get-tuple-element.18.factor_ref, bf16[512,512]{1,0:T(8,128)(2,1)S(1)} %copy-done.8, ...), custom_call_target="tpu_custom_call" | custom-call | tf_op jit(solution)/shard_map/gate/pallas_call | solution.py:343
  85.8 0.0 copy-start.12
  85.8 0.0 copy-start.13
  85.8 0.7 copy.22
  86.5 7.9 %all-to-all-start.2 = ((f32[16,1,1024]{2,1,0:T(1,128)}), f32[16,1,1024]{2,1,0:T(1,128)S(1)}, u32[]{:S(2)}, u32[]{:S(2)}) async-start(f32[16,1,1024]{2,1,0:T(1,128)} %copy.22), calls=%async_computation.2 | async-start | bytes 131072 | tf_op jit(solution)/shard_map/all_to_all | solution.py:373
  94.4 0.0 copy-done.16
  94.4 0.0 copy-start.14
  94.4 1.0 %copy-done.14 = bf16[512,512]{1,0:T(8,128)(2,1)S(1)} copy-done((bf16[512,512]{1,0:T(8,128)(2,1)S(1)}, bf16[512,512]{1,0:T(8,128)(2,1)}, u32[]{:S(2)}) %copy-start.14) | copy-done | bytes 524312
  95.4 1.1 %embed.1.embed_ref = bf16[2,512,512]{2,1,0:T(8,128)(2,1)S(1)} custom-call(s32[2,512]{1,0:T(2,128)S(1)} %copy-done.16, bf16[512,512]{1,0:T(8,128)(2,1)S(1)} %copy-done.14), custom_call_target="tpu_custom_call" | custom-call | flops 536870912 | bytes 4194304 | tf_op jit(solution)/shard_map/embed/pallas_call | solution.py:295
  96.5 3.7 %all-to-all-done.2 = f32[16,1,1024]{2,1,0:T(1,128)S(1)} async-done(((f32[16,1,1024]{2,1,0:T(1,128)}), f32[16,1,1024]{2,1,0:T(1,128)S(1)}, u32[]{:S(2)}, u32[]{:S(2)}) %all-to-all-start.2) | async-done | bytes 65568 | tf_op jit(solution)/shard_map/all_to_all | solution.py:373
  100.2 0.0 copy-done.12
  100.2 0.0 copy-done.13
  100.2 2.9 %norm.1 = bf16[2,512,512]{2,1,0:T(8,128)(2,1)} custom-call(s32[2]{0:T(128)S(1)} %copy-done.13, s32[1]{0:T(128)} %bitcast.first_ref.index_ref, f32[16,1024]{1,0:T(8,128)S(1)} %bitcast.15, f32[2,512,512]{2,1,0:T(8,128)S(1)} %get-tuple-element.24.gated_ref, bf16[2,512,512]{2,1,0:T(8,128)(2,1)S(1)} %embed.1.embed_ref, f32[1,512]{1,0:T(1,128)S(1)} %bitcast.22), custom_call_target="tpu_custom_call" | custom-call | tf_op jit(solution)/shard_map/norm/pallas_call | solution.py:392
  (3 shorter events, 0.0 us)
Async XLA Ops:
  0.0 27.6 %copy-start.17 = (f32[32,16]{0,1:T(8,128)S(1)}, f32[32,16]{0,1:T(8,128)}, u32[]{:S(2)}) copy-start(f32[32,16]{0,1:T(8,128)} %param.19) | copy-start | bytes 6148
  0.0 46.4 %copy-start.15 = (bf16[32,128]{1,0:T(8,128)(2,1)S(1)}, bf16[32,128]{1,0:T(8,128)(2,1)}, u32[]{:S(2)}) copy-start(bf16[32,128]{1,0:T(8,128)(2,1)} %filter_ref.1) | copy-start | bytes 24580
  0.8 1.2 %copy-start.2 = (bf16[2,512,512]{2,1,0:T(8,128)(2,1)S(1)}, bf16[2,512,512]{2,1,0:T(8,128)(2,1)}, u32[]{:S(2)}) copy-start(bf16[2,512,512]{2,1,0:T(8,128)(2,1)} %key_ref.1) | copy-start | bytes 3145732
  2.0 1.2 %copy-start.3 = (bf16[2,512,512]{2,1,0:T(8,128)(2,1)S(1)}, bf16[2,512,512]{2,1,0:T(8,128)(2,1)}, u32[]{:S(2)}) copy-start(bf16[2,512,512]{2,1,0:T(8,128)(2,1)} %value_ref.1) | copy-start | bytes 3145732
  5.8 40.6 %collective-permute-start = (bf16[320,512]{1,0:T(8,128)(2,1)S(1)}, bf16[320,512]{1,0:T(8,128)(2,1)S(1)}, u32[]{:S(2)}, u32[]{:S(2)}) collective-permute-start(bf16[320,512]{1,0:T(8,128)(2,1)S(1)} %get-tuple-element.16), channel_id=1, source_target_pairs={{0,16},{16,32},{32,48},{48,64},{64,80},{80,96},{96,112},{112,128},... | collective-permute-start | bytes 983048 | tf_op jit(solution)/shard_map/ppermute | solution.py:293
  12.0 29.7 %all-to-all-start = ((f32[32,1,512]{2,1,0:T(1,128)}), f32[32,1,512]{2,1,0:T(1,128)S(1)}, u32[]{:S(2)}, u32[]{:S(2)}) async-start(f32[32,1,512]{2,1,0:T(1,128)} %copy.17), calls=%async_computation | async-start | bytes 131072 | tf_op jit(solution)/shard_map/all_to_all | solution.py:292
  42.6 33.9 %all-to-all-start.1 = ((f32[32,1,512]{2,1,0:T(1,128)}), f32[32,1,512]{2,1,0:T(1,128)S(1)}, u32[]{:S(2)}, u32[]{:S(2)}) async-start(f32[32,1,512]{2,1,0:T(1,128)} %copy.19), calls=%async_computation.1 | async-start | bytes 131072 | tf_op jit(solution)/shard_map/all_to_all | solution.py:340
  46.4 30.1 %copy-start.4 = (bf16[2,512,512]{2,1,0:T(8,128)(2,1)S(1)}, bf16[2,512,512]{2,1,0:T(8,128)(2,1)}, u32[]{:S(2)}) copy-start(bf16[2,512,512]{2,1,0:T(8,128)(2,1)} %query_ref.1) | copy-start | bytes 3145732
  46.4 30.1 %copy-start.11 = (f32[512]{0:T(512)S(1)}, f32[512]{0:T(512)}, u32[]{:S(2)}) copy-start(f32[512]{0:T(512)} %param.20) | copy-start | bytes 6148
  72.6 1.3 %copy-start = (f32[2,512,512]{2,1,0:T(8,128)}, f32[2,512,512]{2,1,0:T(8,128)S(1)}, u32[]{:S(2)}) copy-start(f32[2,512,512]{2,1,0:T(8,128)S(1)} %get-tuple-element.21.local_ref) | copy-start | bytes 6291460
  73.9 1.0 copy-start.5
  74.9 0.8 copy-start.7
  75.7 0.8 copy-start.9
  76.5 1.6 %copy-start.1 = (f32[2,512,512]{2,1,0:T(8,128)S(1)}, f32[2,512,512]{2,1,0:T(8,128)}, u32[]{:S(2)}) copy-start(f32[2,512,512]{2,1,0:T(8,128)} %copy-done) | copy-start | bytes 6291460
  78.1 1.2 %copy-start.6 = (bf16[2,512,512]{2,1,0:T(8,128)(2,1)S(1)}, bf16[2,512,512]{2,1,0:T(8,128)(2,1)}, u32[]{:S(2)}) copy-start(bf16[2,512,512]{2,1,0:T(8,128)(2,1)} %copy-done.5) | copy-start | bytes 3145732
  79.3 1.0 %copy-start.8 = (bf16[512,512]{1,0:T(8,128)(2,1)S(1)}, bf16[512,512]{1,0:T(8,128)(2,1)}, u32[]{:S(2)}) copy-start(bf16[512,512]{1,0:T(8,128)(2,1)} %copy-done.7) | copy-start | bytes 1572868
  80.4 1.0 %copy-start.10 = (bf16[512,512]{1,0:T(8,128)(2,1)S(1)}, bf16[512,512]{1,0:T(8,128)(2,1)}, u32[]{:S(2)}) copy-start(bf16[512,512]{1,0:T(8,128)(2,1)} %copy-done.9) | copy-start | bytes 1572868
  81.4 13.0 %copy-start.16 = (s32[2,512]{1,0:T(2,128)S(1)}, s32[2,512]{1,0:T(2,128)}, u32[]{:S(2)}) copy-start(s32[2,512]{1,0:T(2,128)} %token_ref.1) | copy-start | bytes 12292
  85.8 14.4 %copy-start.12 = (f32[512]{0:T(512)S(1)}, f32[512]{0:T(512)}, u32[]{:S(2)}) copy-start(f32[512]{0:T(512)} %param.21) | copy-start | bytes 6148
  85.8 14.4 %copy-start.13 = (s32[2]{0:T(128)S(1)}, s32[2]{0:T(128)}, u32[]{:S(2)}) copy-start(s32[2]{0:T(128)} %length_ref.1) | copy-start | bytes 28
  86.5 13.7 %all-to-all-start.2 = ((f32[16,1,1024]{2,1,0:T(1,128)}), f32[16,1,1024]{2,1,0:T(1,128)S(1)}, u32[]{:S(2)}, u32[]{:S(2)}) async-start(f32[16,1,1024]{2,1,0:T(1,128)} %copy.22), calls=%async_computation.2 | async-start | bytes 131072 | tf_op jit(solution)/shard_map/all_to_all | solution.py:373
  94.4 1.0 %copy-start.14 = (bf16[512,512]{1,0:T(8,128)(2,1)S(1)}, bf16[512,512]{1,0:T(8,128)(2,1)}, u32[]{:S(2)}) copy-start(bf16[512,512]{1,0:T(8,128)(2,1)} %table_ref.1) | copy-start | bytes 1572868

commit v2 on v1

v2 whole, which is shorter than its diff:
```python
import jax
import jax.numpy as jnp
from jax import lax
from jax.experimental import pallas as pl
from jax.experimental.pallas import tpu as pltpu
from jax.sharding import PartitionSpec as P

GROUP = 16
LANES = 128
TILE_GROUPS = LANES // GROUP
F32 = jnp.float32
BF16 = jnp.bfloat16


def iota(shape, dim, dtype=jnp.int32):
    return lax.broadcasted_iota(jnp.int32, shape, dim).astype(dtype)


def own_group(stacked, rows):
    lane_group = iota((rows, LANES), 1) // GROUP
    picked = stacked[:rows]
    for g in range(1, TILE_GROUPS):
        picked = jnp.where(lane_group == g, stacked[g * rows : (g + 1) * rows], picked)
    return picked


def halves(values):
    upper = values.astype(BF16)
    return upper, (values - upper.astype(F32)).astype(BF16)


def dot(a, b):
    return jnp.dot(a, b, preferred_element_type=F32)


def tile_column(table, tile):
    modes, groups = table.shape
    parts = []
    for g in range(TILE_GROUPS):
        here = iota((modes, groups), 1) == tile * TILE_GROUPS + g
        parts.append(jnp.sum(jnp.where(here, table, 0.0), axis=1, keepdims=True))
    return jnp.concatenate(parts, axis=0)


def product_of(key_ref, value_ref, s):
    return (key_ref[s].astype(F32) * value_ref[s].astype(F32)).astype(BF16)


def states_kernel(rate_ref, key_ref, value_ref, state_ref, *, rows):
    samples, here, width = key_ref.shape
    modes = rate_ref.shape[0]
    step = pl.program_id(0)
    first = (rows - 1 - step * here).astype(F32)
    lag = first - iota((1, here), 1, F32)
    for tile in range(width // LANES):
        lanes = slice(tile * LANES, (tile + 1) * LANES)
        weights = jnp.exp(-tile_column(rate_ref[...], tile) * lag)
        weights = jnp.concatenate(halves(weights), axis=0)
        half = weights.shape[0] // 2
        for s in range(samples):
            key, value = key_ref[s, :, lanes].astype(F32), value_ref[s, :, lanes].astype(F32)
            full = dot(weights, (key * value).astype(BF16))
            state = own_group(full[:half] + full[half:], modes).reshape(modes, 1, LANES)
            part = slice(s * modes, (s + 1) * modes)

            @pl.when(step == 0)
            def _():
                state_ref[part, :, lanes] = state

            @pl.when(step > 0)
            def _():
                state_ref[part, :, lanes] = state_ref[part, :, lanes] + state


def border_kernel(rate_ref, key_ref, value_ref, border_ref, *, taps):
    samples, rows, _ = key_ref.shape
    modes = rate_ref.shape[0]
    early = rows - taps
    rate = tile_column(rate_ref[...], pl.program_id(0))
    weights = jnp.exp(-rate * (early - 1.0 - iota((1, early), 1, F32)))
    weights = jnp.concatenate(halves(weights), axis=0)
    half = weights.shape[0] // 2
    for s in range(samples):
        product = product_of(key_ref, value_ref, s)
        border_ref[s * taps : (s + 1) * taps, :] = product[early:]
        full = dot(weights, product[:early])
        upper, lower = halves(own_group(full[:half] + full[half:], modes))
        first = samples * taps + s * modes
        border_ref[first : first + modes, :] = upper
        border_ref[first + samples * modes : first + (samples + 1) * modes, :] = lower


def early_kernel(border_ref, out_ref, mark_ref):
    mark_ref[...] = jnp.zeros_like(mark_ref)
    height = out_ref.shape[0]
    upper = border_ref[:height, :].astype(F32)
    out_ref[...] = upper + border_ref[height:, :].astype(F32)


def scan_kernel(first_ref, rate_ref, state_ref, out_ref, *, chunks, rows):
    total, _, width = state_ref.shape
    each = total // chunks
    groups, modes = rate_ref.shape
    rates = rate_ref[...]
    for r in range(each):
        mode = lax.rem(first_ref[0] * each + r, modes)
        picked = jnp.sum(
            jnp.where(iota(rates.shape, 1) == mode, rates, 0.0), axis=1, keepdims=True
        )
        at_group = iota((groups, width), 0) == iota((groups, width), 1) // GROUP
        rate = jnp.sum(jnp.where(at_group, picked, 0.0), axis=0, keepdims=True)
        decay = jnp.exp(-rate * float(rows))
        held = jnp.zeros((1, width), F32)
        out_ref[r] = held
        for n in range(1, chunks):
            out_ref[n * each + r] = held
            held = decay * held + state_ref[(n - 1) * each + r]


def dot_rows(a, b):
    return lax.dot_general(a, b, (((1,), (1,)), ((), ())), preferred_element_type=F32)


def local_kernel(
    border_ref,
    key_ref,
    value_ref,
    filter_ref,
    rate_ref,
    residue_ref,
    skip_ref,
    base_ref,
    factor_ref,
    product_window,
    mixed_window,
    turned,
):
    samples, rows, _ = key_ref.shape
    modes = rate_ref.shape[0]
    taps = filter_ref.shape[1]
    span = rows + taps
    blocks = rows // taps
    before = span - 2 * taps
    tile = pl.program_id(0)
    rate = tile_column(rate_ref[...], tile)
    residue = tile_column(residue_ref[...], tile)
    filters = filter_ref[...]

    reverse = (iota((taps, 2 * taps), 0) + iota((taps, 2 * taps), 1) == taps).astype(BF16)
    short_base = dot(filters, reverse)
    wide = span + taps
    place = iota((1, wide), 1)
    lag = jnp.where(place <= rows, rows - place, rows + wide - place)
    zero = jnp.logical_and(place > rows, place <= span)
    modal = residue * jnp.exp(-rate * lag.astype(F32))
    modal = jnp.where(zero, 0.0, modal)
    long_base = jnp.sum(modal.reshape(TILE_GROUPS, modes, wide), axis=1)

    for s in range(samples):
        product_window[s, :, :taps] = jnp.zeros((LANES, taps), BF16)
        mixed_window[s, :, :before] = jnp.zeros((LANES, before), BF16)
        border = border_ref[s * taps : (s + 1) * taps, :].astype(F32)
        product_window[s, :, taps : 2 * taps] = border.T.astype(BF16)
        product = product_of(key_ref, value_ref, s).astype(F32)
        product_window[s, :, 2 * taps :] = product.T.astype(BF16)

    skip = jnp.broadcast_to(skip_ref[...], (8, LANES)).T[:, :1]
    for g in range(TILE_GROUPS):
        channels = slice(g * GROUP, (g + 1) * GROUP)
        spread = jnp.broadcast_to(short_base[g : g + 1], (taps, 2 * taps))
        short_table = pltpu.roll(spread, 0, 1, stride=1, stride_axis=0).astype(BF16)
        pieces = [
            product_window[s, channels, b * taps : (b + 2) * taps]
            for s in range(samples)
            for b in range(blocks + 1)
        ]
        mixed = dot_rows(jnp.concatenate(pieces, axis=0), short_table).astype(BF16)
        for s in range(samples):
            for b in range(blocks + 1):
                first = (s * (blocks + 1) + b) * GROUP
                mixed_window[s, channels, before + b * taps : before + (b + 1) * taps] = mixed[
                    first : first + GROUP
                ]
        spread = jnp.broadcast_to(long_base[g : g + 1], (taps, wide))
        long_table = pltpu.roll(spread, 0, 1, stride=1, stride_axis=0)[:, :span].astype(BF16)
        pieces = [
            mixed_window[s, channels, b * taps : b * taps + span]
            for s in range(samples)
            for b in range(blocks)
        ]
        filtered = dot_rows(jnp.concatenate(pieces, axis=0), long_table)
        for s in range(samples):
            for b in range(blocks):
                first = (s * blocks + b) * GROUP
                at = (s * (blocks + 1) + b + 1) * GROUP
                turned[s, channels, b * taps : (b + 1) * taps] = filtered[
                    first : first + GROUP
                ] + skip[channels] * mixed[at : at + GROUP].astype(F32)
    for s in range(samples):
        base_ref[s] = turned[s].T.astype(BF16)

    tap_weights = jnp.exp(-rate * (taps - iota((1, taps), 1, F32)))
    spread = jnp.broadcast_to(
        filters.astype(F32)[:, None, :], (TILE_GROUPS, modes, taps)
    ).reshape(TILE_GROUPS * modes, taps)
    gain = residue * jnp.sum(spread * tap_weights, axis=1, keepdims=True)
    square = (TILE_GROUPS * modes, LANES)
    factor_ref[:modes, :] = own_group(
        jnp.broadcast_to(jnp.exp(-rate * float(rows - taps)), square), modes
    )
    factor_ref[modes:, :] = own_group(jnp.broadcast_to(gain, square), modes)


def embed_kernel(token_ref, table_ref, out_ref, mark_ref):
    mark_ref[...] = jnp.zeros_like(mark_ref)
    samples, rows = token_ref.shape
    vocab = table_ref.shape[0]
    for s in range(samples):
        ids = jnp.broadcast_to(token_ref[s : s + 1, :].astype(F32), (8, rows)).T[:, :1]
        one_hot = (ids == iota((rows, vocab), 1, F32)).astype(BF16)
        out_ref[s] = dot(one_hot, table_ref[...]).astype(BF16)


def gate_kernel(
    carried_ref,
    early_ref,
    factor_ref,
    rate_ref,
    base_source,
    query_source,
    gated_ref,
    sum_ref,
    base_ref,
    query_ref,
    squares,
    arrived,
):
    samples, rows, width = base_ref.shape
    modes = factor_ref.shape[0] // 2
    copies = sum_ref.shape[0]
    own = iota((LANES, LANES), 0) // modes == iota((LANES, LANES), 1) // GROUP
    tiles = [slice(first, first + LANES) for first in range(0, width, LANES)]
    loads = []
    for tile, lanes in enumerate(tiles):
        pair = (
            pltpu.make_async_copy(
                base_source.at[:, :, lanes], base_ref.at[:, :, lanes], arrived.at[0, tile]
            ),
            pltpu.make_async_copy(
                query_source.at[:, :, lanes], query_ref.at[:, :, lanes], arrived.at[1, tile]
            ),
        )
        for load in pair:
            load.start()
        loads.append(pair)
    for tile, lanes in enumerate(tiles):
        rate = rate_ref[:, lanes]
        head = jnp.exp(-rate * (1.0 + iota((LANES, 1), 0, F32)))
        step = jnp.exp(-rate * float(LANES))
        after = [head]
        for _ in range(rows // LANES - 1):
            after.append(after[-1] * step)
        upper, lower = halves(jnp.concatenate(after, axis=0))
        after = jnp.concatenate([upper, lower, upper], axis=1)
        for load in loads[tile]:
            load.wait()
        for s in range(samples):
            part = slice(s * modes, (s + 1) * modes)
            carried = carried_ref[part, :, lanes].reshape(modes, LANES)
            state = factor_ref[:modes, lanes] * carried + early_ref[part, lanes]
            state = state * factor_ref[modes:, lanes]
            spread = jnp.concatenate([state] * TILE_GROUPS, axis=0)
            upper, lower = halves(jnp.where(own, spread, 0.0))
            carry = dot(after, jnp.concatenate([upper, upper, lower], axis=0))
            base = base_ref[s, :, lanes].astype(F32)
            gated = query_ref[s, :, lanes].astype(F32) * (base + carry)
            gated_ref[s, :, lanes] = gated
            if tile == 0:
                squares[s] = gated * gated
            else:
                squares[s] = squares[s] + gated * gated
    for s in range(samples):
        total = jnp.sum(squares[s].T, axis=0, keepdims=True)
        sum_ref[:, :, s * rows : (s + 1) * rows] = jnp.broadcast_to(
            total.reshape(1, 1, rows), (copies, 1, rows)
        )


def norm_kernel(
    length_ref, index_ref, sum_ref, gated_ref, embed_ref, gain_ref, out_target, out_ref, left, *, full
):
    samples, rows, _ = gated_ref.shape
    here = 128
    total = jnp.sum(sum_ref[...], axis=0)
    scale = jnp.broadcast_to(lax.rsqrt(total / full + 1e-06), (8, samples * rows)).T[:, :1]
    stores = []
    for s in range(samples):
        for part in range(rows // here):
            at = slice(part * here, (part + 1) * here)
            start = index_ref[0] * rows + part * here
            valid = start + iota((here, 1), 0) < length_ref[s]
            first = s * rows + part * here
            value = gated_ref[s, at, :] * scale[first : first + here] * gain_ref[...]
            value = value + embed_ref[s, at, :].astype(F32)
            out_ref[s, at, :] = jnp.where(valid, value, 0.0).astype(BF16)
            store = pltpu.make_async_copy(
                out_ref.at[s, at, :], out_target.at[s, at, :], left.at[s, part]
            )
            store.start()
            stores.append(store)
    for store in stores:
        store.wait()


def params(mebibytes):
    return pltpu.CompilerParams(vmem_limit_bytes=mebibytes << 20)


def per_device(
    token_ids,
    lengths,
    embedding,
    query_act,
    key_act,
    value_act,
    short_filter,
    decay_rates,
    residues,
    skip_gain,
    norm_gain,
):
    samples, rows, width = query_act.shape
    taps = short_filter.shape[1]
    groups, modes = decay_rates.shape
    vocab = embedding.shape[0]
    chunks = lax.axis_size("ctx")
    columns = lax.axis_size("tp")
    index = lax.axis_index("ctx").reshape(1)
    tiles = width // LANES
    smem = pl.BlockSpec(memory_space=pltpu.SMEM)

    def cube():
        return pl.BlockSpec((samples, rows, LANES), lambda i: (0, 0, i))

    def flat(height):
        return pl.BlockSpec((height, LANES), lambda i: (0, i))

    def grouped(cols):
        return pl.BlockSpec((TILE_GROUPS, cols), lambda i: (i, 0))

    state_rows = samples * modes
    border_rows = samples * taps + 2 * state_rows
    early_at = samples * taps // (2 * state_rows)
    shape = jax.ShapeDtypeStruct
    whole = pl.BlockSpec((modes, groups), lambda i: (0, 0))
    rates = decay_rates.T

    def states_step(rate_ref, key_ref, value_ref, state_ref):
        states_kernel(rate_ref, key_ref, value_ref, state_ref, rows=rows)

    slab = pl.BlockSpec((samples, rows // 2, width), lambda i: (0, i, 0))
    states = pl.pallas_call(
        states_step,
        grid=(2,),
        in_specs=[whole, slab, slab],
        out_specs=pl.BlockSpec((state_rows, 1, width), lambda i: (0, 0, 0)),
        out_shape=shape((state_rows, 1, width), F32),
        compiler_params=params(60),
        name="states",
    )(rates, key_act, value_act)
    gathered = lax.all_to_all(states, "ctx", split_axis=0, concat_axis=0, tiled=True)

    def border_step(rate_ref, key_ref, value_ref, border_ref):
        border_kernel(rate_ref, key_ref, value_ref, border_ref, taps=taps)

    key_late, value_late, _ = lax.optimization_barrier((key_act, value_act, states))
    border = pl.pallas_call(
        border_step,
        grid=(tiles,),
        in_specs=[whole, cube(), cube()],
        out_specs=flat(border_rows),
        out_shape=shape((border_rows, width), BF16),
        cost_estimate=pl.CostEstimate(
            flops=400_000_000, bytes_accessed=3 << 20, transcendentals=1 << 18
        ),
        compiler_params=params(60),
        name="border",
    )(rates, key_late, value_late)
    before = lax.ppermute(border, "ctx", [(i, i + 1) for i in range(chunks - 1)])

    early, early_mark = pl.pallas_call(
        early_kernel,
        grid=(1,),
        in_specs=[pl.BlockSpec((2 * state_rows, width), lambda i: (early_at, 0))],
        out_specs=[
            pl.BlockSpec((state_rows, width), lambda i: (0, 0)),
            pl.BlockSpec((8, LANES), lambda i: (0, 0)),
        ],
        out_shape=[shape((state_rows, width), F32), shape((8, LANES), F32)],
        compiler_params=params(60),
        name="early",
    )(before)

    embedded, embed_mark = pl.pallas_call(
        embed_kernel,
        out_shape=[shape((samples, rows, width), BF16), shape((8, LANES), F32)],
        cost_estimate=pl.CostEstimate(
            flops=40 * samples * rows * width * vocab, bytes_accessed=4 << 20, transcendentals=0
        ),
        compiler_params=params(16),
        name="embed",
    )(token_ids, embedding)

    base, factors = pl.pallas_call(
        local_kernel,
        grid=(tiles,),
        in_specs=[flat(border_rows), cube(), cube(), grouped(taps), whole, whole, flat(1)],
        out_specs=[cube(), flat(2 * modes)],
        out_shape=[
            shape((samples, rows, width), BF16),
            shape((2 * modes, width), F32),
        ],
        scratch_shapes=[
            pltpu.VMEM((samples, LANES, rows + 2 * taps), BF16),
            pltpu.VMEM((samples, LANES, 2 * rows), BF16),
            pltpu.VMEM((samples, LANES, rows), F32),
        ],
        cost_estimate=pl.CostEstimate(
            flops=12_000_000_000, bytes_accessed=8 << 20, transcendentals=1 << 20
        ),
        compiler_params=params(60),
        name="local",
    )(
        before,
        key_act,
        value_act,
        short_filter,
        rates,
        residues.T,
        skip_gain.reshape(1, width),
    )

    def scan(first_ref, rate_ref, state_ref, early_ref, embed_ref, out_ref):
        scan_kernel(first_ref, rate_ref, state_ref, out_ref, chunks=chunks, rows=rows)

    entering = pl.pallas_call(
        scan,
        in_specs=[smem, pl.BlockSpec(), pl.BlockSpec(), pl.BlockSpec(), pl.BlockSpec()],
        out_shape=shape((state_rows, 1, width), F32),
        compiler_params=params(8),
        name="scan",
    )(index, decay_rates, gathered, early_mark, embed_mark)
    carried = lax.all_to_all(entering, "ctx", split_axis=0, concat_axis=0, tiled=True)

    vmem = pl.BlockSpec(memory_space=pltpu.VMEM)
    anywhere = pl.BlockSpec(memory_space=pl.ANY)
    gated, sums = pl.pallas_call(
        gate_kernel,
        in_specs=[vmem, vmem, vmem, vmem, anywhere, anywhere],
        out_shape=[
            shape((samples, rows, width), F32),
            shape((columns, 1, samples * rows), F32),
        ],
        scratch_shapes=[
            pltpu.VMEM((samples, rows, width), BF16),
            pltpu.VMEM((samples, rows, width), BF16),
            pltpu.VMEM((samples, rows, LANES), F32),
            pltpu.SemaphoreType.DMA((2, tiles)),
        ],
        compiler_params=params(16),
        name="gate",
    )(carried, early, factors, decay_rates.reshape(1, groups * modes), base, query_act)
    shares = lax.all_to_all(sums, "tp", split_axis=0, concat_axis=0, tiled=True)

    def norm(*refs):
        norm_kernel(*refs, full=float(columns * width))

    return pl.pallas_call(
        norm,
        in_specs=[smem, smem, vmem, vmem, vmem, vmem],
        out_specs=anywhere,
        out_shape=shape((samples, rows, width), BF16),
        scratch_shapes=[
            pltpu.VMEM((samples, rows, width), BF16),
            pltpu.SemaphoreType.DMA((samples, rows // 128)),
        ],
        compiler_params=params(16),
        name="norm",
    )(lengths, index, shares, gated, embedded, norm_gain.reshape(1, width))


def solution(mesh):
    placed = (
        P(None, "ctx"),
        P(),
        P(None, "tp"),
        P(None, "ctx", "tp"),
        P(None, "ctx", "tp"),
        P(None, "ctx", "tp"),
        P("tp", None),
        P("tp", None),
        P("tp", None),
        P("tp"),
        P("tp"),
    )
    return jax.shard_map(
        per_device, mesh=mesh, in_specs=placed, out_specs=P(None, "ctx", "tp"), check_vma=False
    )
```

time: 104 us -> 93.4 us (0.90)
  blocking collectives: 0 us -> 13.8 us
  local copies, waits for them, and re-layouts: 15.3 us -> 3.67 us
  waiting for transfers between devices: 17.7 us -> 6.52 us
  Pallas kernels: 37.3 us -> 30.7 us
  starting transfers between devices: 32.8 us -> 38 us
    all_to_all x1, waiting for transfers between devices: 14 us -> 0.01 us  [per_device(): lax.all_to_all(states, 'ctx', split_axis=0, concat_axis=0, tiled=True)]
    all_to_all x0 -> x1, blocking collectives: none -> 13.8 us  [per_device(): shares = lax.all_to_all(sums, 'tp', split_axis=0, concat_axis=0, tiled=True)]
    all_to_all x1, starting transfers between devices: 3.84 us -> 14.7 us  [per_device(): lax.all_to_all(entering, 'ctx', split_axis=0, concat_axis=0, tiled=True)]
    unnamed x41 -> x23, local copies, waits for them, and re-layouts: 13.2 us -> 3.58 us
    all_to_all x1 -> x0, starting transfers between devices: 7.85 us -> none  [per_device(): shares = lax.all_to_all(sums, 'tp', split_axis=0, concat_axis=0, tiled=True)]
    pallas_call x6 -> x8, Pallas kernels: 37.3 us -> 30.7 us  [the longest x1 12.4 us: per_device(): pl.pallas_call(local_kernel, grid=(tiles,), in_specs=[flat(border_rows),...]
    ppermute x1, waiting for transfers between devices: 0.01 us -> 4.9 us  [per_device(): lax.ppermute(border, 'ctx', [(i, i + 1) for i in range(chunks - 1)])]
    all_to_all x1 -> x0, waiting for transfers between devices: 3.7 us -> none  [per_device(): shares = lax.all_to_all(sums, 'tp', split_axis=0, concat_axis=0, tiled=True)]
  transfers between devices with their start and end apart: 4 -> 3, of which waited for: 2 -> 2; matrix products, arithmetic and copies ran while one was open for 1% -> 0% of each run, Pallas kernels for 27% -> 21%
where the time goes in v2:
time: 93.4 us; the launch traced here: 92.8 us
  starting transfers between devices  38 us (41%)
  Pallas kernels  30.7 us (33%)
  blocking collectives  13.8 us (15%)
  waiting for transfers between devices  6.52 us (7%)
  local copies, waits for them, and re-layouts  3.67 us (4%)
    all_to_all x1, starting transfers between devices, per_device(): lax.all_to_all(states, 'ctx', split_axis=0, concat_axis=0, tiled=True)  18.5 us
    all_to_all x1, starting transfers between devices, per_device(): lax.all_to_all(entering, 'ctx', split_axis=0, concat_axis=0, tiled=True)  14.7 us
    all_to_all x1, blocking collectives, per_device(): shares = lax.all_to_all(sums, 'tp', split_axis=0, concat_axis=0, tiled=True)  13.8 us
    pallas_call x1, Pallas kernels, per_device(): pl.pallas_call(local_kernel, grid=(tiles,), in_specs=[flat(border_rows),...  12.4 us
    pallas_call x1, Pallas kernels, per_device(): pl.pallas_call(states_step, grid=(2,), in_specs=[whole, slab, slab], out_...  6.58 us
    ppermute x1, waiting for transfers between devices, per_device(): lax.ppermute(border, 'ctx', [(i, i + 1) for i in range(chunks - 1)])  4.9 us
    ppermute x1, starting transfers between devices, per_device(): lax.ppermute(border, 'ctx', [(i, i + 1) for i in range(chunks - 1)])  4.78 us
    pallas_call x1, Pallas kernels, per_device(): pl.pallas_call(border_step, grid=(tiles,), in_specs=[whole, cube(), cube(...  4.25 us
  transfers between devices with their start and end apart: 3, of which 2 were waited for; matrix products, arithmetic and copies ran while one was open for 0% of the time, Pallas kernels for 21%

profile of v2, /device:TPU:1, one launch (start us, length us, event | category | flops | bytes accessed | tf_op | source)
XLA Modules:
  0.0 92.8 jit_solution(15881730425746686645)
XLA Ops:
  0.0 0.0 copy-start.7
  0.0 0.0 copy-start.8
  0.0 6.6 %states.1 = f32[32,1,512]{2,1,0:T(1,128)} custom-call(f32[16,32]{1,0:T(8,128)} %bitcast.6, bf16[2,512,512]{2,1,0:T(8,128)(2,1)} %key_ref.4, bf16[2,512,512]{2,1,0:T(8,128)(2,1)} %value_ref.4), custom_call_target="tpu_custom_call" | custom-call | tf_op jit(solution)/shard_map/states/pallas_call | solution.py:362
  6.6 18.5 %all-to-all-start = ((f32[32,1,512]{2,1,0:T(1,128)}), f32[32,1,512]{2,1,0:T(1,128)S(1)}, u32[]{:S(2)}, u32[]{:S(2)}) async-start(f32[32,1,512]{2,1,0:T(1,128)} %states.1), calls=%async_computation | async-start | bytes 131072 | tf_op jit(solution)/shard_map/all_to_all | solution.py:371
  25.1 4.3 %border.1 = bf16[320,512]{1,0:T(8,128)(2,1)} custom-call(f32[16,32]{1,0:T(8,128)} %bitcast.7, bf16[2,512,512]{2,1,0:T(8,128)(2,1)} %key_ref.4, bf16[2,512,512]{2,1,0:T(8,128)(2,1)} %value_ref.4), custom_call_target="tpu_custom_call" | custom-call | flops 400000000 | bytes 3145728 | tf_op jit(solution)/shard_map/border/pallas_call | solution.py:377
  29.3 0.0 copy-start.10
  29.3 4.8 %collective-permute-start = (bf16[320,512]{1,0:T(8,128)(2,1)}, bf16[320,512]{1,0:T(8,128)(2,1)S(1)}, u32[]{:S(2)}, u32[]{:S(2)}) collective-permute-start(bf16[320,512]{1,0:T(8,128)(2,1)} %border.1), channel_id=1, source_target_pairs={{0,16},{16,32},{32,48},{48,64},{64,80},{80,96},{96,112},{112,128},... | collective-permute-start | bytes 983048 | tf_op jit(solution)/shard_map/ppermute | solution.py:389
  34.1 0.0 copy-done.7
  34.1 0.0 copy-done.8
  34.1 1.1 %embed.1 = (bf16[2,512,512]{2,1,0:T(8,128)(2,1)S(1)}, f32[8,128]{1,0:T(8,128)S(1)}) custom-call(s32[2,512]{1,0:T(2,128)S(1)} %copy-done.8, bf16[512,512]{1,0:T(8,128)(2,1)S(1)} %copy-done.7), custom_call_target="tpu_custom_call" | custom-call | flops 10737418240 | bytes 4194304 | tf_op jit(solution)/shard_map/embed/pallas_call | solution.py:404
  35.2 0.0 copy-done.10
  35.2 0.1 copy.14.rate_ref
  35.3 0.1 reshape.14.rate_ref
  35.4 4.9 %collective-permute-done.border_ref = bf16[320,512]{1,0:T(8,128)(2,1)S(1)} collective-permute-done((bf16[320,512]{1,0:T(8,128)(2,1)}, bf16[320,512]{1,0:T(8,128)(2,1)S(1)}, u32[]{:S(2)}, u32[]{:S(2)}) %collective-permute-start) | collective-permute-done | bytes 327712 | tf_op jit(solution)/shard_map/ppermute | solution.py:389
  40.3 0.0 copy-start.9
  40.3 0.7 copy-done.9
  41.0 1.5 %early.1 = (f32[32,512]{1,0:T(8,128)}, f32[8,128]{1,0:T(8,128)}) custom-call(bf16[320,512]{1,0:T(8,128)(2,1)} %copy-done.9), custom_call_target="tpu_custom_call" | custom-call | tf_op jit(solution)/shard_map/early/pallas_call | solution.py:391
  42.5 0.0 all-to-all-done.state_ref
  42.5 0.0 copy-start.4
  42.5 0.7 copy-done.4
  43.2 0.8 scan.1
  44.0 14.7 %all-to-all-start.1 = ((f32[32,1,512]{2,1,0:T(1,128)}), f32[32,1,512]{2,1,0:T(1,128)S(1)}, u32[]{:S(2)}, u32[]{:S(2)}) async-start(f32[32,1,512]{2,1,0:T(1,128)} %scan.1), calls=%async_computation.1 | async-start | bytes 131072 | tf_op jit(solution)/shard_map/all_to_all | solution.py:453
  58.7 0.0 copy-start
  58.7 0.0 copy-start.2
  58.7 12.4 %local.1 = (bf16[2,512,512]{2,1,0:T(8,128)(2,1)}, f32[32,512]{1,0:T(8,128)}) custom-call(bf16[320,512]{1,0:T(8,128)(2,1)} %copy-done.9, bf16[2,512,512]{2,1,0:T(8,128)(2,1)} %key_ref.4, bf16[2,512,512]{2,1,0:T(8,128)(2,1)} %value_ref.4, bf16[32,128]{1,0:T(8,128)(2,1)} %filter_ref.1, f32[16,32]{1,0:T(8,128)} %bitcast.8, f32[16,32]{1,0:T(8,128)} %bitcast.9, ...), custom_call_target="tpu_custom_call" | custom-call | flops 12000000000 | bytes 8388608 | tf_op jit(solution)/shard_map/local/pallas_call | solution.py:414
  71.1 0.0 copy-start.5
  71.2 0.0 copy-start.6
  71.2 1.6 %all-to-all-done.1.carried_ref = f32[32,1,512]{2,1,0:T(1,128)S(1)} async-done(((f32[32,1,512]{2,1,0:T(1,128)}), f32[32,1,512]{2,1,0:T(1,128)S(1)}, u32[]{:S(2)}, u32[]{:S(2)}) %all-to-all-start.1) | async-done | bytes 65568 | tf_op jit(solution)/shard_map/all_to_all | solution.py:453
  72.8 0.0 copy-done
  72.8 0.0 copy-done.2
  72.8 0.0 copy-start.1
  72.8 1.2 %copy-done.1 = bf16[2,512,512]{2,1,0:T(8,128)(2,1)S(1)} copy-done((bf16[2,512,512]{2,1,0:T(8,128)(2,1)S(1)}, bf16[2,512,512]{2,1,0:T(8,128)(2,1)}, u32[]{:S(2)}) %copy-start.1) | copy-done | bytes 1048600
  74.0 0.0 copy-start.3
  74.0 0.8 copy-done.3
  74.9 2.2 %gate.1 = (f32[2,512,512]{2,1,0:T(8,128)S(1)}, f32[16,1,1024]{2,1,0:T(1,128)S(1)}) custom-call(f32[32,1,512]{2,1,0:T(1,128)S(1)} %all-to-all-done.1.carried_ref, f32[32,512]{1,0:T(8,128)S(1)} %copy-done.2, f32[32,512]{1,0:T(8,128)S(1)} %copy-done.3, f32[1,512]{1,0:T(1,128)S(1)} %reshape.14.rate_ref, bf16[2,512,512]{2,1,0:T(8,128)(2,1)S(1)} %copy-done.1, ...), custom_call_target="tpu_custom_call" | custom-call | tf_op jit(solution)/shard_map/gate/pallas_call | solution.py:457
  77.1 13.8 %all_to_all.15.refs_2_ = f32[16,1,1024]{2,1,0:T(1,128)S(1)} all-to-all(f32[16,1,1024]{2,1,0:T(1,128)S(1)} %get-tuple-element.22), channel_id=1, replica_groups=mesh['ctx'=32,'tp'=16] {'tp'}, dimensions={0} | all-to-all | bytes 131072 | tf_op jit(solution)/shard_map/all_to_all | solution.py:473
  90.9 0.0 copy-done.5
  90.9 0.0 copy-done.6
  90.9 1.9 %norm.1 = bf16[2,512,512]{2,1,0:T(8,128)(2,1)} custom-call(s32[2]{0:T(128)S(1)} %copy-done.6, s32[1]{0:T(128)} %bitcast.first_ref.refs_1_, f32[16,1,1024]{2,1,0:T(1,128)S(1)} %all_to_all.15.refs_2_, f32[2,512,512]{2,1,0:T(8,128)S(1)} %get-tuple-element.23.refs_3_, bf16[2,512,512]{2,1,0:T(8,128)(2,1)S(1)} %get-tuple-element.24.refs_4_, f32[1,512]{1,0:T(1,128)S(1)} %bitcast.5), custom_call_target="tpu_custom_call" | custom-call | tf_op jit(solution)/shard_map/norm/pallas_call | solution.py:478
Async XLA Ops:
  0.0 34.1 %copy-start.7 = (bf16[512,512]{1,0:T(8,128)(2,1)S(1)}, bf16[512,512]{1,0:T(8,128)(2,1)}, u32[]{:S(2)}) copy-start(bf16[512,512]{1,0:T(8,128)(2,1)} %table_ref.1) | copy-start | bytes 1572868
  0.0 34.1 %copy-start.8 = (s32[2,512]{1,0:T(2,128)S(1)}, s32[2,512]{1,0:T(2,128)}, u32[]{:S(2)}) copy-start(s32[2,512]{1,0:T(2,128)} %token_ref.1) | copy-start | bytes 12292
  6.6 35.9 %all-to-all-start = ((f32[32,1,512]{2,1,0:T(1,128)}), f32[32,1,512]{2,1,0:T(1,128)S(1)}, u32[]{:S(2)}, u32[]{:S(2)}) async-start(f32[32,1,512]{2,1,0:T(1,128)} %states.1), calls=%async_computation | async-start | bytes 131072 | tf_op jit(solution)/shard_map/all_to_all | solution.py:371
  29.3 5.9 %copy-start.10 = (f32[32,16]{0,1:T(8,128)S(1)}, f32[32,16]{0,1:T(8,128)}, u32[]{:S(2)}) copy-start(f32[32,16]{0,1:T(8,128)} %param.18) | copy-start | bytes 6148
  29.3 11.0 %collective-permute-start = (bf16[320,512]{1,0:T(8,128)(2,1)}, bf16[320,512]{1,0:T(8,128)(2,1)S(1)}, u32[]{:S(2)}, u32[]{:S(2)}) collective-permute-start(bf16[320,512]{1,0:T(8,128)(2,1)} %border.1), channel_id=1, source_target_pairs={{0,16},{16,32},{32,48},{48,64},{64,80},{80,96},{96,112},{112,128},... | collective-permute-start | bytes 983048 | tf_op jit(solution)/shard_map/ppermute | solution.py:389
  40.3 0.7 copy-start.9
  42.5 0.7 copy-start.4
  44.0 28.8 %all-to-all-start.1 = ((f32[32,1,512]{2,1,0:T(1,128)}), f32[32,1,512]{2,1,0:T(1,128)S(1)}, u32[]{:S(2)}, u32[]{:S(2)}) async-start(f32[32,1,512]{2,1,0:T(1,128)} %scan.1), calls=%async_computation.1 | async-start | bytes 131072 | tf_op jit(solution)/shard_map/all_to_all | solution.py:453
  58.7 14.1 %copy-start = (bf16[2,512,512]{2,1,0:T(8,128)(2,1)S(1)}, bf16[2,512,512]{2,1,0:T(8,128)(2,1)}, u32[]{:S(2)}) copy-start(bf16[2,512,512]{2,1,0:T(8,128)(2,1)} %query_source.1) | copy-start | bytes 3145732
  58.7 14.1 %copy-start.2 = (f32[32,512]{1,0:T(8,128)S(1)}, f32[32,512]{1,0:T(8,128)}, u32[]{:S(2)}) copy-start(f32[32,512]{1,0:T(8,128)} %get-tuple-element.19.early_ref) | copy-start | bytes 196612
  71.1 19.8 %copy-start.5 = (f32[512]{0:T(512)S(1)}, f32[512]{0:T(512)}, u32[]{:S(2)}) copy-start(f32[512]{0:T(512)} %param.21) | copy-start | bytes 6148
  71.2 19.8 %copy-start.6 = (s32[2]{0:T(128)S(1)}, s32[2]{0:T(128)}, u32[]{:S(2)}) copy-start(s32[2]{0:T(128)} %refs_0_.1) | copy-start | bytes 28
  72.8 1.2 %copy-start.1 = (bf16[2,512,512]{2,1,0:T(8,128)(2,1)S(1)}, bf16[2,512,512]{2,1,0:T(8,128)(2,1)}, u32[]{:S(2)}) copy-start(bf16[2,512,512]{2,1,0:T(8,128)(2,1)} %get-tuple-element.21.base_source) | copy-start | bytes 3145732
  74.0 0.8 copy-start.3

commit v3 on v2

--- a/solution.py
+++ b/solution.py
@@ -42,59 +42,51 @@
     return jnp.concatenate(parts, axis=0)
 
 
-def product_of(key_ref, value_ref, s):
-    return (key_ref[s].astype(F32) * value_ref[s].astype(F32)).astype(BF16)
-
-
-def states_kernel(rate_ref, key_ref, value_ref, state_ref, *, rows):
-    samples, here, width = key_ref.shape
+def product_of(key, value):
+    return (key.astype(F32) * value.astype(F32)).astype(BF16)
+
+
+def states_kernel(
+    rate_ref, key_source, value_source, state_ref, border_ref, key_ref, value_ref, arrived, *, taps
+):
+    samples, rows, width = key_ref.shape
     modes = rate_ref.shape[0]
-    step = pl.program_id(0)
-    first = (rows - 1 - step * here).astype(F32)
-    lag = first - iota((1, here), 1, F32)
-    for tile in range(width // LANES):
-        lanes = slice(tile * LANES, (tile + 1) * LANES)
-        weights = jnp.exp(-tile_column(rate_ref[...], tile) * lag)
-        weights = jnp.concatenate(halves(weights), axis=0)
+    tiles = [slice(first, first + LANES) for first in range(0, width, LANES)]
+    loads = []
+    for tile, lanes in enumerate(tiles):
+        pair = (
+            pltpu.make_async_copy(
+                key_source.at[:, :, lanes], key_ref.at[:, :, lanes], arrived.at[0, tile]
+            ),
+            pltpu.make_async_copy(
+                value_source.at[:, :, lanes], value_ref.at[:, :, lanes], arrived.at[1, tile]
+            ),
+        )
+        for load in pair:
+            load.start()
+        loads.append(pair)
+    for tile, lanes in enumerate(tiles):
+        groups = range(tile * TILE_GROUPS, (tile + 1) * TILE_GROUPS)
+        rate = jnp.concatenate([rate_ref[:, g : g + 1] for g in groups], axis=0)
+        weights = [jnp.exp(-rate * (taps - 1.0 - iota((1, taps), 1, F32)))]
+        step = jnp.exp(-rate * float(taps))
+        for _ in range(rows // taps - 1):
+            weights.insert(0, weights[0] * step)
+        weights = jnp.concatenate(halves(jnp.concatenate(weights, axis=1)), axis=0)
         half = weights.shape[0] // 2
+        for load in loads[tile]:
+            load.wait()
         for s in range(samples):
-            key, value = key_ref[s, :, lanes].astype(F32), value_ref[s, :, lanes].astype(F32)
-            full = dot(weights, (key * value).astype(BF16))
-            state = own_group(full[:half] + full[half:], modes).reshape(modes, 1, LANES)
-            part = slice(s * modes, (s + 1) * modes)
-
-            @pl.when(step == 0)
-            def _():
-                state_ref[part, :, lanes] = state
-
-            @pl.when(step > 0)
-            def _():
-                state_ref[part, :, lanes] = state_ref[part, :, lanes] + state
-
-
-def border_kernel(rate_ref, key_ref, value_ref, border_ref, *, taps):
-    samples, rows, _ = key_ref.shape
-    modes = rate_ref.shape[0]
-    early = rows - taps
-    rate = tile_column(rate_ref[...], pl.program_id(0))
-    weights = jnp.exp(-rate * (early - 1.0 - iota((1, early), 1, F32)))
-    weights = jnp.concatenate(halves(weights), axis=0)
-    half = weights.shape[0] // 2
-    for s in range(samples):
-        product = product_of(key_ref, value_ref, s)
-        border_ref[s * taps : (s + 1) * taps, :] = product[early:]
-        full = dot(weights, product[:early])
-        upper, lower = halves(own_group(full[:half] + full[half:], modes))
-        first = samples * taps + s * modes
-        border_ref[first : first + modes, :] = upper
-        border_ref[first + samples * modes : first + (samples + 1) * modes, :] = lower
-
-
-def early_kernel(border_ref, out_ref, mark_ref):
-    mark_ref[...] = jnp.zeros_like(mark_ref)
-    height = out_ref.shape[0]
-    upper = border_ref[:height, :].astype(F32)
-    out_ref[...] = upper + border_ref[height:, :].astype(F32)
+            product = product_of(key_ref[s, :, lanes], value_ref[s, :, lanes])
+            full = dot(weights, product)
+            state = own_group(full[:half] + full[half:], modes)
+            state_ref[s * modes : (s + 1) * modes, :, lanes] = state.reshape(modes, 1, LANES)
+            border_ref[s * taps : (s + 1) * taps, lanes] = product[rows - taps :]
+            early = dot(weights[:, taps:], product[: rows - taps])
+            upper, lower = halves(own_group(early[:half] + early[half:], modes))
+            first = samples * taps + s * modes
+            border_ref[first : first + modes, lanes] = upper
+            border_ref[first + samples * modes : first + (samples + 1) * modes, lanes] = lower
 
 
 def scan_kernel(first_ref, rate_ref, state_ref, out_ref, *, chunks, rows):
@@ -161,7 +153,7 @@
         mixed_window[s, :, :before] = jnp.zeros((LANES, before), BF16)
         border = border_ref[s * taps : (s + 1) * taps, :].astype(F32)
         product_window[s, :, taps : 2 * taps] = border.T.astype(BF16)
-        product = product_of(key_ref, value_ref, s).astype(F32)
+        product = product_of(key_ref[s], value_ref[s]).astype(F32)
         product_window[s, :, 2 * taps :] = product.T.astype(BF16)
 
     skip = jnp.broadcast_to(skip_ref[...], (8, LANES)).T[:, :1]
@@ -211,8 +203,7 @@
     factor_ref[modes:, :] = own_group(jnp.broadcast_to(gain, square), modes)
 
 
-def embed_kernel(token_ref, table_ref, out_ref, mark_ref):
-    mark_ref[...] = jnp.zeros_like(mark_ref)
+def embed_kernel(token_ref, table_ref, out_ref):
     samples, rows = token_ref.shape
     vocab = table_ref.shape[0]
     for s in range(samples):
@@ -223,7 +214,7 @@
 
 def gate_kernel(
     carried_ref,
-    early_ref,
+    before_ref,
     factor_ref,
     rate_ref,
     base_source,
@@ -238,6 +229,7 @@
     samples, rows, width = base_ref.shape
     modes = factor_ref.shape[0] // 2
     copies = sum_ref.shape[0]
+    early_at = before_ref.shape[0] - 2 * samples * modes
     own = iota((LANES, LANES), 0) // modes == iota((LANES, LANES), 1) // GROUP
     tiles = [slice(first, first + LANES) for first in range(0, width, LANES)]
     loads = []
@@ -267,7 +259,11 @@
         for s in range(samples):
             part = slice(s * modes, (s + 1) * modes)
             carried = carried_ref[part, :, lanes].reshape(modes, LANES)
-            state = factor_ref[:modes, lanes] * carried + early_ref[part, lanes]
+            first = early_at + s * modes
+            early = before_ref[first : first + modes, lanes].astype(F32)
+            first = first + samples * modes
+            early = early + before_ref[first : first + modes, lanes].astype(F32)
+            state = factor_ref[:modes, lanes] * carried + early
             state = state * factor_ref[modes:, lanes]
             spread = jnp.concatenate([state] * TILE_GROUPS, axis=0)
             upper, lower = halves(jnp.where(own, spread, 0.0))
@@ -313,7 +309,7 @@
 
 
 def params(mebibytes):
-    return pltpu.CompilerParams(vmem_limit_bytes=mebibytes << 20)
+    return pltpu.CompilerParams(vmem_limit_bytes=int(mebibytes * (1 << 20)))
 
 
 def per_device(
@@ -350,62 +346,39 @@
 
     state_rows = samples * modes
     border_rows = samples * taps + 2 * state_rows
-    early_at = samples * taps // (2 * state_rows)
     shape = jax.ShapeDtypeStruct
     whole = pl.BlockSpec((modes, groups), lambda i: (0, 0))
     rates = decay_rates.T
 
-    def states_step(rate_ref, key_ref, value_ref, state_ref):
-        states_kernel(rate_ref, key_ref, value_ref, state_ref, rows=rows)
-
-    slab = pl.BlockSpec((samples, rows // 2, width), lambda i: (0, i, 0))
-    states = pl.pallas_call(
+    vmem = pl.BlockSpec(memory_space=pltpu.VMEM)
+    anywhere = pl.BlockSpec(memory_space=pl.ANY)
+
+    def states_step(*refs):
+        states_kernel(*refs, taps=taps)
+
+    states, border = pl.pallas_call(
         states_step,
-        grid=(2,),
-        in_specs=[whole, slab, slab],
-        out_specs=pl.BlockSpec((state_rows, 1, width), lambda i: (0, 0, 0)),
-        out_shape=shape((state_rows, 1, width), F32),
+        in_specs=[vmem, anywhere, anywhere],
+        out_shape=[
+            shape((state_rows, 1, width), F32),
+            shape((border_rows, width), BF16),
+        ],
+        scratch_shapes=[
+            pltpu.VMEM((samples, rows, width), BF16),
+            pltpu.VMEM((samples, rows, width), BF16),
+            pltpu.SemaphoreType.DMA((2, tiles)),
+        ],
         compiler_params=params(60),
         name="states",
     )(rates, key_act, value_act)
+    before = lax.ppermute(border, "ctx", [(i, i + 1) for i in range(chunks - 1)])
     gathered = lax.all_to_all(states, "ctx", split_axis=0, concat_axis=0, tiled=True)
 
-    def border_step(rate_ref, key_ref, value_ref, border_ref):
-        border_kernel(rate_ref, key_ref, value_ref, border_ref, taps=taps)
-
-    key_late, value_late, _ = lax.optimization_barrier((key_act, value_act, states))
-    border = pl.pallas_call(
-        border_step,
-        grid=(tiles,),
-        in_specs=[whole, cube(), cube()],
-        out_specs=flat(border_rows),
-        out_shape=shape((border_rows, width), BF16),
+    embedded = pl.pallas_call(
+        embed_kernel,
+        out_shape=shape((samples, rows, width), BF16),
         cost_estimate=pl.CostEstimate(
-            flops=400_000_000, bytes_accessed=3 << 20, transcendentals=1 << 18
-        ),
-        compiler_params=params(60),
-        name="border",
-    )(rates, key_late, value_late)
-    before = lax.ppermute(border, "ctx", [(i, i + 1) for i in range(chunks - 1)])
-
-    early, early_mark = pl.pallas_call(
-        early_kernel,
-        grid=(1,),
-        in_specs=[pl.BlockSpec((2 * state_rows, width), lambda i: (early_at, 0))],
-        out_specs=[
-            pl.BlockSpec((state_rows, width), lambda i: (0, 0)),
-            pl.BlockSpec((8, LANES), lambda i: (0, 0)),
-        ],
-        out_shape=[shape((state_rows, width), F32), shape((8, LANES), F32)],
-        compiler_params=params(60),
-        name="early",
-    )(before)
-
-    embedded, embed_mark = pl.pallas_call(
-        embed_kernel,
-        out_shape=[shape((samples, rows, width), BF16), shape((8, LANES), F32)],
-        cost_estimate=pl.CostEstimate(
-            flops=40 * samples * rows * width * vocab, bytes_accessed=4 << 20, transcendentals=0
+            flops=2 * samples * rows * width * vocab, bytes_accessed=4 << 20, transcendentals=0
         ),
         compiler_params=params(16),
         name="embed",
@@ -440,20 +413,18 @@
         skip_gain.reshape(1, width),
     )
 
-    def scan(first_ref, rate_ref, state_ref, early_ref, embed_ref, out_ref):
+    def scan(first_ref, rate_ref, state_ref, out_ref):
         scan_kernel(first_ref, rate_ref, state_ref, out_ref, chunks=chunks, rows=rows)
 
     entering = pl.pallas_call(
         scan,
-        in_specs=[smem, pl.BlockSpec(), pl.BlockSpec(), pl.BlockSpec(), pl.BlockSpec()],
+        in_specs=[smem, vmem, vmem],
         out_shape=shape((state_rows, 1, width), F32),
         compiler_params=params(8),
         name="scan",
-    )(index, decay_rates, gathered, early_mark, embed_mark)
+    )(index, decay_rates, gathered)
     carried = lax.all_to_all(entering, "ctx", split_axis=0, concat_axis=0, tiled=True)
 
-    vmem = pl.BlockSpec(memory_space=pltpu.VMEM)
-    anywhere = pl.BlockSpec(memory_space=pl.ANY)
     gated, sums = pl.pallas_call(
         gate_kernel,
         in_specs=[vmem, vmem, vmem, vmem, anywhere, anywhere],
@@ -469,7 +440,7 @@
         ],
         compiler_params=params(16),
         name="gate",
-    )(carried, early, factors, decay_rates.reshape(1, groups * modes), base, query_act)
+    )(carried, before, factors, decay_rates.reshape(1, groups * modes), base, query_act)
     shares = lax.all_to_all(sums, "tp", split_axis=0, concat_axis=0, tiled=True)
 
     def norm(*refs):

time: 93.4 us -> 81.4 us (0.87)
  blocking collectives: 13.8 us -> 0 us
  waiting for transfers between devices: 6.52 us -> 18.5 us
  Pallas kernels: 30.7 us -> 23.3 us
  starting transfers between devices: 38 us -> 34 us
  local copies, waits for them, and re-layouts: 3.67 us -> 4.97 us
    all_to_all x1, waiting for transfers between devices: 0.01 us -> 13.9 us  [per_device(): lax.all_to_all(states, 'ctx', split_axis=0, concat_axis=0, tiled=True)]
    all_to_all x1 -> x0, blocking collectives: 13.8 us -> none  [per_device(): shares = lax.all_to_all(sums, 'tp', split_axis=0, concat_axis=0, tiled=True)]
    all_to_all x1, starting transfers between devices: 14.7 us -> 3.8 us  [per_device(): lax.all_to_all(entering, 'ctx', split_axis=0, concat_axis=0, tiled=True)]
    all_to_all x0 -> x1, starting transfers between devices: none -> 9.1 us  [per_device(): shares = lax.all_to_all(sums, 'tp', split_axis=0, concat_axis=0, tiled=True)]
    pallas_call x5 -> x3, Pallas kernels: 14.1 us -> 6.12 us  [the longest x1 4.28 us: per_device(): pl.pallas_call(states_step, in_specs=[vmem, anywhere, anywhere], out_shap...]
    ppermute x1, waiting for transfers between devices: 4.9 us -> 0.01 us  [per_device(): lax.ppermute(border, 'ctx', [(i, i + 1) for i in range(chunks - 1)])]
    all_to_all x0 -> x1, waiting for transfers between devices: none -> 3.71 us  [per_device(): shares = lax.all_to_all(sums, 'tp', split_axis=0, concat_axis=0, tiled=True)]
    all_to_all x1, starting transfers between devices: 18.5 us -> 15.6 us  [per_device(): lax.all_to_all(states, 'ctx', split_axis=0, concat_axis=0, tiled=True)]
  transfers between devices with their start and end apart: 3 -> 4, of which waited for: 2 -> 3; matrix products, arithmetic and copies ran while one was open for 0% -> 0% of each run, Pallas kernels for 21% -> 18%
where the time goes in v3:
time: 81.4 us; the launch traced here: 80.9 us
  starting transfers between devices  34 us (42%)
  Pallas kernels  23.3 us (29%)
  waiting for transfers between devices  18.5 us (23%)
  local copies, waits for them, and re-layouts  4.97 us (6%)
    all_to_all x1, starting transfers between devices, per_device(): lax.all_to_all(states, 'ctx', split_axis=0, concat_axis=0, tiled=True)  15.6 us
    all_to_all x1, waiting for transfers between devices, per_device(): lax.all_to_all(states, 'ctx', split_axis=0, concat_axis=0, tiled=True)  13.9 us
    pallas_call x1, Pallas kernels, per_device(): pl.pallas_call(local_kernel, grid=(tiles,), in_specs=[flat(border_rows),...  12.4 us
    all_to_all x1, starting transfers between devices, per_device(): shares = lax.all_to_all(sums, 'tp', split_axis=0, concat_axis=0, tiled=True)  9.1 us
    ppermute x1, starting transfers between devices, per_device(): lax.ppermute(border, 'ctx', [(i, i + 1) for i in range(chunks - 1)])  5.5 us
    unnamed x21, local copies, waits for them, and re-layouts  4.89 us
    pallas_call x1, Pallas kernels, per_device(): pl.pallas_call(states_step, in_specs=[vmem, anywhere, anywhere], out_shap...  4.28 us
    all_to_all x1, starting transfers between devices, per_device(): lax.all_to_all(entering, 'ctx', split_axis=0, concat_axis=0, tiled=True)  3.8 us
  transfers between devices with their start and end apart: 4, of which 3 were waited for; matrix products, arithmetic and copies ran while one was open for 0% of the time, Pallas kernels for 18%

profile of v3, /device:TPU:1, one launch (start us, length us, event | category | flops | bytes accessed | tf_op | source)
XLA Modules:
  0.0 80.9 jit_solution(2244239659947652168)
XLA Ops:
  0.0 0.0 copy-start.9
  0.0 4.3 %states.1 = (f32[32,1,512]{2,1,0:T(1,128)}, bf16[320,512]{1,0:T(8,128)(2,1)}) custom-call(f32[16,32]{1,0:T(8,128)} %bitcast.6, bf16[2,512,512]{2,1,0:T(8,128)(2,1)} %key_ref.1, bf16[2,512,512]{2,1,0:T(8,128)(2,1)} %value_ref.1), custom_call_target="tpu_custom_call" | custom-call | tf_op jit(solution)/shard_map/states/pallas_call | solution.py:359
  4.3 5.5 %collective-permute-start = (bf16[320,512]{1,0:T(8,128)(2,1)}, bf16[320,512]{1,0:T(8,128)(2,1)S(1)}, u32[]{:S(2)}, u32[]{:S(2)}) collective-permute-start(bf16[320,512]{1,0:T(8,128)(2,1)} %get-tuple-element.12), channel_id=1, source_target_pairs={{0,16},{16,32},{32,48},{48,64},{64,80},{80,96},{96,112},{112,128},... | collective-permute-start | bytes 983048 | tf_op jit(solution)/shard_map/ppermute | solution.py:374
  9.8 15.6 %all-to-all-start = ((f32[32,1,512]{2,1,0:T(1,128)}), f32[32,1,512]{2,1,0:T(1,128)S(1)}, u32[]{:S(2)}, u32[]{:S(2)}) async-start(f32[32,1,512]{2,1,0:T(1,128)} %get-tuple-element.11), calls=%async_computation | async-start | bytes 131072 | tf_op jit(solution)/shard_map/all_to_all | solution.py:375
  25.4 0.0 copy-done.9
  25.4 0.1 copy.14.rate_ref
  25.5 0.1 reshape.14.rate_ref
  25.6 13.9 %all-to-all-done.state_ref = f32[32,1,512]{2,1,0:T(1,128)S(1)} async-done(((f32[32,1,512]{2,1,0:T(1,128)}), f32[32,1,512]{2,1,0:T(1,128)S(1)}, u32[]{:S(2)}, u32[]{:S(2)}) %all-to-all-start) | async-done | bytes 65568 | tf_op jit(solution)/shard_map/all_to_all | solution.py:375
  39.5 0.8 scan.1
  40.3 3.8 %all-to-all-start.1 = ((f32[32,1,512]{2,1,0:T(1,128)}), f32[32,1,512]{2,1,0:T(1,128)S(1)}, u32[]{:S(2)}, u32[]{:S(2)}) async-start(f32[32,1,512]{2,1,0:T(1,128)} %scan.1), calls=%async_computation.1 | async-start | bytes 131072 | tf_op jit(solution)/shard_map/all_to_all | solution.py:426
  44.1 0.0 collective-permute-done.border_ref.before_ref
  44.1 0.0 copy-start.2
  44.1 0.7 copy-done.2
  44.8 0.0 copy-start
  44.8 0.0 copy-start.8
  44.8 12.4 %local.1 = (bf16[2,512,512]{2,1,0:T(8,128)(2,1)}, f32[32,512]{1,0:T(8,128)}) custom-call(bf16[320,512]{1,0:T(8,128)(2,1)} %copy-done.2, bf16[2,512,512]{2,1,0:T(8,128)(2,1)} %key_ref.1, bf16[2,512,512]{2,1,0:T(8,128)(2,1)} %value_ref.1, bf16[32,128]{1,0:T(8,128)(2,1)} %filter_ref.1, f32[16,32]{1,0:T(8,128)} %bitcast.7, f32[16,32]{1,0:T(8,128)} %bitcast.8, ...), custom_call_target="tpu_custom_call" | custom-call | flops 12000000000 | bytes 8388608 | tf_op jit(solution)/shard_map/local/pallas_call | solution.py:387
  57.2 0.9 %all-to-all-done.1.carried_ref = f32[32,1,512]{2,1,0:T(1,128)S(1)} async-done(((f32[32,1,512]{2,1,0:T(1,128)}), f32[32,1,512]{2,1,0:T(1,128)S(1)}, u32[]{:S(2)}, u32[]{:S(2)}) %all-to-all-start.1) | async-done | bytes 65568 | tf_op jit(solution)/shard_map/all_to_all | solution.py:426
  58.1 0.0 copy-done
  58.1 0.0 copy-start.1
  58.1 1.2 %copy-done.1 = bf16[2,512,512]{2,1,0:T(8,128)(2,1)S(1)} copy-done((bf16[2,512,512]{2,1,0:T(8,128)(2,1)S(1)}, bf16[2,512,512]{2,1,0:T(8,128)(2,1)}, u32[]{:S(2)}) %copy-start.1) | copy-done | bytes 1048600
  59.3 0.0 copy-start.3
  59.3 1.0 %copy-done.3 = bf16[320,512]{1,0:T(8,128)(2,1)S(1)} copy-done((bf16[320,512]{1,0:T(8,128)(2,1)S(1)}, bf16[320,512]{1,0:T(8,128)(2,1)}, u32[]{:S(2)}) %copy-start.3) | copy-done | bytes 327704
  60.3 0.0 copy-start.4
  60.3 0.8 %copy-done.4 = f32[32,512]{1,0:T(8,128)S(1)} copy-done((f32[32,512]{1,0:T(8,128)S(1)}, f32[32,512]{1,0:T(8,128)}, u32[]{:S(2)}) %copy-start.4) | copy-done | bytes 65560
  61.1 0.0 copy-start.5
  61.1 0.0 copy-start.6
  61.1 2.8 %gate.1 = (f32[2,512,512]{2,1,0:T(8,128)S(1)}, f32[16,1,1024]{2,1,0:T(1,128)}) custom-call(f32[32,1,512]{2,1,0:T(1,128)S(1)} %all-to-all-done.1.carried_ref, bf16[320,512]{1,0:T(8,128)(2,1)S(1)} %copy-done.3, f32[32,512]{1,0:T(8,128)S(1)} %copy-done.4, f32[1,512]{1,0:T(1,128)S(1)} %reshape.14.rate_ref, bf16[2,512,512]{2,1,0:T(8,128)(2,1)S(1)} %copy-done.1, ...), custom_call_target="tpu_custom_call" | custom-call | tf_op jit(solution)/shard_map/gate/pallas_call | solution.py:428
  64.0 9.1 %all-to-all-start.2 = ((f32[16,1,1024]{2,1,0:T(1,128)}), f32[16,1,1024]{2,1,0:T(1,128)S(1)}, u32[]{:S(2)}, u32[]{:S(2)}) async-start(f32[16,1,1024]{2,1,0:T(1,128)} %get-tuple-element.15), calls=%async_computation.2 | async-start | bytes 131072 | tf_op jit(solution)/shard_map/all_to_all | solution.py:444
  73.1 0.0 copy-done.8
  73.1 0.0 copy-start.7
  73.1 1.0 %copy-done.7 = bf16[512,512]{1,0:T(8,128)(2,1)S(1)} copy-done((bf16[512,512]{1,0:T(8,128)(2,1)S(1)}, bf16[512,512]{1,0:T(8,128)(2,1)}, u32[]{:S(2)}) %copy-start.7) | copy-done | bytes 524312
  74.1 1.1 %embed.1.refs_4_ = bf16[2,512,512]{2,1,0:T(8,128)(2,1)S(1)} custom-call(s32[2,512]{1,0:T(2,128)S(1)} %copy-done.8, bf16[512,512]{1,0:T(8,128)(2,1)S(1)} %copy-done.7), custom_call_target="tpu_custom_call" | custom-call | flops 536870912 | bytes 4194304 | tf_op jit(solution)/shard_map/embed/pallas_call | solution.py:377
  75.2 3.7 %all-to-all-done.2.refs_2_ = f32[16,1,1024]{2,1,0:T(1,128)S(1)} async-done(((f32[16,1,1024]{2,1,0:T(1,128)}), f32[16,1,1024]{2,1,0:T(1,128)S(1)}, u32[]{:S(2)}, u32[]{:S(2)}) %all-to-all-start.2) | async-done | bytes 65568 | tf_op jit(solution)/shard_map/all_to_all | solution.py:444
  78.9 0.0 copy-done.5
  78.9 0.0 copy-done.6
  78.9 2.0 %norm.1 = bf16[2,512,512]{2,1,0:T(8,128)(2,1)} custom-call(s32[2]{0:T(128)S(1)} %copy-done.6, s32[1]{0:T(128)} %bitcast.first_ref.refs_1_, f32[16,1,1024]{2,1,0:T(1,128)S(1)} %all-to-all-done.2.refs_2_, f32[2,512,512]{2,1,0:T(8,128)S(1)} %get-tuple-element.16.refs_3_, bf16[2,512,512]{2,1,0:T(8,128)(2,1)S(1)} %embed.1.refs_4_, f32[1,512]{1,0:T(1,128)S(1)} %bitcast.5), custom_call_target="tpu_custom_call" | custom-call | tf_op jit(solution)/shard_map/norm/pallas_call | solution.py:449
Async XLA Ops:
  0.0 25.4 %copy-start.9 = (f32[32,16]{0,1:T(8,128)S(1)}, f32[32,16]{0,1:T(8,128)}, u32[]{:S(2)}) copy-start(f32[32,16]{0,1:T(8,128)} %param.18) | copy-start | bytes 6148
  4.3 39.8 %collective-permute-start = (bf16[320,512]{1,0:T(8,128)(2,1)}, bf16[320,512]{1,0:T(8,128)(2,1)S(1)}, u32[]{:S(2)}, u32[]{:S(2)}) collective-permute-start(bf16[320,512]{1,0:T(8,128)(2,1)} %get-tuple-element.12), channel_id=1, source_target_pairs={{0,16},{16,32},{32,48},{48,64},{64,80},{80,96},{96,112},{112,128},... | collective-permute-start | bytes 983048 | tf_op jit(solution)/shard_map/ppermute | solution.py:374
  9.8 29.7 %all-to-all-start = ((f32[32,1,512]{2,1,0:T(1,128)}), f32[32,1,512]{2,1,0:T(1,128)S(1)}, u32[]{:S(2)}, u32[]{:S(2)}) async-start(f32[32,1,512]{2,1,0:T(1,128)} %get-tuple-element.11), calls=%async_computation | async-start | bytes 131072 | tf_op jit(solution)/shard_map/all_to_all | solution.py:375
  40.3 17.8 %all-to-all-start.1 = ((f32[32,1,512]{2,1,0:T(1,128)}), f32[32,1,512]{2,1,0:T(1,128)S(1)}, u32[]{:S(2)}, u32[]{:S(2)}) async-start(f32[32,1,512]{2,1,0:T(1,128)} %scan.1), calls=%async_computation.1 | async-start | bytes 131072 | tf_op jit(solution)/shard_map/all_to_all | solution.py:426
  44.1 0.7 copy-start.2
  44.8 13.3 %copy-start = (bf16[2,512,512]{2,1,0:T(8,128)(2,1)S(1)}, bf16[2,512,512]{2,1,0:T(8,128)(2,1)}, u32[]{:S(2)}) copy-start(bf16[2,512,512]{2,1,0:T(8,128)(2,1)} %query_source.1) | copy-start | bytes 3145732
  44.8 28.3 %copy-start.8 = (s32[2,512]{1,0:T(2,128)S(1)}, s32[2,512]{1,0:T(2,128)}, u32[]{:S(2)}) copy-start(s32[2,512]{1,0:T(2,128)} %token_ref.1) | copy-start | bytes 12292
  58.1 1.2 %copy-start.1 = (bf16[2,512,512]{2,1,0:T(8,128)(2,1)S(1)}, bf16[2,512,512]{2,1,0:T(8,128)(2,1)}, u32[]{:S(2)}) copy-start(bf16[2,512,512]{2,1,0:T(8,128)(2,1)} %get-tuple-element.14.base_source) | copy-start | bytes 3145732
  59.3 1.0 %copy-start.3 = (bf16[320,512]{1,0:T(8,128)(2,1)S(1)}, bf16[320,512]{1,0:T(8,128)(2,1)}, u32[]{:S(2)}) copy-start(bf16[320,512]{1,0:T(8,128)(2,1)} %copy-done.2) | copy-start | bytes 983044
  60.3 0.8 %copy-start.4 = (f32[32,512]{1,0:T(8,128)S(1)}, f32[32,512]{1,0:T(8,128)}, u32[]{:S(2)}) copy-start(f32[32,512]{1,0:T(8,128)} %get-tuple-element.13.factor_ref) | copy-start | bytes 196612
  61.1 17.8 %copy-start.5 = (f32[512]{0:T(512)S(1)}, f32[512]{0:T(512)}, u32[]{:S(2)}) copy-start(f32[512]{0:T(512)} %param.21) | copy-start | bytes 6148
  61.1 17.8 %copy-start.6 = (s32[2]{0:T(128)S(1)}, s32[2]{0:T(128)}, u32[]{:S(2)}) copy-start(s32[2]{0:T(128)} %refs_0_.1) | copy-start | bytes 28
  64.0 14.9 %all-to-all-start.2 = ((f32[16,1,1024]{2,1,0:T(1,128)}), f32[16,1,1024]{2,1,0:T(1,128)S(1)}, u32[]{:S(2)}, u32[]{:S(2)}) async-start(f32[16,1,1024]{2,1,0:T(1,128)} %get-tuple-element.15), calls=%async_computation.2 | async-start | bytes 131072 | tf_op jit(solution)/shard_map/all_to_all | solution.py:444
  73.1 1.0 %copy-start.7 = (bf16[512,512]{1,0:T(8,128)(2,1)S(1)}, bf16[512,512]{1,0:T(8,128)(2,1)}, u32[]{:S(2)}) copy-start(bf16[512,512]{1,0:T(8,128)(2,1)} %table_ref.1) | copy-start | bytes 1572868

commit v4 on v3

--- a/solution.py
+++ b/solution.py
@@ -47,12 +47,28 @@
 
 
 def states_kernel(
-    rate_ref, key_source, value_source, state_ref, border_ref, key_ref, value_ref, arrived, *, taps
+    rate_source,
+    key_source,
+    value_source,
+    state_target,
+    border_target,
+    rate_ref,
+    key_ref,
+    value_ref,
+    state_ref,
+    border_ref,
+    ready,
+    arrived,
+    left,
+    *,
+    taps,
 ):
     samples, rows, width = key_ref.shape
     modes = rate_ref.shape[0]
     tiles = [slice(first, first + LANES) for first in range(0, width, LANES)]
-    loads = []
+    rate_load = pltpu.make_async_copy(rate_source, rate_ref, ready.at[0])
+    rate_load.start()
+    loads, stores = [], []
     for tile, lanes in enumerate(tiles):
         pair = (
             pltpu.make_async_copy(
@@ -65,14 +81,18 @@
         for load in pair:
             load.start()
         loads.append(pair)
-    for tile, lanes in enumerate(tiles):
+    rate_load.wait()
+    tables = []
+    for tile in range(len(tiles)):
         groups = range(tile * TILE_GROUPS, (tile + 1) * TILE_GROUPS)
         rate = jnp.concatenate([rate_ref[:, g : g + 1] for g in groups], axis=0)
         weights = [jnp.exp(-rate * (taps - 1.0 - iota((1, taps), 1, F32)))]
         step = jnp.exp(-rate * float(taps))
         for _ in range(rows // taps - 1):
             weights.insert(0, weights[0] * step)
-        weights = jnp.concatenate(halves(jnp.concatenate(weights, axis=1)), axis=0)
+        tables.append(jnp.concatenate(halves(jnp.concatenate(weights, axis=1)), axis=0))
+    for tile, lanes in enumerate(tiles):
+        weights = tables[tile]
         half = weights.shape[0] // 2
         for load in loads[tile]:
             load.wait()
@@ -87,6 +107,19 @@
             first = samples * taps + s * modes
             border_ref[first : first + modes, lanes] = upper
             border_ref[first + samples * modes : first + (samples + 1) * modes, lanes] = lower
+        pair = (
+            pltpu.make_async_copy(
+                state_ref.at[:, :, lanes], state_target.at[:, :, lanes], left.at[0, tile]
+            ),
+            pltpu.make_async_copy(
+                border_ref.at[:, lanes], border_target.at[:, lanes], left.at[1, tile]
+            ),
+        )
+        for store in pair:
+            store.start()
+            stores.append(store)
+    for store in stores:
+        store.wait()
 
 
 def scan_kernel(first_ref, rate_ref, state_ref, out_ref, *, chunks, rows):
@@ -114,6 +147,7 @@
 
 
 def local_kernel(
+    index_ref,
     border_ref,
     key_ref,
     value_ref,
@@ -122,7 +156,7 @@
     residue_ref,
     skip_ref,
     base_ref,
-    factor_ref,
+    turn_ref,
     product_window,
     mixed_window,
     turned,
@@ -189,7 +223,7 @@
                     first : first + GROUP
                 ] + skip[channels] * mixed[at : at + GROUP].astype(F32)
     for s in range(samples):
-        base_ref[s] = turned[s].T.astype(BF16)
+        base_ref[s * rows : (s + 1) * rows, :] = turned[s].T.astype(BF16)
 
     tap_weights = jnp.exp(-rate * (taps - iota((1, taps), 1, F32)))
     spread = jnp.broadcast_to(
@@ -197,10 +231,14 @@
     ).reshape(TILE_GROUPS * modes, taps)
     gain = residue * jnp.sum(spread * tap_weights, axis=1, keepdims=True)
     square = (TILE_GROUPS * modes, LANES)
-    factor_ref[:modes, :] = own_group(
-        jnp.broadcast_to(jnp.exp(-rate * float(rows - taps)), square), modes
-    )
-    factor_ref[modes:, :] = own_group(jnp.broadcast_to(gain, square), modes)
+    decay = own_group(jnp.broadcast_to(jnp.exp(-rate * float(rows - taps)), square), modes)
+    gain = own_group(jnp.broadcast_to(gain, square), modes)
+    first, state_rows = samples * taps, samples * modes
+    early = border_ref[first : first + state_rows, :].astype(F32)
+    early = early + border_ref[first + state_rows :, :].astype(F32)
+    factors = jnp.concatenate([decay, gain, early], axis=0)
+    base_ref[samples * rows :, :] = jnp.concatenate(halves(factors), axis=0)
+    turn_ref[0] = index_ref[0]
 
 
 def embed_kernel(token_ref, table_ref, out_ref):
@@ -213,39 +251,15 @@
 
 
 def gate_kernel(
-    carried_ref,
-    before_ref,
-    factor_ref,
-    rate_ref,
-    base_source,
-    query_source,
-    gated_ref,
-    sum_ref,
-    base_ref,
-    query_ref,
-    squares,
-    arrived,
+    carried_ref, rate_ref, base_ref, query_ref, gated_ref, sum_ref, squares
 ):
-    samples, rows, width = base_ref.shape
-    modes = factor_ref.shape[0] // 2
+    samples, rows, width = query_ref.shape
+    height = (base_ref.shape[0] - samples * rows) // 2
+    modes = carried_ref.shape[0] // samples
     copies = sum_ref.shape[0]
-    early_at = before_ref.shape[0] - 2 * samples * modes
     own = iota((LANES, LANES), 0) // modes == iota((LANES, LANES), 1) // GROUP
-    tiles = [slice(first, first + LANES) for first in range(0, width, LANES)]
-    loads = []
-    for tile, lanes in enumerate(tiles):
-        pair = (
-            pltpu.make_async_copy(
-                base_source.at[:, :, lanes], base_ref.at[:, :, lanes], arrived.at[0, tile]
-            ),
-            pltpu.make_async_copy(
-                query_source.at[:, :, lanes], query_ref.at[:, :, lanes], arrived.at[1, tile]
-            ),
-        )
-        for load in pair:
-            load.start()
-        loads.append(pair)
-    for tile, lanes in enumerate(tiles):
+    for tile in range(width // LANES):
+        lanes = slice(tile * LANES, (tile + 1) * LANES)
         rate = rate_ref[:, lanes]
         head = jnp.exp(-rate * (1.0 + iota((LANES, 1), 0, F32)))
         step = jnp.exp(-rate * float(LANES))
@@ -254,21 +268,16 @@
             after.append(after[-1] * step)
         upper, lower = halves(jnp.concatenate(after, axis=0))
         after = jnp.concatenate([upper, lower, upper], axis=1)
-        for load in loads[tile]:
-            load.wait()
+        factors = base_ref[samples * rows :, lanes].astype(F32)
+        factors = factors[:height] + factors[height:]
         for s in range(samples):
-            part = slice(s * modes, (s + 1) * modes)
-            carried = carried_ref[part, :, lanes].reshape(modes, LANES)
-            first = early_at + s * modes
-            early = before_ref[first : first + modes, lanes].astype(F32)
-            first = first + samples * modes
-            early = early + before_ref[first : first + modes, lanes].astype(F32)
-            state = factor_ref[:modes, lanes] * carried + early
-            state = state * factor_ref[modes:, lanes]
+            carried = carried_ref[s * modes : (s + 1) * modes, :, lanes].reshape(modes, LANES)
+            early = factors[(s + 2) * modes : (s + 3) * modes]
+            state = (factors[:modes] * carried + early) * factors[modes : 2 * modes]
             spread = jnp.concatenate([state] * TILE_GROUPS, axis=0)
             upper, lower = halves(jnp.where(own, spread, 0.0))
             carry = dot(after, jnp.concatenate([upper, upper, lower], axis=0))
-            base = base_ref[s, :, lanes].astype(F32)
+            base = base_ref[s * rows : (s + 1) * rows, lanes].astype(F32)
             gated = query_ref[s, :, lanes].astype(F32) * (base + carry)
             gated_ref[s, :, lanes] = gated
             if tile == 0:
@@ -346,6 +355,7 @@
 
     state_rows = samples * modes
     border_rows = samples * taps + 2 * state_rows
+    base_rows = samples * rows + 2 * (2 * modes + state_rows)
     shape = jax.ShapeDtypeStruct
     whole = pl.BlockSpec((modes, groups), lambda i: (0, 0))
     rates = decay_rates.T
@@ -358,14 +368,20 @@
 
     states, border = pl.pallas_call(
         states_step,
-        in_specs=[vmem, anywhere, anywhere],
+        in_specs=[anywhere, anywhere, anywhere],
+        out_specs=[anywhere, anywhere],
         out_shape=[
             shape((state_rows, 1, width), F32),
             shape((border_rows, width), BF16),
         ],
         scratch_shapes=[
+            pltpu.VMEM((modes, groups), F32),
             pltpu.VMEM((samples, rows, width), BF16),
             pltpu.VMEM((samples, rows, width), BF16),
+            pltpu.VMEM((state_rows, 1, width), F32),
+            pltpu.VMEM((border_rows, width), BF16),
+            pltpu.SemaphoreType.DMA((1,)),
+            pltpu.SemaphoreType.DMA((2, tiles)),
             pltpu.SemaphoreType.DMA((2, tiles)),
         ],
         compiler_params=params(60),
@@ -384,14 +400,14 @@
         name="embed",
     )(token_ids, embedding)
 
-    base, factors = pl.pallas_call(
+    base, turn = pl.pallas_call(
         local_kernel,
         grid=(tiles,),
-        in_specs=[flat(border_rows), cube(), cube(), grouped(taps), whole, whole, flat(1)],
-        out_specs=[cube(), flat(2 * modes)],
+        in_specs=[smem, flat(border_rows), cube(), cube(), grouped(taps), whole, whole, flat(1)],
+        out_specs=[flat(base_rows), smem],
         out_shape=[
-            shape((samples, rows, width), BF16),
-            shape((2 * modes, width), F32),
+            shape((base_rows, width), BF16),
+            shape((1,), jnp.int32),
         ],
         scratch_shapes=[
             pltpu.VMEM((samples, LANES, rows + 2 * taps), BF16),
@@ -404,6 +420,7 @@
         compiler_params=params(60),
         name="local",
     )(
+        index,
         before,
         key_act,
         value_act,
@@ -422,25 +439,21 @@
         out_shape=shape((state_rows, 1, width), F32),
         compiler_params=params(8),
         name="scan",
-    )(index, decay_rates, gathered)
+    )(turn, decay_rates, gathered)
     carried = lax.all_to_all(entering, "ctx", split_axis=0, concat_axis=0, tiled=True)
 
     gated, sums = pl.pallas_call(
         gate_kernel,
-        in_specs=[vmem, vmem, vmem, vmem, anywhere, anywhere],
         out_shape=[
             shape((samples, rows, width), F32),
             shape((columns, 1, samples * rows), F32),
         ],
         scratch_shapes=[
-            pltpu.VMEM((samples, rows, width), BF16),
-            pltpu.VMEM((samples, rows, width), BF16),
             pltpu.VMEM((samples, rows, LANES), F32),
-            pltpu.SemaphoreType.DMA((2, tiles)),
         ],
         compiler_params=params(16),
         name="gate",
-    )(carried, before, factors, decay_rates.reshape(1, groups * modes), base, query_act)
+    )(carried, decay_rates.reshape(1, groups * modes), base, query_act)
     shares = lax.all_to_all(sums, "tp", split_axis=0, concat_axis=0, tiled=True)
 
     def norm(*refs):

time: 81.4 us -> 87.6 us (1.076)
  starting transfers between devices: 34 us -> 42.6 us
  local copies, waits for them, and re-layouts: 4.97 us -> 3.21 us
    all_to_all x1, waiting for transfers between devices: 0.85 us -> 14.1 us  [per_device(): lax.all_to_all(entering, 'ctx', split_axis=0, concat_axis=0, tiled=True)]
    all_to_all x1, waiting for transfers between devices: 13.9 us -> 0.91 us  [per_device(): lax.all_to_all(states, 'ctx', split_axis=0, concat_axis=0, tiled=True)]
    all_to_all x1, starting transfers between devices: 3.8 us -> 13.1 us  [per_device(): lax.all_to_all(entering, 'ctx', split_axis=0, concat_axis=0, tiled=True)]
    unnamed x21 -> x17, local copies, waits for them, and re-layouts: 4.89 us -> 3.13 us
    pallas_call x3, Pallas kernels: 19.5 us -> 18.2 us  [the longest x1 12.3 us: per_device(): pl.pallas_call(local_kernel, grid=(tiles,), in_specs=[smem, flat(border_r...]
  transfers between devices with their start and end apart: 4 -> 4, of which waited for: 3 -> 3; matrix products, arithmetic and copies ran while one was open for 0% -> 0% of each run, Pallas kernels for 18% -> 15%
where the time goes in v4:
time: 87.6 us; the launch traced here: 87.2 us
  starting transfers between devices  42.6 us (49%)
  Pallas kernels  22.6 us (26%)
  waiting for transfers between devices  18.7 us (21%)
  local copies, waits for them, and re-layouts  3.21 us (4%)
    all_to_all x1, starting transfers between devices, per_device(): lax.all_to_all(states, 'ctx', split_axis=0, concat_axis=0, tiled=True)  15.6 us
    all_to_all x1, waiting for transfers between devices, per_device(): lax.all_to_all(entering, 'ctx', split_axis=0, concat_axis=0, tiled=True)  14.1 us
    all_to_all x1, starting transfers between devices, per_device(): lax.all_to_all(entering, 'ctx', split_axis=0, concat_axis=0, tiled=True)  13.1 us
    pallas_call x1, Pallas kernels, per_device(): pl.pallas_call(local_kernel, grid=(tiles,), in_specs=[smem, flat(border_r...  12.3 us
    all_to_all x1, starting transfers between devices, per_device(): shares = lax.all_to_all(sums, 'tp', split_axis=0, concat_axis=0, tiled=True)  8.36 us
    ppermute x1, starting transfers between devices, per_device(): lax.ppermute(border, 'ctx', [(i, i + 1) for i in range(chunks - 1)])  5.5 us
    pallas_call x1, Pallas kernels, per_device(): pl.pallas_call(states_step, in_specs=[anywhere, anywhere, anywhere], out_...  4.08 us
    all_to_all x1, waiting for transfers between devices, per_device(): shares = lax.all_to_all(sums, 'tp', split_axis=0, concat_axis=0, tiled=True)  3.71 us
  transfers between devices with their start and end apart: 4, of which 3 were waited for; matrix products, arithmetic and copies ran while one was open for 0% of the time, Pallas kernels for 15%

profile of v4, /device:TPU:1, one launch (start us, length us, event | category | flops | bytes accessed | tf_op | source)
XLA Modules:
  0.0 87.2 jit_solution(16627910712599941345)
XLA Ops:
  0.0 0.0 copy-start.6
  0.0 4.1 %states.1 = (f32[32,1,512]{2,1,0:T(1,128)}, bf16[320,512]{1,0:T(8,128)(2,1)}) custom-call(f32[16,32]{1,0:T(8,128)} %bitcast.6, bf16[2,512,512]{2,1,0:T(8,128)(2,1)} %key_ref.1, bf16[2,512,512]{2,1,0:T(8,128)(2,1)} %value_ref.1), custom_call_target="tpu_custom_call" | custom-call | tf_op jit(solution)/shard_map/states/pallas_call | solution.py:369
  4.1 5.5 %collective-permute-start = (bf16[320,512]{1,0:T(8,128)(2,1)}, bf16[320,512]{1,0:T(8,128)(2,1)S(1)}, u32[]{:S(2)}, u32[]{:S(2)}) collective-permute-start(bf16[320,512]{1,0:T(8,128)(2,1)} %get-tuple-element.11), channel_id=1, source_target_pairs={{0,16},{16,32},{32,48},{48,64},{64,80},{80,96},{96,112},{112,128},... | collective-permute-start | bytes 983048 | tf_op jit(solution)/shard_map/ppermute | solution.py:390
  9.6 15.6 %all-to-all-start = ((f32[32,1,512]{2,1,0:T(1,128)}), f32[32,1,512]{2,1,0:T(1,128)S(1)}, u32[]{:S(2)}, u32[]{:S(2)}) async-start(f32[32,1,512]{2,1,0:T(1,128)} %get-tuple-element.13), calls=%async_computation | async-start | bytes 131072 | tf_op jit(solution)/shard_map/all_to_all | solution.py:391
  25.2 0.0 copy-done.6
  25.2 0.1 copy.14.rate_ref
  25.3 0.0 collective-permute-done.border_ref
  25.3 0.0 copy-start.7
  25.3 0.7 copy-done.7
  26.0 0.0 copy-start.1
  26.0 12.3 %local.1 = (bf16[1152,512]{1,0:T(8,128)(2,1)}, s32[1]{0:T(128)}) custom-call(s32[1]{0:T(128)} %bitcast.index_ref.refs_1_, bf16[320,512]{1,0:T(8,128)(2,1)} %copy-done.7, bf16[2,512,512]{2,1,0:T(8,128)(2,1)} %key_ref.1, bf16[2,512,512]{2,1,0:T(8,128)(2,1)} %value_ref.1, bf16[32,128]{1,0:T(8,128)(2,1)} %filter_ref.1, f32[16,32]{1,0:T(8,128)} %bitcast.7, ...), custom_call_target="tpu_custom_call" | custom-call | flops 12000000000 | bytes 8388608 | tf_op jit(solution)/shard_map/local/pallas_call | solution.py:403
  38.4 0.0 copy-start.5
  38.4 0.9 %all-to-all-done.state_ref = f32[32,1,512]{2,1,0:T(1,128)S(1)} async-done(((f32[32,1,512]{2,1,0:T(1,128)}), f32[32,1,512]{2,1,0:T(1,128)S(1)}, u32[]{:S(2)}, u32[]{:S(2)}) %all-to-all-start) | async-done | bytes 65568 | tf_op jit(solution)/shard_map/all_to_all | solution.py:391
  39.3 1.4 %scan.1 = f32[32,1,512]{2,1,0:T(1,128)} custom-call(s32[1]{0:T(128)} %get-tuple-element.12.first_ref, f32[32,16]{1,0:T(8,128)S(1)} %copy.14.rate_ref, f32[32,1,512]{2,1,0:T(1,128)S(1)} %all-to-all-done.state_ref), custom_call_target="tpu_custom_call" | custom-call | tf_op jit(solution)/shard_map/scan/pallas_call | solution.py:436
  40.6 13.1 %all-to-all-start.1 = ((f32[32,1,512]{2,1,0:T(1,128)}), f32[32,1,512]{2,1,0:T(1,128)S(1)}, u32[]{:S(2)}, u32[]{:S(2)}) async-start(f32[32,1,512]{2,1,0:T(1,128)} %scan.1), calls=%async_computation.1 | async-start | bytes 131072 | tf_op jit(solution)/shard_map/all_to_all | solution.py:443
  53.8 0.1 reshape.14.rate_ref
  53.8 14.1 %all-to-all-done.1.carried_ref = f32[32,1,512]{2,1,0:T(1,128)S(1)} async-done(((f32[32,1,512]{2,1,0:T(1,128)}), f32[32,1,512]{2,1,0:T(1,128)S(1)}, u32[]{:S(2)}, u32[]{:S(2)}) %all-to-all-start.1) | async-done | bytes 65568 | tf_op jit(solution)/shard_map/all_to_all | solution.py:443
  67.9 0.0 copy-done.1
  67.9 0.0 copy-start
  67.9 1.3 %copy-done = bf16[1152,512]{1,0:T(8,128)(2,1)S(1)} copy-done((bf16[1152,512]{1,0:T(8,128)(2,1)S(1)}, bf16[1152,512]{1,0:T(8,128)(2,1)}, u32[]{:S(2)}) %copy-start) | copy-done | bytes 1179672
  69.2 0.0 copy-start.2
  69.2 0.0 copy-start.3
  69.2 1.8 %gate.1 = (f32[2,512,512]{2,1,0:T(8,128)S(1)}, f32[16,1,1024]{2,1,0:T(1,128)}) custom-call(f32[32,1,512]{2,1,0:T(1,128)S(1)} %all-to-all-done.1.carried_ref, f32[1,512]{1,0:T(1,128)S(1)} %reshape.14.rate_ref, bf16[1152,512]{1,0:T(8,128)(2,1)S(1)} %copy-done, bf16[2,512,512]{2,1,0:T(8,128)(2,1)S(1)} %copy-done.1), custom_call_target="tpu_custom_call" | custom-call | tf_op jit(solution)/shard_map/gate/pallas_call | solution.py:445
  71.0 8.4 %all-to-all-start.2 = ((f32[16,1,1024]{2,1,0:T(1,128)}), f32[16,1,1024]{2,1,0:T(1,128)S(1)}, u32[]{:S(2)}, u32[]{:S(2)}) async-start(f32[16,1,1024]{2,1,0:T(1,128)} %get-tuple-element.15), calls=%async_computation.2 | async-start | bytes 131072 | tf_op jit(solution)/shard_map/all_to_all | solution.py:457
  79.4 0.0 copy-done.5
  79.4 0.0 copy-start.4
  79.4 1.0 %copy-done.4 = bf16[512,512]{1,0:T(8,128)(2,1)S(1)} copy-done((bf16[512,512]{1,0:T(8,128)(2,1)S(1)}, bf16[512,512]{1,0:T(8,128)(2,1)}, u32[]{:S(2)}) %copy-start.4) | copy-done | bytes 524312
  80.4 1.1 %embed.1.refs_4_ = bf16[2,512,512]{2,1,0:T(8,128)(2,1)S(1)} custom-call(s32[2,512]{1,0:T(2,128)S(1)} %copy-done.5, bf16[512,512]{1,0:T(8,128)(2,1)S(1)} %copy-done.4), custom_call_target="tpu_custom_call" | custom-call | flops 536870912 | bytes 4194304 | tf_op jit(solution)/shard_map/embed/pallas_call | solution.py:393
  81.5 3.7 %all-to-all-done.2.refs_2_ = f32[16,1,1024]{2,1,0:T(1,128)S(1)} async-done(((f32[16,1,1024]{2,1,0:T(1,128)}), f32[16,1,1024]{2,1,0:T(1,128)S(1)}, u32[]{:S(2)}, u32[]{:S(2)}) %all-to-all-start.2) | async-done | bytes 65568 | tf_op jit(solution)/shard_map/all_to_all | solution.py:457
  85.2 0.0 copy-done.2
  85.2 0.0 copy-done.3
  85.2 2.0 %norm.1 = bf16[2,512,512]{2,1,0:T(8,128)(2,1)} custom-call(s32[2]{0:T(128)S(1)} %copy-done.3, s32[1]{0:T(128)} %bitcast.index_ref.refs_1_, f32[16,1,1024]{2,1,0:T(1,128)S(1)} %all-to-all-done.2.refs_2_, f32[2,512,512]{2,1,0:T(8,128)S(1)} %get-tuple-element.16.refs_3_, bf16[2,512,512]{2,1,0:T(8,128)(2,1)S(1)} %embed.1.refs_4_, f32[1,512]{1,0:T(1,128)S(1)} %bitcast.5), custom_call_target="tpu_custom_call" | custom-call | tf_op jit(solution)/shard_map/norm/pallas_call | solution.py:462
Async XLA Ops:
  0.0 25.2 %copy-start.6 = (f32[32,16]{0,1:T(8,128)S(1)}, f32[32,16]{0,1:T(8,128)}, u32[]{:S(2)}) copy-start(f32[32,16]{0,1:T(8,128)} %param.18) | copy-start | bytes 6148
  4.1 21.2 %collective-permute-start = (bf16[320,512]{1,0:T(8,128)(2,1)}, bf16[320,512]{1,0:T(8,128)(2,1)S(1)}, u32[]{:S(2)}, u32[]{:S(2)}) collective-permute-start(bf16[320,512]{1,0:T(8,128)(2,1)} %get-tuple-element.11), channel_id=1, source_target_pairs={{0,16},{16,32},{32,48},{48,64},{64,80},{80,96},{96,112},{112,128},... | collective-permute-start | bytes 983048 | tf_op jit(solution)/shard_map/ppermute | solution.py:390
  9.6 29.7 %all-to-all-start = ((f32[32,1,512]{2,1,0:T(1,128)}), f32[32,1,512]{2,1,0:T(1,128)S(1)}, u32[]{:S(2)}, u32[]{:S(2)}) async-start(f32[32,1,512]{2,1,0:T(1,128)} %get-tuple-element.13), calls=%async_computation | async-start | bytes 131072 | tf_op jit(solution)/shard_map/all_to_all | solution.py:391
  25.3 0.7 copy-start.7
  26.0 41.9 %copy-start.1 = (bf16[2,512,512]{2,1,0:T(8,128)(2,1)S(1)}, bf16[2,512,512]{2,1,0:T(8,128)(2,1)}, u32[]{:S(2)}) copy-start(bf16[2,512,512]{2,1,0:T(8,128)(2,1)} %query_ref.1) | copy-start | bytes 3145732
  38.4 41.0 %copy-start.5 = (s32[2,512]{1,0:T(2,128)S(1)}, s32[2,512]{1,0:T(2,128)}, u32[]{:S(2)}) copy-start(s32[2,512]{1,0:T(2,128)} %token_ref.1) | copy-start | bytes 12292
  40.6 27.3 %all-to-all-start.1 = ((f32[32,1,512]{2,1,0:T(1,128)}), f32[32,1,512]{2,1,0:T(1,128)S(1)}, u32[]{:S(2)}, u32[]{:S(2)}) async-start(f32[32,1,512]{2,1,0:T(1,128)} %scan.1), calls=%async_computation.1 | async-start | bytes 131072 | tf_op jit(solution)/shard_map/all_to_all | solution.py:443
  67.9 1.3 %copy-start = (bf16[1152,512]{1,0:T(8,128)(2,1)S(1)}, bf16[1152,512]{1,0:T(8,128)(2,1)}, u32[]{:S(2)}) copy-start(bf16[1152,512]{1,0:T(8,128)(2,1)} %get-tuple-element.14.base_ref) | copy-start | bytes 3538948
  69.2 16.0 %copy-start.2 = (f32[512]{0:T(512)S(1)}, f32[512]{0:T(512)}, u32[]{:S(2)}) copy-start(f32[512]{0:T(512)} %param.21) | copy-start | bytes 6148
  69.2 16.0 %copy-start.3 = (s32[2]{0:T(128)S(1)}, s32[2]{0:T(128)}, u32[]{:S(2)}) copy-start(s32[2]{0:T(128)} %refs_0_.1) | copy-start | bytes 28
  71.0 14.2 %all-to-all-start.2 = ((f32[16,1,1024]{2,1,0:T(1,128)}), f32[16,1,1024]{2,1,0:T(1,128)S(1)}, u32[]{:S(2)}, u32[]{:S(2)}) async-start(f32[16,1,1024]{2,1,0:T(1,128)} %get-tuple-element.15), calls=%async_computation.2 | async-start | bytes 131072 | tf_op jit(solution)/shard_map/all_to_all | solution.py:457
  79.4 1.0 %copy-start.4 = (bf16[512,512]{1,0:T(8,128)(2,1)S(1)}, bf16[512,512]{1,0:T(8,128)(2,1)}, u32[]{:S(2)}) copy-start(bf16[512,512]{1,0:T(8,128)(2,1)} %table_ref.1) | copy-start | bytes 1572868

commit v5 on v4

--- a/solution.py
+++ b/solution.py
@@ -100,7 +100,10 @@
             product = product_of(key_ref[s, :, lanes], value_ref[s, :, lanes])
             full = dot(weights, product)
             state = own_group(full[:half] + full[half:], modes)
-            state_ref[s * modes : (s + 1) * modes, :, lanes] = state.reshape(modes, 1, LANES)
+            state = state.astype(BF16)
+            for copy in range(state_ref.shape[0] // (samples * modes)):
+                at = (copy * samples + s) * modes
+                state_ref[at : at + modes, lanes] = state
             border_ref[s * taps : (s + 1) * taps, lanes] = product[rows - taps :]
             early = dot(weights[:, taps:], product[: rows - taps])
             upper, lower = halves(own_group(early[:half] + early[half:], modes))
@@ -109,7 +112,7 @@
             border_ref[first + samples * modes : first + (samples + 1) * modes, lanes] = lower
         pair = (
             pltpu.make_async_copy(
-                state_ref.at[:, :, lanes], state_target.at[:, :, lanes], left.at[0, tile]
+                state_ref.at[:, lanes], state_target.at[:, lanes], left.at[0, tile]
             ),
             pltpu.make_async_copy(
                 border_ref.at[:, lanes], border_target.at[:, lanes], left.at[1, tile]
@@ -122,24 +125,26 @@
         store.wait()
 
 
-def scan_kernel(first_ref, rate_ref, state_ref, out_ref, *, chunks, rows):
-    total, _, width = state_ref.shape
-    each = total // chunks
-    groups, modes = rate_ref.shape
-    rates = rate_ref[...]
-    for r in range(each):
-        mode = lax.rem(first_ref[0] * each + r, modes)
-        picked = jnp.sum(
-            jnp.where(iota(rates.shape, 1) == mode, rates, 0.0), axis=1, keepdims=True
-        )
-        at_group = iota((groups, width), 0) == iota((groups, width), 1) // GROUP
-        rate = jnp.sum(jnp.where(at_group, picked, 0.0), axis=0, keepdims=True)
-        decay = jnp.exp(-rate * float(rows))
-        held = jnp.zeros((1, width), F32)
-        out_ref[r] = held
-        for n in range(1, chunks):
-            out_ref[n * each + r] = held
-            held = decay * held + state_ref[(n - 1) * each + r]
+def group_kernel(index_ref, rate_ref, state_ref, far_ref, own_ref, *, near, rows):
+    height = own_ref.shape[0]
+    far = far_ref.shape[0] // height
+    modes = rate_ref.shape[0]
+    group, place = index_ref[0] // near, lax.rem(index_ref[0], near)
+    rate = jnp.concatenate([rate_ref[...]] * (height // modes), axis=0) * float(rows)
+    decay = jnp.exp(-rate)
+    held = jnp.zeros(own_ref.shape, F32)
+    own, short = held, held
+    for p in range(near):
+        own = jnp.where(place == p + 1, held, own)
+        short = held
+        held = decay * held + state_ref[p * height : (p + 1) * height, :].astype(F32)
+    own_ref[...] = own
+    for other in range(far):
+        ahead = (other - group) * near + place - near - 1
+        weight = jnp.exp(-rate * jnp.maximum(ahead, 0).astype(F32))
+        value = jnp.where(ahead < 0, short, weight * held)
+        value = jnp.where(other > group, value, 0.0)
+        far_ref[other * height : (other + 1) * height, :] = value.astype(BF16)
 
 
 def dot_rows(a, b):
@@ -147,7 +152,6 @@
 
 
 def local_kernel(
-    index_ref,
     border_ref,
     key_ref,
     value_ref,
@@ -156,7 +160,6 @@
     residue_ref,
     skip_ref,
     base_ref,
-    turn_ref,
     product_window,
     mixed_window,
     turned,
@@ -238,7 +241,6 @@
     early = early + border_ref[first + state_rows :, :].astype(F32)
     factors = jnp.concatenate([decay, gain, early], axis=0)
     base_ref[samples * rows :, :] = jnp.concatenate(halves(factors), axis=0)
-    turn_ref[0] = index_ref[0]
 
 
 def embed_kernel(token_ref, table_ref, out_ref):
@@ -251,11 +253,11 @@
 
 
 def gate_kernel(
-    carried_ref, rate_ref, base_ref, query_ref, gated_ref, sum_ref, squares
+    far_ref, own_ref, rate_ref, base_ref, query_ref, gated_ref, sum_ref, squares
 ):
     samples, rows, width = query_ref.shape
     height = (base_ref.shape[0] - samples * rows) // 2
-    modes = carried_ref.shape[0] // samples
+    modes = own_ref.shape[0] // samples
     copies = sum_ref.shape[0]
     own = iota((LANES, LANES), 0) // modes == iota((LANES, LANES), 1) // GROUP
     for tile in range(width // LANES):
@@ -271,7 +273,9 @@
         factors = base_ref[samples * rows :, lanes].astype(F32)
         factors = factors[:height] + factors[height:]
         for s in range(samples):
-            carried = carried_ref[s * modes : (s + 1) * modes, :, lanes].reshape(modes, LANES)
+            carried = own_ref[s * modes : (s + 1) * modes, lanes]
+            for first in range(s * modes, far_ref.shape[0], samples * modes):
+                carried = carried + far_ref[first : first + modes, lanes].astype(F32)
             early = factors[(s + 2) * modes : (s + 3) * modes]
             state = (factors[:modes] * carried + early) * factors[modes : 2 * modes]
             spread = jnp.concatenate([state] * TILE_GROUPS, axis=0)
@@ -359,6 +363,16 @@
     shape = jax.ShapeDtypeStruct
     whole = pl.BlockSpec((modes, groups), lambda i: (0, 0))
     rates = decay_rates.T
+    near = 8 if chunks % 16 == 0 else 2
+    far = chunks // near
+    near_groups = [[g * near + i for i in range(near)] for g in range(far)]
+    far_groups = [[g * near + i for g in range(far)] for i in range(near)]
+
+    def exchange(blocks, groups):
+        return lax.all_to_all(
+            blocks, "ctx", split_axis=0, concat_axis=0, axis_index_groups=groups, tiled=True
+        )
+
 
     vmem = pl.BlockSpec(memory_space=pltpu.VMEM)
     anywhere = pl.BlockSpec(memory_space=pl.ANY)
@@ -371,14 +385,14 @@
         in_specs=[anywhere, anywhere, anywhere],
         out_specs=[anywhere, anywhere],
         out_shape=[
-            shape((state_rows, 1, width), F32),
+            shape((near * state_rows, width), BF16),
             shape((border_rows, width), BF16),
         ],
         scratch_shapes=[
             pltpu.VMEM((modes, groups), F32),
             pltpu.VMEM((samples, rows, width), BF16),
             pltpu.VMEM((samples, rows, width), BF16),
-            pltpu.VMEM((state_rows, 1, width), F32),
+            pltpu.VMEM((near * state_rows, width), BF16),
             pltpu.VMEM((border_rows, width), BF16),
             pltpu.SemaphoreType.DMA((1,)),
             pltpu.SemaphoreType.DMA((2, tiles)),
@@ -388,7 +402,7 @@
         name="states",
     )(rates, key_act, value_act)
     before = lax.ppermute(border, "ctx", [(i, i + 1) for i in range(chunks - 1)])
-    gathered = lax.all_to_all(states, "ctx", split_axis=0, concat_axis=0, tiled=True)
+    gathered = exchange(states, near_groups)
 
     embedded = pl.pallas_call(
         embed_kernel,
@@ -400,15 +414,12 @@
         name="embed",
     )(token_ids, embedding)
 
-    base, turn = pl.pallas_call(
+    base = pl.pallas_call(
         local_kernel,
         grid=(tiles,),
-        in_specs=[smem, flat(border_rows), cube(), cube(), grouped(taps), whole, whole, flat(1)],
-        out_specs=[flat(base_rows), smem],
-        out_shape=[
-            shape((base_rows, width), BF16),
-            shape((1,), jnp.int32),
-        ],
+        in_specs=[flat(border_rows), cube(), cube(), grouped(taps), whole, whole, flat(1)],
+        out_specs=flat(base_rows),
+        out_shape=shape((base_rows, width), BF16),
         scratch_shapes=[
             pltpu.VMEM((samples, LANES, rows + 2 * taps), BF16),
             pltpu.VMEM((samples, LANES, 2 * rows), BF16),
@@ -420,7 +431,6 @@
         compiler_params=params(60),
         name="local",
     )(
-        index,
         before,
         key_act,
         value_act,
@@ -430,17 +440,17 @@
         skip_gain.reshape(1, width),
     )
 
-    def scan(first_ref, rate_ref, state_ref, out_ref):
-        scan_kernel(first_ref, rate_ref, state_ref, out_ref, chunks=chunks, rows=rows)
-
-    entering = pl.pallas_call(
-        scan,
+    def group_step(*refs):
+        group_kernel(*refs, near=near, rows=rows)
+
+    sent, own = pl.pallas_call(
+        group_step,
         in_specs=[smem, vmem, vmem],
-        out_shape=shape((state_rows, 1, width), F32),
+        out_shape=[shape((far * state_rows, width), BF16), shape((state_rows, width), F32)],
         compiler_params=params(8),
-        name="scan",
-    )(turn, decay_rates, gathered)
-    carried = lax.all_to_all(entering, "ctx", split_axis=0, concat_axis=0, tiled=True)
+        name="group",
+    )(index, jnp.repeat(rates, GROUP, axis=1), gathered)
+    carried = exchange(sent, far_groups)
 
     gated, sums = pl.pallas_call(
         gate_kernel,
@@ -453,7 +463,7 @@
         ],
         compiler_params=params(16),
         name="gate",
-    )(carried, decay_rates.reshape(1, groups * modes), base, query_act)
+    )(carried, own, decay_rates.reshape(1, groups * modes), base, query_act)
     shares = lax.all_to_all(sums, "tp", split_axis=0, concat_axis=0, tiled=True)
 
     def norm(*refs):

time: 87.6 us -> 67.7 us (0.77)
  waiting for transfers between devices: 18.7 us -> 7.05 us
  starting transfers between devices: 42.6 us -> 34.6 us
    all_to_all x2, waiting for transfers between devices: 15 us -> 3.34 us  [exchange(): lax.all_to_all(blocks, 'ctx', split_axis=0, concat_axis=0, axis_index_gro...]
    all_to_all x2, starting transfers between devices: 28.7 us -> 21.6 us  [exchange(): lax.all_to_all(blocks, 'ctx', split_axis=0, concat_axis=0, axis_index_gro...]
  transfers between devices with their start and end apart: 4 -> 4, of which waited for: 3 -> 2; matrix products, arithmetic and copies ran while one was open for 0% -> 1% of each run, Pallas kernels for 15% -> 21%
where the time goes in v5:
time: 67.7 us; the launch traced here: 67.2 us
  starting transfers between devices  34.6 us (51%)
  Pallas kernels  22 us (32%)
  waiting for transfers between devices  7.05 us (10%)
  local copies, waits for them, and re-layouts  3.48 us (5%)
    all_to_all x2, starting transfers between devices, exchange(): lax.all_to_all(blocks, 'ctx', split_axis=0, concat_axis=0, axis_index_gro...  21.6 us
    pallas_call x1, Pallas kernels, per_device(): pl.pallas_call(local_kernel, grid=(tiles,), in_specs=[flat(border_rows),...  12.3 us
    all_to_all x1, starting transfers between devices, per_device(): shares = lax.all_to_all(sums, 'tp', split_axis=0, concat_axis=0, tiled=True)  8.15 us
    ppermute x1, starting transfers between devices, per_device(): lax.ppermute(border, 'ctx', [(i, i + 1) for i in range(chunks - 1)])  4.88 us
    pallas_call x1, Pallas kernels, per_device(): pl.pallas_call(states_step, in_specs=[anywhere, anywhere, anywhere], out_...  4.08 us
    all_to_all x1, waiting for transfers between devices, per_device(): shares = lax.all_to_all(sums, 'tp', split_axis=0, concat_axis=0, tiled=True)  3.71 us
    all_to_all x2, waiting for transfers between devices, exchange(): lax.all_to_all(blocks, 'ctx', split_axis=0, concat_axis=0, axis_index_gro...  3.34 us
    unnamed x17, local copies, waits for them, and re-layouts  3.12 us
  transfers between devices with their start and end apart: 4, of which 2 were waited for; matrix products, arithmetic and copies ran while one was open for 1% of the time, Pallas kernels for 21%

profile of v5, /device:TPU:1, one launch (start us, length us, event | category | flops | bytes accessed | tf_op | source)
XLA Modules:
  0.0 67.2 jit_solution(18297574631316953792)
XLA Ops:
  0.0 0.0 copy-start.6
  0.0 4.1 %states.1 = (bf16[256,512]{1,0:T(8,128)(2,1)}, bf16[320,512]{1,0:T(8,128)(2,1)}) custom-call(f32[16,32]{1,0:T(8,128)} %bitcast.13, bf16[2,512,512]{2,1,0:T(8,128)(2,1)} %key_ref.1, bf16[2,512,512]{2,1,0:T(8,128)(2,1)} %value_ref.1), custom_call_target="tpu_custom_call" | custom-call | tf_op jit(solution)/shard_map/states/pallas_call | solution.py:383
  4.1 8.9 %all-to-all-start = ((bf16[8,32,512]{2,1,0:T(8,128)(2,1)}), bf16[8,32,512]{2,1,0:T(8,128)(2,1)S(1)}, u32[]{:S(2)}, u32[]{:S(2)}) async-start(bf16[8,32,512]{2,1,0:T(8,128)(2,1)} %bitcast.12), calls=%async_computation | async-start | bytes 524288 | tf_op jit(solution)/shard_map/all_to_all | solution.py:372
  13.0 4.9 %collective-permute-start = (bf16[320,512]{1,0:T(8,128)(2,1)}, bf16[320,512]{1,0:T(8,128)(2,1)S(1)}, u32[]{:S(2)}, u32[]{:S(2)}) collective-permute-start(bf16[320,512]{1,0:T(8,128)(2,1)} %get-tuple-element.14), channel_id=1, source_target_pairs={{0,16},{16,32},{32,48},{48,64},{64,80},{80,96},{96,112},{112,128},... | collective-permute-start | bytes 983048 | tf_op jit(solution)/shard_map/ppermute | solution.py:404
  17.9 0.0 copy-done.6
  17.9 0.1 copy.13
  18.0 0.1 reshape.21.rate_ref
  18.1 0.1 broadcast_in_dim.3
  18.2 0.2 reshape.20.refs_1_
  18.4 3.3 %all-to-all-done = bf16[8,32,512]{2,1,0:T(8,128)(2,1)S(1)} async-done(((bf16[8,32,512]{2,1,0:T(8,128)(2,1)}), bf16[8,32,512]{2,1,0:T(8,128)(2,1)S(1)}, u32[]{:S(2)}, u32[]{:S(2)}) %all-to-all-start) | async-done | bytes 262176 | tf_op jit(solution)/shard_map/all_to_all | solution.py:372
  21.7 0.8 %group.1 = (bf16[128,512]{1,0:T(8,128)(2,1)}, f32[32,512]{1,0:T(8,128)S(1)}) custom-call(s32[1]{0:T(128)} %bitcast.refs_0_.refs_1_, f32[16,512]{1,0:T(8,128)S(1)} %reshape.20.refs_1_, bf16[256,512]{1,0:T(8,128)(2,1)S(1)} %bitcast.9), custom_call_target="tpu_custom_call" | custom-call | tf_op jit(solution)/shard_map/group/pallas_call | solution.py:446
  22.5 12.7 %all-to-all-start.1 = ((bf16[4,32,512]{2,1,0:T(8,128)(2,1)}), bf16[4,32,512]{2,1,0:T(8,128)(2,1)S(1)}, u32[]{:S(2)}, u32[]{:S(2)}) async-start(bf16[4,32,512]{2,1,0:T(8,128)(2,1)} %bitcast.4), calls=%async_computation.1 | async-start | bytes 262144 | tf_op jit(solution)/shard_map/all_to_all | solution.py:372
  35.2 0.0 collective-permute-done.border_ref
  35.2 0.0 copy-start.7
  35.2 0.7 %copy-done.7 = bf16[320,512]{1,0:T(8,128)(2,1)} copy-done((bf16[320,512]{1,0:T(8,128)(2,1)}, bf16[320,512]{1,0:T(8,128)(2,1)S(1)}, u32[]{:S(2)}) %copy-start.7) | copy-done | bytes 327704
  35.9 0.0 copy-start.1
  35.9 0.0 copy-start.5
  35.9 12.3 %local.1.base_ref = bf16[1152,512]{1,0:T(8,128)(2,1)} custom-call(bf16[320,512]{1,0:T(8,128)(2,1)} %copy-done.7, bf16[2,512,512]{2,1,0:T(8,128)(2,1)} %key_ref.1, bf16[2,512,512]{2,1,0:T(8,128)(2,1)} %value_ref.1, bf16[32,128]{1,0:T(8,128)(2,1)} %filter_ref.1, f32[16,32]{1,0:T(8,128)} %bitcast.14, f32[16,32]{1,0:T(8,128)} %bitcast.16, f32[1,512]{1,0:T(1,128)} %bitcast.17), custom_call_target="tpu_custom_call" | custom-call | flops 12000000000 | bytes 8388608 | tf_op jit(solution)/shard_map/local/pallas_call | solution.py:417
  48.2 0.0 all-to-all-done.1
  48.2 0.0 copy-done.1
  48.2 0.0 copy-start
  48.2 1.3 %copy-done = bf16[1152,512]{1,0:T(8,128)(2,1)S(1)} copy-done((bf16[1152,512]{1,0:T(8,128)(2,1)S(1)}, bf16[1152,512]{1,0:T(8,128)(2,1)}, u32[]{:S(2)}) %copy-start) | copy-done | bytes 1179672
  49.5 0.0 copy-start.2
  49.5 0.0 copy-start.3
  49.5 1.8 %gate.1 = (f32[2,512,512]{2,1,0:T(8,128)S(1)}, f32[16,1,1024]{2,1,0:T(1,128)}) custom-call(bf16[128,512]{1,0:T(8,128)(2,1)S(1)} %bitcast.10, f32[32,512]{1,0:T(8,128)S(1)} %get-tuple-element.13.own_ref, f32[1,512]{1,0:T(1,128)S(1)} %reshape.21.rate_ref, bf16[1152,512]{1,0:T(8,128)(2,1)S(1)} %copy-done, bf16[2,512,512]{2,1,0:T(8,128)(2,1)S(1)} %copy-done.1), custom_call_target="tpu_custom_call" | custom-call | tf_op jit(solution)/shard_map/gate/pallas_call | solution.py:455
  51.3 8.2 %all-to-all-start.2 = ((f32[16,1,1024]{2,1,0:T(1,128)}), f32[16,1,1024]{2,1,0:T(1,128)S(1)}, u32[]{:S(2)}, u32[]{:S(2)}) async-start(f32[16,1,1024]{2,1,0:T(1,128)} %get-tuple-element.15), calls=%async_computation.2 | async-start | bytes 131072 | tf_op jit(solution)/shard_map/all_to_all | solution.py:467
  59.4 0.0 copy-done.5
  59.5 0.0 copy-start.4
  59.5 1.0 %copy-done.4 = bf16[512,512]{1,0:T(8,128)(2,1)S(1)} copy-done((bf16[512,512]{1,0:T(8,128)(2,1)S(1)}, bf16[512,512]{1,0:T(8,128)(2,1)}, u32[]{:S(2)}) %copy-start.4) | copy-done | bytes 524312
  60.5 1.1 %embed.1.refs_4_ = bf16[2,512,512]{2,1,0:T(8,128)(2,1)S(1)} custom-call(s32[2,512]{1,0:T(2,128)S(1)} %copy-done.5, bf16[512,512]{1,0:T(8,128)(2,1)S(1)} %copy-done.4), custom_call_target="tpu_custom_call" | custom-call | flops 536870912 | bytes 4194304 | tf_op jit(solution)/shard_map/embed/pallas_call | solution.py:407
  61.6 3.7 %all-to-all-done.2.refs_2_ = f32[16,1,1024]{2,1,0:T(1,128)S(1)} async-done(((f32[16,1,1024]{2,1,0:T(1,128)}), f32[16,1,1024]{2,1,0:T(1,128)S(1)}, u32[]{:S(2)}, u32[]{:S(2)}) %all-to-all-start.2) | async-done | bytes 65568 | tf_op jit(solution)/shard_map/all_to_all | solution.py:467
  65.3 0.0 copy-done.2
  65.3 0.0 copy-done.3
  65.3 2.0 %norm.1 = bf16[2,512,512]{2,1,0:T(8,128)(2,1)} custom-call(s32[2]{0:T(128)S(1)} %copy-done.3, s32[1]{0:T(128)} %bitcast.refs_0_.refs_1_, f32[16,1,1024]{2,1,0:T(1,128)S(1)} %all-to-all-done.2.refs_2_, f32[2,512,512]{2,1,0:T(8,128)S(1)} %get-tuple-element.16.refs_3_, bf16[2,512,512]{2,1,0:T(8,128)(2,1)S(1)} %embed.1.refs_4_, f32[1,512]{1,0:T(1,128)S(1)} %bitcast.11), custom_call_target="tpu_custom_call" | custom-call | tf_op jit(solution)/shard_map/norm/pallas_call | solution.py:472
Async XLA Ops:
  0.0 17.9 %copy-start.6 = (f32[32,16]{0,1:T(8,128)S(1)}, f32[32,16]{0,1:T(8,128)}, u32[]{:S(2)}) copy-start(f32[32,16]{0,1:T(8,128)} %param.18) | copy-start | bytes 6148
  4.1 17.6 %all-to-all-start = ((bf16[8,32,512]{2,1,0:T(8,128)(2,1)}), bf16[8,32,512]{2,1,0:T(8,128)(2,1)S(1)}, u32[]{:S(2)}, u32[]{:S(2)}) async-start(bf16[8,32,512]{2,1,0:T(8,128)(2,1)} %bitcast.12), calls=%async_computation | async-start | bytes 524288 | tf_op jit(solution)/shard_map/all_to_all | solution.py:372
  13.0 22.1 %collective-permute-start = (bf16[320,512]{1,0:T(8,128)(2,1)}, bf16[320,512]{1,0:T(8,128)(2,1)S(1)}, u32[]{:S(2)}, u32[]{:S(2)}) collective-permute-start(bf16[320,512]{1,0:T(8,128)(2,1)} %get-tuple-element.14), channel_id=1, source_target_pairs={{0,16},{16,32},{32,48},{48,64},{64,80},{80,96},{96,112},{112,128},... | collective-permute-start | bytes 983048 | tf_op jit(solution)/shard_map/ppermute | solution.py:404
  22.5 25.7 %all-to-all-start.1 = ((bf16[4,32,512]{2,1,0:T(8,128)(2,1)}), bf16[4,32,512]{2,1,0:T(8,128)(2,1)S(1)}, u32[]{:S(2)}, u32[]{:S(2)}) async-start(bf16[4,32,512]{2,1,0:T(8,128)(2,1)} %bitcast.4), calls=%async_computation.1 | async-start | bytes 262144 | tf_op jit(solution)/shard_map/all_to_all | solution.py:372
  35.2 0.7 %copy-start.7 = (bf16[320,512]{1,0:T(8,128)(2,1)}, bf16[320,512]{1,0:T(8,128)(2,1)S(1)}, u32[]{:S(2)}) copy-start(bf16[320,512]{1,0:T(8,128)(2,1)S(1)} %collective-permute-done.border_ref) | copy-start | bytes 983044
  35.9 12.3 %copy-start.1 = (bf16[2,512,512]{2,1,0:T(8,128)(2,1)S(1)}, bf16[2,512,512]{2,1,0:T(8,128)(2,1)}, u32[]{:S(2)}) copy-start(bf16[2,512,512]{2,1,0:T(8,128)(2,1)} %query_ref.1) | copy-start | bytes 3145732
  35.9 23.6 %copy-start.5 = (s32[2,512]{1,0:T(2,128)S(1)}, s32[2,512]{1,0:T(2,128)}, u32[]{:S(2)}) copy-start(s32[2,512]{1,0:T(2,128)} %token_ref.1) | copy-start | bytes 12292
  48.2 1.3 %copy-start = (bf16[1152,512]{1,0:T(8,128)(2,1)S(1)}, bf16[1152,512]{1,0:T(8,128)(2,1)}, u32[]{:S(2)}) copy-start(bf16[1152,512]{1,0:T(8,128)(2,1)} %local.1.base_ref) | copy-start | bytes 3538948
  49.5 15.8 %copy-start.2 = (f32[512]{0:T(512)S(1)}, f32[512]{0:T(512)}, u32[]{:S(2)}) copy-start(f32[512]{0:T(512)} %param.21) | copy-start | bytes 6148
  49.5 15.8 %copy-start.3 = (s32[2]{0:T(128)S(1)}, s32[2]{0:T(128)}, u32[]{:S(2)}) copy-start(s32[2]{0:T(128)} %refs_0_.1) | copy-start | bytes 28
  51.3 14.0 %all-to-all-start.2 = ((f32[16,1,1024]{2,1,0:T(1,128)}), f32[16,1,1024]{2,1,0:T(1,128)S(1)}, u32[]{:S(2)}, u32[]{:S(2)}) async-start(f32[16,1,1024]{2,1,0:T(1,128)} %get-tuple-element.15), calls=%async_computation.2 | async-start | bytes 131072 | tf_op jit(solution)/shard_map/all_to_all | solution.py:467
  59.5 1.0 %copy-start.4 = (bf16[512,512]{1,0:T(8,128)(2,1)S(1)}, bf16[512,512]{1,0:T(8,128)(2,1)}, u32[]{:S(2)}) copy-start(bf16[512,512]{1,0:T(8,128)(2,1)} %table_ref.1) | copy-start | bytes 1572868

commit v6 on v5

--- a/solution.py
+++ b/solution.py
@@ -363,7 +363,7 @@
     shape = jax.ShapeDtypeStruct
     whole = pl.BlockSpec((modes, groups), lambda i: (0, 0))
     rates = decay_rates.T
-    near = 8 if chunks % 16 == 0 else 2
+    near = 4 if chunks % 16 == 0 else 2
     far = chunks // near
     near_groups = [[g * near + i for i in range(near)] for g in range(far)]
     far_groups = [[g * near + i for g in range(far)] for i in range(near)]

time: 67.7 us -> 69.1 us (1.021)
  starting transfers between devices: 34.6 us -> 35.4 us
    all_to_all x1, starting transfers between devices: 8.15 us -> 10.4 us  [per_device(): shares = lax.all_to_all(sums, 'tp', split_axis=0, concat_axis=0, tiled=True)]
    all_to_all x2, starting transfers between devices: 21.6 us -> 20.1 us  [exchange(): lax.all_to_all(blocks, 'ctx', split_axis=0, concat_axis=0, axis_index_gro...]
where the time goes in v6:
time: 69.1 us; the launch traced here: 68.6 us
  starting transfers between devices  35.4 us (51%)
  Pallas kernels  22 us (32%)
  waiting for transfers between devices  7.67 us (11%)
  local copies, waits for them, and re-layouts  3.48 us (5%)
    all_to_all x2, starting transfers between devices, exchange(): lax.all_to_all(blocks, 'ctx', split_axis=0, concat_axis=0, axis_index_gro...  20.1 us
    pallas_call x1, Pallas kernels, per_device(): pl.pallas_call(local_kernel, grid=(tiles,), in_specs=[flat(border_rows),...  12.3 us
    all_to_all x1, starting transfers between devices, per_device(): shares = lax.all_to_all(sums, 'tp', split_axis=0, concat_axis=0, tiled=True)  10.4 us
    ppermute x1, starting transfers between devices, per_device(): lax.ppermute(border, 'ctx', [(i, i + 1) for i in range(chunks - 1)])  4.88 us
    pallas_call x1, Pallas kernels, per_device(): pl.pallas_call(states_step, in_specs=[anywhere, anywhere, anywhere], out_...  4.08 us
    all_to_all x2, waiting for transfers between devices, exchange(): lax.all_to_all(blocks, 'ctx', split_axis=0, concat_axis=0, axis_index_gro...  3.96 us
    all_to_all x1, waiting for transfers between devices, per_device(): shares = lax.all_to_all(sums, 'tp', split_axis=0, concat_axis=0, tiled=True)  3.7 us
    unnamed x17, local copies, waits for them, and re-layouts  3.12 us
  transfers between devices with their start and end apart: 4, of which 2 were waited for; matrix products, arithmetic and copies ran while one was open for 1% of the time, Pallas kernels for 21%

profile of v6, /device:TPU:1, one launch (start us, length us, event | category | flops | bytes accessed | tf_op | source)
XLA Modules:
  0.0 68.6 jit_solution(6271507817698753538)
XLA Ops:
  0.0 0.0 copy-start.6
  0.0 4.1 %states.1 = (bf16[128,512]{1,0:T(8,128)(2,1)}, bf16[320,512]{1,0:T(8,128)(2,1)}) custom-call(f32[16,32]{1,0:T(8,128)} %bitcast.13, bf16[2,512,512]{2,1,0:T(8,128)(2,1)} %key_ref.1, bf16[2,512,512]{2,1,0:T(8,128)(2,1)} %value_ref.1), custom_call_target="tpu_custom_call" | custom-call | tf_op jit(solution)/shard_map/states/pallas_call | solution.py:383
  4.1 6.2 %all-to-all-start = ((bf16[4,32,512]{2,1,0:T(8,128)(2,1)}), bf16[4,32,512]{2,1,0:T(8,128)(2,1)S(1)}, u32[]{:S(2)}, u32[]{:S(2)}) async-start(bf16[4,32,512]{2,1,0:T(8,128)(2,1)} %bitcast.12), calls=%async_computation | async-start | bytes 262144 | tf_op jit(solution)/shard_map/all_to_all | solution.py:372
  10.3 4.9 %collective-permute-start = (bf16[320,512]{1,0:T(8,128)(2,1)}, bf16[320,512]{1,0:T(8,128)(2,1)S(1)}, u32[]{:S(2)}, u32[]{:S(2)}) collective-permute-start(bf16[320,512]{1,0:T(8,128)(2,1)} %get-tuple-element.14), channel_id=1, source_target_pairs={{0,16},{16,32},{32,48},{48,64},{64,80},{80,96},{96,112},{112,128},... | collective-permute-start | bytes 983048 | tf_op jit(solution)/shard_map/ppermute | solution.py:404
  15.2 0.0 copy-done.6
  15.2 0.1 copy.13
  15.3 0.1 reshape.21.rate_ref
  15.4 0.1 broadcast_in_dim.3
  15.5 0.2 reshape.20.refs_1_
  15.7 0.0 all-to-all-done
  15.7 0.8 %group.1 = (bf16[256,512]{1,0:T(8,128)(2,1)}, f32[32,512]{1,0:T(8,128)S(1)}) custom-call(s32[1]{0:T(128)} %bitcast.refs_0_.refs_1_, f32[16,512]{1,0:T(8,128)S(1)} %reshape.20.refs_1_, bf16[128,512]{1,0:T(8,128)(2,1)S(1)} %bitcast.10), custom_call_target="tpu_custom_call" | custom-call | tf_op jit(solution)/shard_map/group/pallas_call | solution.py:446
  16.5 13.9 %all-to-all-start.1 = ((bf16[8,32,512]{2,1,0:T(8,128)(2,1)}), bf16[8,32,512]{2,1,0:T(8,128)(2,1)S(1)}, u32[]{:S(2)}, u32[]{:S(2)}) async-start(bf16[8,32,512]{2,1,0:T(8,128)(2,1)} %bitcast.4), calls=%async_computation.1 | async-start | bytes 524288 | tf_op jit(solution)/shard_map/all_to_all | solution.py:372
  30.4 0.0 collective-permute-done.border_ref
  30.4 0.0 copy-start.7
  30.4 0.7 %copy-done.7 = bf16[320,512]{1,0:T(8,128)(2,1)} copy-done((bf16[320,512]{1,0:T(8,128)(2,1)}, bf16[320,512]{1,0:T(8,128)(2,1)S(1)}, u32[]{:S(2)}) %copy-start.7) | copy-done | bytes 327704
  31.2 0.0 copy-start.1
  31.2 0.0 copy-start.5
  31.2 12.3 %local.1.base_ref = bf16[1152,512]{1,0:T(8,128)(2,1)} custom-call(bf16[320,512]{1,0:T(8,128)(2,1)} %copy-done.7, bf16[2,512,512]{2,1,0:T(8,128)(2,1)} %key_ref.1, bf16[2,512,512]{2,1,0:T(8,128)(2,1)} %value_ref.1, bf16[32,128]{1,0:T(8,128)(2,1)} %filter_ref.1, f32[16,32]{1,0:T(8,128)} %bitcast.14, f32[16,32]{1,0:T(8,128)} %bitcast.16, f32[1,512]{1,0:T(1,128)} %bitcast.17), custom_call_target="tpu_custom_call" | custom-call | flops 12000000000 | bytes 8388608 | tf_op jit(solution)/shard_map/local/pallas_call | solution.py:417
  43.4 3.9 %all-to-all-done.1 = bf16[8,32,512]{2,1,0:T(8,128)(2,1)S(1)} async-done(((bf16[8,32,512]{2,1,0:T(8,128)(2,1)}), bf16[8,32,512]{2,1,0:T(8,128)(2,1)S(1)}, u32[]{:S(2)}, u32[]{:S(2)}) %all-to-all-start.1) | async-done | bytes 262176 | tf_op jit(solution)/shard_map/all_to_all | solution.py:372
  47.4 0.0 copy-done.1
  47.4 0.0 copy-start
  47.4 1.3 %copy-done = bf16[1152,512]{1,0:T(8,128)(2,1)S(1)} copy-done((bf16[1152,512]{1,0:T(8,128)(2,1)S(1)}, bf16[1152,512]{1,0:T(8,128)(2,1)}, u32[]{:S(2)}) %copy-start) | copy-done | bytes 1179672
  48.7 0.0 copy-start.2
  48.7 0.0 copy-start.3
  48.7 1.8 %gate.1 = (f32[2,512,512]{2,1,0:T(8,128)S(1)}, f32[16,1,1024]{2,1,0:T(1,128)}) custom-call(bf16[256,512]{1,0:T(8,128)(2,1)S(1)} %bitcast.9, f32[32,512]{1,0:T(8,128)S(1)} %get-tuple-element.13.own_ref, f32[1,512]{1,0:T(1,128)S(1)} %reshape.21.rate_ref, bf16[1152,512]{1,0:T(8,128)(2,1)S(1)} %copy-done, bf16[2,512,512]{2,1,0:T(8,128)(2,1)S(1)} %copy-done.1), custom_call_target="tpu_custom_call" | custom-call | tf_op jit(solution)/shard_map/gate/pallas_call | solution.py:455
  50.5 10.4 %all-to-all-start.2 = ((f32[16,1,1024]{2,1,0:T(1,128)}), f32[16,1,1024]{2,1,0:T(1,128)S(1)}, u32[]{:S(2)}, u32[]{:S(2)}) async-start(f32[16,1,1024]{2,1,0:T(1,128)} %get-tuple-element.15), calls=%async_computation.2 | async-start | bytes 131072 | tf_op jit(solution)/shard_map/all_to_all | solution.py:467
  60.8 0.0 copy-done.5
  60.8 0.0 copy-start.4
  60.8 1.0 %copy-done.4 = bf16[512,512]{1,0:T(8,128)(2,1)S(1)} copy-done((bf16[512,512]{1,0:T(8,128)(2,1)S(1)}, bf16[512,512]{1,0:T(8,128)(2,1)}, u32[]{:S(2)}) %copy-start.4) | copy-done | bytes 524312
  61.9 1.1 %embed.1.refs_4_ = bf16[2,512,512]{2,1,0:T(8,128)(2,1)S(1)} custom-call(s32[2,512]{1,0:T(2,128)S(1)} %copy-done.5, bf16[512,512]{1,0:T(8,128)(2,1)S(1)} %copy-done.4), custom_call_target="tpu_custom_call" | custom-call | flops 536870912 | bytes 4194304 | tf_op jit(solution)/shard_map/embed/pallas_call | solution.py:407
  62.9 3.7 %all-to-all-done.2.refs_2_ = f32[16,1,1024]{2,1,0:T(1,128)S(1)} async-done(((f32[16,1,1024]{2,1,0:T(1,128)}), f32[16,1,1024]{2,1,0:T(1,128)S(1)}, u32[]{:S(2)}, u32[]{:S(2)}) %all-to-all-start.2) | async-done | bytes 65568 | tf_op jit(solution)/shard_map/all_to_all | solution.py:467
  66.6 0.0 copy-done.2
  66.6 0.0 copy-done.3
  66.7 1.9 %norm.1 = bf16[2,512,512]{2,1,0:T(8,128)(2,1)} custom-call(s32[2]{0:T(128)S(1)} %copy-done.3, s32[1]{0:T(128)} %bitcast.refs_0_.refs_1_, f32[16,1,1024]{2,1,0:T(1,128)S(1)} %all-to-all-done.2.refs_2_, f32[2,512,512]{2,1,0:T(8,128)S(1)} %get-tuple-element.16.refs_3_, bf16[2,512,512]{2,1,0:T(8,128)(2,1)S(1)} %embed.1.refs_4_, f32[1,512]{1,0:T(1,128)S(1)} %bitcast.11), custom_call_target="tpu_custom_call" | custom-call | tf_op jit(solution)/shard_map/norm/pallas_call | solution.py:472
Async XLA Ops:
  0.0 15.2 %copy-start.6 = (f32[32,16]{0,1:T(8,128)S(1)}, f32[32,16]{0,1:T(8,128)}, u32[]{:S(2)}) copy-start(f32[32,16]{0,1:T(8,128)} %param.18) | copy-start | bytes 6148
  4.1 11.6 %all-to-all-start = ((bf16[4,32,512]{2,1,0:T(8,128)(2,1)}), bf16[4,32,512]{2,1,0:T(8,128)(2,1)S(1)}, u32[]{:S(2)}, u32[]{:S(2)}) async-start(bf16[4,32,512]{2,1,0:T(8,128)(2,1)} %bitcast.12), calls=%async_computation | async-start | bytes 262144 | tf_op jit(solution)/shard_map/all_to_all | solution.py:372
  10.3 20.1 %collective-permute-start = (bf16[320,512]{1,0:T(8,128)(2,1)}, bf16[320,512]{1,0:T(8,128)(2,1)S(1)}, u32[]{:S(2)}, u32[]{:S(2)}) collective-permute-start(bf16[320,512]{1,0:T(8,128)(2,1)} %get-tuple-element.14), channel_id=1, source_target_pairs={{0,16},{16,32},{32,48},{48,64},{64,80},{80,96},{96,112},{112,128},... | collective-permute-start | bytes 983048 | tf_op jit(solution)/shard_map/ppermute | solution.py:404
  16.5 30.9 %all-to-all-start.1 = ((bf16[8,32,512]{2,1,0:T(8,128)(2,1)}), bf16[8,32,512]{2,1,0:T(8,128)(2,1)S(1)}, u32[]{:S(2)}, u32[]{:S(2)}) async-start(bf16[8,32,512]{2,1,0:T(8,128)(2,1)} %bitcast.4), calls=%async_computation.1 | async-start | bytes 524288 | tf_op jit(solution)/shard_map/all_to_all | solution.py:372
  30.4 0.7 %copy-start.7 = (bf16[320,512]{1,0:T(8,128)(2,1)}, bf16[320,512]{1,0:T(8,128)(2,1)S(1)}, u32[]{:S(2)}) copy-start(bf16[320,512]{1,0:T(8,128)(2,1)S(1)} %collective-permute-done.border_ref) | copy-start | bytes 983044
  31.2 16.2 %copy-start.1 = (bf16[2,512,512]{2,1,0:T(8,128)(2,1)S(1)}, bf16[2,512,512]{2,1,0:T(8,128)(2,1)}, u32[]{:S(2)}) copy-start(bf16[2,512,512]{2,1,0:T(8,128)(2,1)} %query_ref.1) | copy-start | bytes 3145732
  31.2 29.7 %copy-start.5 = (s32[2,512]{1,0:T(2,128)S(1)}, s32[2,512]{1,0:T(2,128)}, u32[]{:S(2)}) copy-start(s32[2,512]{1,0:T(2,128)} %token_ref.1) | copy-start | bytes 12292
  47.4 1.3 %copy-start = (bf16[1152,512]{1,0:T(8,128)(2,1)S(1)}, bf16[1152,512]{1,0:T(8,128)(2,1)}, u32[]{:S(2)}) copy-start(bf16[1152,512]{1,0:T(8,128)(2,1)} %local.1.base_ref) | copy-start | bytes 3538948
  48.7 18.0 %copy-start.2 = (f32[512]{0:T(512)S(1)}, f32[512]{0:T(512)}, u32[]{:S(2)}) copy-start(f32[512]{0:T(512)} %param.21) | copy-start | bytes 6148
  48.7 18.0 %copy-start.3 = (s32[2]{0:T(128)S(1)}, s32[2]{0:T(128)}, u32[]{:S(2)}) copy-start(s32[2]{0:T(128)} %refs_0_.1) | copy-start | bytes 28
  50.5 16.2 %all-to-all-start.2 = ((f32[16,1,1024]{2,1,0:T(1,128)}), f32[16,1,1024]{2,1,0:T(1,128)S(1)}, u32[]{:S(2)}, u32[]{:S(2)}) async-start(f32[16,1,1024]{2,1,0:T(1,128)} %get-tuple-element.15), calls=%async_computation.2 | async-start | bytes 131072 | tf_op jit(solution)/shard_map/all_to_all | solution.py:467
  60.8 1.0 %copy-start.4 = (bf16[512,512]{1,0:T(8,128)(2,1)S(1)}, bf16[512,512]{1,0:T(8,128)(2,1)}, u32[]{:S(2)}) copy-start(bf16[512,512]{1,0:T(8,128)(2,1)} %table_ref.1) | copy-start | bytes 1572868

commit v7 on v5

--- a/solution.py
+++ b/solution.py
@@ -125,26 +125,29 @@
         store.wait()
 
 
-def group_kernel(index_ref, rate_ref, state_ref, far_ref, own_ref, *, near, rows):
-    height = own_ref.shape[0]
-    far = far_ref.shape[0] // height
+def group_kernel(index_ref, rate_ref, state_ref, near_ref, *, near, far, rows):
+    height = near_ref.shape[0] // near
     modes = rate_ref.shape[0]
     group, place = index_ref[0] // near, lax.rem(index_ref[0], near)
     rate = jnp.concatenate([rate_ref[...]] * (height // modes), axis=0) * float(rows)
-    decay = jnp.exp(-rate)
-    held = jnp.zeros(own_ref.shape, F32)
-    own, short = held, held
-    for p in range(near):
-        own = jnp.where(place == p + 1, held, own)
-        short = held
-        held = decay * held + state_ref[p * height : (p + 1) * height, :].astype(F32)
-    own_ref[...] = own
-    for other in range(far):
-        ahead = (other - group) * near + place - near - 1
+    stride = jnp.exp(-rate * float(near))
+    held = jnp.zeros(rate.shape, F32)
+    mine, past, short, last = held, held, held, held
+    for g in range(far):
+        state = state_ref[g * height : (g + 1) * height, :].astype(F32)
+        mine = jnp.where(group == g, state, mine)
+        past = jnp.where(group == g, held, past)
+        short = jnp.where(group == g, last, short)
+        last = held
+        held = stride * held + state
+    short = jnp.exp(-rate * (near - 1.0)) * short
+    for other in range(near):
+        ahead = other - place - 2
         weight = jnp.exp(-rate * jnp.maximum(ahead, 0).astype(F32))
-        value = jnp.where(ahead < 0, short, weight * held)
-        value = jnp.where(other > group, value, 0.0)
-        far_ref[other * height : (other + 1) * height, :] = value.astype(BF16)
+        value = jnp.where(ahead >= 0, weight * mine, 0.0)
+        weight = jnp.exp(-rate * jnp.maximum(ahead + near, 0).astype(F32))
+        value = value + jnp.where(ahead + near >= 0, weight * past, short)
+        near_ref[other * height : (other + 1) * height, :] = value.astype(BF16)
 
 
 def dot_rows(a, b):
@@ -152,6 +155,7 @@
 
 
 def local_kernel(
+    index_ref,
     border_ref,
     key_ref,
     value_ref,
@@ -160,6 +164,7 @@
     residue_ref,
     skip_ref,
     base_ref,
+    turn_ref,
     product_window,
     mixed_window,
     turned,
@@ -241,6 +246,7 @@
     early = early + border_ref[first + state_rows :, :].astype(F32)
     factors = jnp.concatenate([decay, gain, early], axis=0)
     base_ref[samples * rows :, :] = jnp.concatenate(halves(factors), axis=0)
+    turn_ref[0] = index_ref[0]
 
 
 def embed_kernel(token_ref, table_ref, out_ref):
@@ -253,11 +259,11 @@
 
 
 def gate_kernel(
-    far_ref, own_ref, rate_ref, base_ref, query_ref, gated_ref, sum_ref, squares
+    part_ref, rate_ref, base_ref, query_ref, gated_ref, sum_ref, squares
 ):
     samples, rows, width = query_ref.shape
     height = (base_ref.shape[0] - samples * rows) // 2
-    modes = own_ref.shape[0] // samples
+    modes = height // (2 + samples)
     copies = sum_ref.shape[0]
     own = iota((LANES, LANES), 0) // modes == iota((LANES, LANES), 1) // GROUP
     for tile in range(width // LANES):
@@ -273,9 +279,9 @@
         factors = base_ref[samples * rows :, lanes].astype(F32)
         factors = factors[:height] + factors[height:]
         for s in range(samples):
-            carried = own_ref[s * modes : (s + 1) * modes, lanes]
-            for first in range(s * modes, far_ref.shape[0], samples * modes):
-                carried = carried + far_ref[first : first + modes, lanes].astype(F32)
+            carried = jnp.zeros((modes, LANES), F32)
+            for first in range(s * modes, part_ref.shape[0], samples * modes):
+                carried = carried + part_ref[first : first + modes, lanes].astype(F32)
             early = factors[(s + 2) * modes : (s + 3) * modes]
             state = (factors[:modes] * carried + early) * factors[modes : 2 * modes]
             spread = jnp.concatenate([state] * TILE_GROUPS, axis=0)
@@ -385,14 +391,14 @@
         in_specs=[anywhere, anywhere, anywhere],
         out_specs=[anywhere, anywhere],
         out_shape=[
-            shape((near * state_rows, width), BF16),
+            shape((far * state_rows, width), BF16),
             shape((border_rows, width), BF16),
         ],
         scratch_shapes=[
             pltpu.VMEM((modes, groups), F32),
             pltpu.VMEM((samples, rows, width), BF16),
             pltpu.VMEM((samples, rows, width), BF16),
-            pltpu.VMEM((near * state_rows, width), BF16),
+            pltpu.VMEM((far * state_rows, width), BF16),
             pltpu.VMEM((border_rows, width), BF16),
             pltpu.SemaphoreType.DMA((1,)),
             pltpu.SemaphoreType.DMA((2, tiles)),
@@ -402,7 +408,7 @@
         name="states",
     )(rates, key_act, value_act)
     before = lax.ppermute(border, "ctx", [(i, i + 1) for i in range(chunks - 1)])
-    gathered = exchange(states, near_groups)
+    gathered = exchange(states, far_groups)
 
     embedded = pl.pallas_call(
         embed_kernel,
@@ -414,12 +420,12 @@
         name="embed",
     )(token_ids, embedding)
 
-    base = pl.pallas_call(
+    base, turn = pl.pallas_call(
         local_kernel,
         grid=(tiles,),
-        in_specs=[flat(border_rows), cube(), cube(), grouped(taps), whole, whole, flat(1)],
-        out_specs=flat(base_rows),
-        out_shape=shape((base_rows, width), BF16),
+        in_specs=[smem, flat(border_rows), cube(), cube(), grouped(taps), whole, whole, flat(1)],
+        out_specs=[flat(base_rows), smem],
+        out_shape=[shape((base_rows, width), BF16), shape((1,), jnp.int32)],
         scratch_shapes=[
             pltpu.VMEM((samples, LANES, rows + 2 * taps), BF16),
             pltpu.VMEM((samples, LANES, 2 * rows), BF16),
@@ -431,6 +437,7 @@
         compiler_params=params(60),
         name="local",
     )(
+        index,
         before,
         key_act,
         value_act,
@@ -441,16 +448,16 @@
     )
 
     def group_step(*refs):
-        group_kernel(*refs, near=near, rows=rows)
-
-    sent, own = pl.pallas_call(
+        group_kernel(*refs, near=near, far=far, rows=rows)
+
+    sent = pl.pallas_call(
         group_step,
         in_specs=[smem, vmem, vmem],
-        out_shape=[shape((far * state_rows, width), BF16), shape((state_rows, width), F32)],
+        out_shape=shape((near * state_rows, width), BF16),
         compiler_params=params(8),
         name="group",
-    )(index, jnp.repeat(rates, GROUP, axis=1), gathered)
-    carried = exchange(sent, far_groups)
+    )(turn, jnp.repeat(rates, GROUP, axis=1), gathered)
+    carried = exchange(sent, near_groups)
 
     gated, sums = pl.pallas_call(
         gate_kernel,
@@ -463,7 +470,7 @@
         ],
         compiler_params=params(16),
         name="gate",
-    )(carried, own, decay_rates.reshape(1, groups * modes), base, query_act)
+    )(carried, decay_rates.reshape(1, groups * modes), base, query_act)
     shares = lax.all_to_all(sums, "tp", split_axis=0, concat_axis=0, tiled=True)
 
     def norm(*refs):

time: 67.7 us -> 72.4 us (1.069)
  waiting for transfers between devices: 7.05 us -> 12.1 us
  starting transfers between devices: 34.6 us -> 33.5 us
  Pallas kernels: 22 us -> 22.8 us
    all_to_all x2, waiting for transfers between devices: 3.34 us -> 8.35 us  [exchange(): lax.all_to_all(blocks, 'ctx', split_axis=0, concat_axis=0, axis_index_gro...]
    all_to_all x2, starting transfers between devices: 21.6 us -> 18.2 us  [exchange(): lax.all_to_all(blocks, 'ctx', split_axis=0, concat_axis=0, axis_index_gro...]
    all_to_all x1, starting transfers between devices: 8.15 us -> 9.82 us  [per_device(): shares = lax.all_to_all(sums, 'tp', split_axis=0, concat_axis=0, tiled=True)]
    pallas_call x2, Pallas kernels: 13 us -> 13.8 us  [the longest x1 12.4 us: per_device(): pl.pallas_call(local_kernel, grid=(tiles,), in_specs=[smem, flat(border_r...]
    unnamed x17 -> x19, local copies, waits for them, and re-layouts: 3.12 us -> 3.12 us
  transfers between devices with their start and end apart: 4 -> 4, of which waited for: 2 -> 2; matrix products, arithmetic and copies ran while one was open for 1% -> 1% of each run, Pallas kernels for 21% -> 19%
where the time goes in v7:
time: 72.4 us; the launch traced here: 71.9 us
  starting transfers between devices  33.5 us (46%)
  Pallas kernels  22.8 us (31%)
  waiting for transfers between devices  12.1 us (17%)
  local copies, waits for them, and re-layouts  3.48 us (5%)
    all_to_all x2, starting transfers between devices, exchange(): lax.all_to_all(blocks, 'ctx', split_axis=0, concat_axis=0, axis_index_gro...  18.2 us
    pallas_call x1, Pallas kernels, per_device(): pl.pallas_call(local_kernel, grid=(tiles,), in_specs=[smem, flat(border_r...  12.4 us
    all_to_all x1, starting transfers between devices, per_device(): shares = lax.all_to_all(sums, 'tp', split_axis=0, concat_axis=0, tiled=True)  9.82 us
    all_to_all x2, waiting for transfers between devices, exchange(): lax.all_to_all(blocks, 'ctx', split_axis=0, concat_axis=0, axis_index_gro...  8.35 us
    ppermute x1, starting transfers between devices, per_device(): lax.ppermute(border, 'ctx', [(i, i + 1) for i in range(chunks - 1)])  5.5 us
    pallas_call x1, Pallas kernels, per_device(): pl.pallas_call(states_step, in_specs=[anywhere, anywhere, anywhere], out_...  4.08 us
    all_to_all x1, waiting for transfers between devices, per_device(): shares = lax.all_to_all(sums, 'tp', split_axis=0, concat_axis=0, tiled=True)  3.7 us
    unnamed x19, local copies, waits for them, and re-layouts  3.12 us
  transfers between devices with their start and end apart: 4, of which 2 were waited for; matrix products, arithmetic and copies ran while one was open for 1% of the time, Pallas kernels for 19%

profile of v7, /device:TPU:1, one launch (start us, length us, event | category | flops | bytes accessed | tf_op | source)
XLA Modules:
  0.0 71.9 jit_solution(17097247514182242294)
XLA Ops:
  0.0 0.0 copy-start.6
  0.0 4.1 %states.1 = (bf16[128,512]{1,0:T(8,128)(2,1)}, bf16[320,512]{1,0:T(8,128)(2,1)}) custom-call(f32[16,32]{1,0:T(8,128)} %bitcast.13, bf16[2,512,512]{2,1,0:T(8,128)(2,1)} %key_ref.1, bf16[2,512,512]{2,1,0:T(8,128)(2,1)} %value_ref.1), custom_call_target="tpu_custom_call" | custom-call | tf_op jit(solution)/shard_map/states/pallas_call | solution.py:389
  4.1 5.5 %collective-permute-start = (bf16[320,512]{1,0:T(8,128)(2,1)}, bf16[320,512]{1,0:T(8,128)(2,1)S(1)}, u32[]{:S(2)}, u32[]{:S(2)}) collective-permute-start(bf16[320,512]{1,0:T(8,128)(2,1)} %get-tuple-element.11), channel_id=1, source_target_pairs={{0,16},{16,32},{32,48},{48,64},{64,80},{80,96},{96,112},{112,128},... | collective-permute-start | bytes 983048 | tf_op jit(solution)/shard_map/ppermute | solution.py:410
  9.6 14.8 %all-to-all-start = ((bf16[4,32,512]{2,1,0:T(8,128)(2,1)}), bf16[4,32,512]{2,1,0:T(8,128)(2,1)S(1)}, u32[]{:S(2)}, u32[]{:S(2)}) async-start(bf16[4,32,512]{2,1,0:T(8,128)(2,1)} %bitcast.12), calls=%async_computation | async-start | bytes 262144 | tf_op jit(solution)/shard_map/all_to_all | solution.py:378
  24.4 0.0 copy-done.6
  24.4 0.1 broadcast_in_dim.3
  24.5 0.2 reshape.21.refs_1_
  24.7 0.0 collective-permute-done.border_ref
  24.7 0.0 copy-start.8
  24.7 0.7 copy-done.8
  25.4 0.0 copy-start.7
  25.4 0.0 copy-start.1
  25.4 12.4 %local.1 = (bf16[1152,512]{1,0:T(8,128)(2,1)}, s32[1]{0:T(128)}) custom-call(s32[1]{0:T(128)} %bitcast.index_ref.refs_1_, bf16[320,512]{1,0:T(8,128)(2,1)} %copy-done.8, bf16[2,512,512]{2,1,0:T(8,128)(2,1)} %key_ref.1, bf16[2,512,512]{2,1,0:T(8,128)(2,1)} %value_ref.1, bf16[32,128]{1,0:T(8,128)(2,1)} %filter_ref.1, f32[16,32]{1,0:T(8,128)} %bitcast.14, ...), custom_call_target="tpu_custom_call" | custom-call | flops 12000000000 | bytes 8388608 | tf_op jit(solution)/shard_map/local/pallas_call | solution.py:423
  37.8 0.0 copy-start.5
  37.8 0.0 all-to-all-done
  37.8 1.5 %group.1 = bf16[256,512]{1,0:T(8,128)(2,1)} custom-call(s32[1]{0:T(128)} %get-tuple-element.12.refs_0_, f32[16,512]{1,0:T(8,128)S(1)} %reshape.21.refs_1_, bf16[128,512]{1,0:T(8,128)(2,1)S(1)} %bitcast.10), custom_call_target="tpu_custom_call" | custom-call | tf_op jit(solution)/shard_map/group/pallas_call | solution.py:453
  39.2 3.4 %all-to-all-start.1 = ((bf16[8,32,512]{2,1,0:T(8,128)(2,1)}), bf16[8,32,512]{2,1,0:T(8,128)(2,1)S(1)}, u32[]{:S(2)}, u32[]{:S(2)}) async-start(bf16[8,32,512]{2,1,0:T(8,128)(2,1)} %bitcast.6), calls=%async_computation.1 | async-start | bytes 524288 | tf_op jit(solution)/shard_map/all_to_all | solution.py:378
  42.7 0.0 copy-done.7
  42.7 0.1 copy.13
  42.8 0.1 reshape.22.rate_ref
  42.8 8.3 %all-to-all-done.1 = bf16[8,32,512]{2,1,0:T(8,128)(2,1)S(1)} async-done(((bf16[8,32,512]{2,1,0:T(8,128)(2,1)}), bf16[8,32,512]{2,1,0:T(8,128)(2,1)S(1)}, u32[]{:S(2)}, u32[]{:S(2)}) %all-to-all-start.1) | async-done | bytes 262176 | tf_op jit(solution)/shard_map/all_to_all | solution.py:378
  51.2 0.0 copy-done.1
  51.2 0.0 copy-start
  51.2 1.3 %copy-done = bf16[1152,512]{1,0:T(8,128)(2,1)S(1)} copy-done((bf16[1152,512]{1,0:T(8,128)(2,1)S(1)}, bf16[1152,512]{1,0:T(8,128)(2,1)}, u32[]{:S(2)}) %copy-start) | copy-done | bytes 1179672
  52.5 0.0 copy-start.2
  52.5 0.0 copy-start.3
  52.5 1.8 %gate.1 = (f32[2,512,512]{2,1,0:T(8,128)S(1)}, f32[16,1,1024]{2,1,0:T(1,128)}) custom-call(bf16[256,512]{1,0:T(8,128)(2,1)S(1)} %bitcast.9, f32[1,512]{1,0:T(1,128)S(1)} %reshape.22.rate_ref, bf16[1152,512]{1,0:T(8,128)(2,1)S(1)} %copy-done, bf16[2,512,512]{2,1,0:T(8,128)(2,1)S(1)} %copy-done.1), custom_call_target="tpu_custom_call" | custom-call | tf_op jit(solution)/shard_map/gate/pallas_call | solution.py:462
  54.3 9.8 %all-to-all-start.2 = ((f32[16,1,1024]{2,1,0:T(1,128)}), f32[16,1,1024]{2,1,0:T(1,128)S(1)}, u32[]{:S(2)}, u32[]{:S(2)}) async-start(f32[16,1,1024]{2,1,0:T(1,128)} %get-tuple-element.15), calls=%async_computation.2 | async-start | bytes 131072 | tf_op jit(solution)/shard_map/all_to_all | solution.py:474
  64.1 0.0 copy-done.5
  64.1 0.0 copy-start.4
  64.1 1.0 %copy-done.4 = bf16[512,512]{1,0:T(8,128)(2,1)S(1)} copy-done((bf16[512,512]{1,0:T(8,128)(2,1)S(1)}, bf16[512,512]{1,0:T(8,128)(2,1)}, u32[]{:S(2)}) %copy-start.4) | copy-done | bytes 524312
  65.2 1.1 %embed.1.refs_4_ = bf16[2,512,512]{2,1,0:T(8,128)(2,1)S(1)} custom-call(s32[2,512]{1,0:T(2,128)S(1)} %copy-done.5, bf16[512,512]{1,0:T(8,128)(2,1)S(1)} %copy-done.4), custom_call_target="tpu_custom_call" | custom-call | flops 536870912 | bytes 4194304 | tf_op jit(solution)/shard_map/embed/pallas_call | solution.py:413
  66.2 3.7 %all-to-all-done.2.refs_2_ = f32[16,1,1024]{2,1,0:T(1,128)S(1)} async-done(((f32[16,1,1024]{2,1,0:T(1,128)}), f32[16,1,1024]{2,1,0:T(1,128)S(1)}, u32[]{:S(2)}, u32[]{:S(2)}) %all-to-all-start.2) | async-done | bytes 65568 | tf_op jit(solution)/shard_map/all_to_all | solution.py:474
  69.9 0.0 copy-done.2
  70.0 0.0 copy-done.3
  70.0 2.0 %norm.1 = bf16[2,512,512]{2,1,0:T(8,128)(2,1)} custom-call(s32[2]{0:T(128)S(1)} %copy-done.3, s32[1]{0:T(128)} %bitcast.index_ref.refs_1_, f32[16,1,1024]{2,1,0:T(1,128)S(1)} %all-to-all-done.2.refs_2_, f32[2,512,512]{2,1,0:T(8,128)S(1)} %get-tuple-element.16.refs_3_, bf16[2,512,512]{2,1,0:T(8,128)(2,1)S(1)} %embed.1.refs_4_, f32[1,512]{1,0:T(1,128)S(1)} %bitcast.11), custom_call_target="tpu_custom_call" | custom-call | tf_op jit(solution)/shard_map/norm/pallas_call | solution.py:479
Async XLA Ops:
  0.0 24.4 %copy-start.6 = (f32[32,16]{0,1:T(8,128)S(1)}, f32[32,16]{0,1:T(8,128)}, u32[]{:S(2)}) copy-start(f32[32,16]{0,1:T(8,128)} %param.18) | copy-start | bytes 6148
  4.1 20.6 %collective-permute-start = (bf16[320,512]{1,0:T(8,128)(2,1)}, bf16[320,512]{1,0:T(8,128)(2,1)S(1)}, u32[]{:S(2)}, u32[]{:S(2)}) collective-permute-start(bf16[320,512]{1,0:T(8,128)(2,1)} %get-tuple-element.11), channel_id=1, source_target_pairs={{0,16},{16,32},{32,48},{48,64},{64,80},{80,96},{96,112},{112,128},... | collective-permute-start | bytes 983048 | tf_op jit(solution)/shard_map/ppermute | solution.py:410
  9.6 28.2 %all-to-all-start = ((bf16[4,32,512]{2,1,0:T(8,128)(2,1)}), bf16[4,32,512]{2,1,0:T(8,128)(2,1)S(1)}, u32[]{:S(2)}, u32[]{:S(2)}) async-start(bf16[4,32,512]{2,1,0:T(8,128)(2,1)} %bitcast.12), calls=%async_computation | async-start | bytes 262144 | tf_op jit(solution)/shard_map/all_to_all | solution.py:378
  24.7 0.7 %copy-start.8 = (bf16[320,512]{1,0:T(8,128)(2,1)}, bf16[320,512]{1,0:T(8,128)(2,1)S(1)}, u32[]{:S(2)}) copy-start(bf16[320,512]{1,0:T(8,128)(2,1)S(1)} %collective-permute-done.border_ref) | copy-start | bytes 983044
  25.4 17.2 %copy-start.7 = (f32[32,16]{0,1:T(8,128)S(1)}, f32[32,16]{0,1:T(8,128)}, u32[]{:S(2)}) copy-start(f32[32,16]{0,1:T(8,128)} %param.18) | copy-start | bytes 6148
  25.4 25.8 %copy-start.1 = (bf16[2,512,512]{2,1,0:T(8,128)(2,1)S(1)}, bf16[2,512,512]{2,1,0:T(8,128)(2,1)}, u32[]{:S(2)}) copy-start(bf16[2,512,512]{2,1,0:T(8,128)(2,1)} %query_ref.1) | copy-start | bytes 3145732
  37.8 26.3 %copy-start.5 = (s32[2,512]{1,0:T(2,128)S(1)}, s32[2,512]{1,0:T(2,128)}, u32[]{:S(2)}) copy-start(s32[2,512]{1,0:T(2,128)} %token_ref.1) | copy-start | bytes 12292
  39.2 11.9 %all-to-all-start.1 = ((bf16[8,32,512]{2,1,0:T(8,128)(2,1)}), bf16[8,32,512]{2,1,0:T(8,128)(2,1)S(1)}, u32[]{:S(2)}, u32[]{:S(2)}) async-start(bf16[8,32,512]{2,1,0:T(8,128)(2,1)} %bitcast.6), calls=%async_computation.1 | async-start | bytes 524288 | tf_op jit(solution)/shard_map/all_to_all | solution.py:378
  51.2 1.3 %copy-start = (bf16[1152,512]{1,0:T(8,128)(2,1)S(1)}, bf16[1152,512]{1,0:T(8,128)(2,1)}, u32[]{:S(2)}) copy-start(bf16[1152,512]{1,0:T(8,128)(2,1)} %get-tuple-element.14.base_ref) | copy-start | bytes 3538948
  52.5 17.5 %copy-start.2 = (f32[512]{0:T(512)S(1)}, f32[512]{0:T(512)}, u32[]{:S(2)}) copy-start(f32[512]{0:T(512)} %param.21) | copy-start | bytes 6148
  52.5 17.5 %copy-start.3 = (s32[2]{0:T(128)S(1)}, s32[2]{0:T(128)}, u32[]{:S(2)}) copy-start(s32[2]{0:T(128)} %refs_0_.1) | copy-start | bytes 28
  54.3 15.6 %all-to-all-start.2 = ((f32[16,1,1024]{2,1,0:T(1,128)}), f32[16,1,1024]{2,1,0:T(1,128)S(1)}, u32[]{:S(2)}, u32[]{:S(2)}) async-start(f32[16,1,1024]{2,1,0:T(1,128)} %get-tuple-element.15), calls=%async_computation.2 | async-start | bytes 131072 | tf_op jit(solution)/shard_map/all_to_all | solution.py:474
  64.1 1.0 %copy-start.4 = (bf16[512,512]{1,0:T(8,128)(2,1)S(1)}, bf16[512,512]{1,0:T(8,128)(2,1)}, u32[]{:S(2)}) copy-start(bf16[512,512]{1,0:T(8,128)(2,1)} %table_ref.1) | copy-start | bytes 1572868

commit v8 on v5

--- a/solution.py
+++ b/solution.py
@@ -8,6 +8,7 @@
 GROUP = 16
 LANES = 128
 TILE_GROUPS = LANES // GROUP
+AHEAD = 3
 F32 = jnp.float32
 BF16 = jnp.bfloat16
 
@@ -78,9 +79,10 @@
                 value_source.at[:, :, lanes], value_ref.at[:, :, lanes], arrived.at[1, tile]
             ),
         )
+        loads.append(pair)
+    for pair in loads[:AHEAD]:
         for load in pair:
             load.start()
-        loads.append(pair)
     rate_load.wait()
     tables = []
     for tile in range(len(tiles)):
@@ -96,6 +98,8 @@
         half = weights.shape[0] // 2
         for load in loads[tile]:
             load.wait()
+        for load in loads[tile + AHEAD] if tile + AHEAD < len(tiles) else ():
+            load.start()
         for s in range(samples):
             product = product_of(key_ref[s, :, lanes], value_ref[s, :, lanes])
             full = dot(weights, product)
@@ -106,10 +110,9 @@
                 state_ref[at : at + modes, lanes] = state
             border_ref[s * taps : (s + 1) * taps, lanes] = product[rows - taps :]
             early = dot(weights[:, taps:], product[: rows - taps])
-            upper, lower = halves(own_group(early[:half] + early[half:], modes))
             first = samples * taps + s * modes
-            border_ref[first : first + modes, lanes] = upper
-            border_ref[first + samples * modes : first + (samples + 1) * modes, lanes] = lower
+            early = own_group(early[:half] + early[half:], modes)
+            border_ref[first : first + modes, lanes] = early.astype(BF16)
         pair = (
             pltpu.make_async_copy(
                 state_ref.at[:, lanes], state_target.at[:, lanes], left.at[0, tile]
@@ -236,9 +239,7 @@
     square = (TILE_GROUPS * modes, LANES)
     decay = own_group(jnp.broadcast_to(jnp.exp(-rate * float(rows - taps)), square), modes)
     gain = own_group(jnp.broadcast_to(gain, square), modes)
-    first, state_rows = samples * taps, samples * modes
-    early = border_ref[first : first + state_rows, :].astype(F32)
-    early = early + border_ref[first + state_rows :, :].astype(F32)
+    early = border_ref[samples * taps :, :].astype(F32)
     factors = jnp.concatenate([decay, gain, early], axis=0)
     base_ref[samples * rows :, :] = jnp.concatenate(halves(factors), axis=0)
 
@@ -358,7 +359,7 @@
         return pl.BlockSpec((TILE_GROUPS, cols), lambda i: (i, 0))
 
     state_rows = samples * modes
-    border_rows = samples * taps + 2 * state_rows
+    border_rows = samples * taps + state_rows
     base_rows = samples * rows + 2 * (2 * modes + state_rows)
     shape = jax.ShapeDtypeStruct
     whole = pl.BlockSpec((modes, groups), lambda i: (0, 0))

time: 67.7 us -> 67.6 us (level)
  no operation moved by 1% of the time
where the time goes in v8:
time: 67.6 us; the launch traced here: 67.1 us
  starting transfers between devices  34.7 us (51%)
  Pallas kernels  21.9 us (32%)
  waiting for transfers between devices  7.05 us (10%)
  local copies, waits for them, and re-layouts  3.47 us (5%)
    all_to_all x2, starting transfers between devices, exchange(): lax.all_to_all(blocks, 'ctx', split_axis=0, concat_axis=0, axis_index_gro...  21.6 us
    pallas_call x1, Pallas kernels, per_device(): pl.pallas_call(local_kernel, grid=(tiles,), in_specs=[flat(border_rows),...  12.3 us
    all_to_all x1, starting transfers between devices, per_device(): shares = lax.all_to_all(sums, 'tp', split_axis=0, concat_axis=0, tiled=True)  8.19 us
    ppermute x1, starting transfers between devices, per_device(): lax.ppermute(border, 'ctx', [(i, i + 1) for i in range(chunks - 1)])  4.87 us
    pallas_call x1, Pallas kernels, per_device(): pl.pallas_call(states_step, in_specs=[anywhere, anywhere, anywhere], out_...  3.99 us
    all_to_all x1, waiting for transfers between devices, per_device(): shares = lax.all_to_all(sums, 'tp', split_axis=0, concat_axis=0, tiled=True)  3.71 us
    all_to_all x2, waiting for transfers between devices, exchange(): lax.all_to_all(blocks, 'ctx', split_axis=0, concat_axis=0, axis_index_gro...  3.34 us
    unnamed x17, local copies, waits for them, and re-layouts  3.11 us
  transfers between devices with their start and end apart: 4, of which 2 were waited for; matrix products, arithmetic and copies ran while one was open for 1% of the time, Pallas kernels for 21%

profile of v8, /device:TPU:1, one launch (start us, length us, event | category | flops | bytes accessed | tf_op | source)
XLA Modules:
  0.0 67.1 jit_solution(11790381770323473476)
XLA Ops:
  0.0 0.0 copy-start.6
  0.0 4.0 %states.1 = (bf16[256,512]{1,0:T(8,128)(2,1)}, bf16[288,512]{1,0:T(8,128)(2,1)}) custom-call(f32[16,32]{1,0:T(8,128)} %bitcast.13, bf16[2,512,512]{2,1,0:T(8,128)(2,1)} %key_ref.1, bf16[2,512,512]{2,1,0:T(8,128)(2,1)} %value_ref.1), custom_call_target="tpu_custom_call" | custom-call | tf_op jit(solution)/shard_map/states/pallas_call | solution.py:384
  4.0 8.9 %all-to-all-start = ((bf16[8,32,512]{2,1,0:T(8,128)(2,1)}), bf16[8,32,512]{2,1,0:T(8,128)(2,1)S(1)}, u32[]{:S(2)}, u32[]{:S(2)}) async-start(bf16[8,32,512]{2,1,0:T(8,128)(2,1)} %bitcast.12), calls=%async_computation | async-start | bytes 524288 | tf_op jit(solution)/shard_map/all_to_all | solution.py:373
  12.9 4.9 %collective-permute-start = (bf16[288,512]{1,0:T(8,128)(2,1)}, bf16[288,512]{1,0:T(8,128)(2,1)S(1)}, u32[]{:S(2)}, u32[]{:S(2)}) collective-permute-start(bf16[288,512]{1,0:T(8,128)(2,1)} %get-tuple-element.14), channel_id=1, source_target_pairs={{0,16},{16,32},{32,48},{48,64},{64,80},{80,96},{96,112},{112,128},... | collective-permute-start | bytes 884744 | tf_op jit(solution)/shard_map/ppermute | solution.py:405
  17.8 0.0 copy-done.6
  17.8 0.1 copy.13
  17.9 0.1 reshape.21.rate_ref
  18.0 0.1 broadcast_in_dim.3
  18.1 0.2 reshape.20.refs_1_
  18.3 3.3 %all-to-all-done = bf16[8,32,512]{2,1,0:T(8,128)(2,1)S(1)} async-done(((bf16[8,32,512]{2,1,0:T(8,128)(2,1)}), bf16[8,32,512]{2,1,0:T(8,128)(2,1)S(1)}, u32[]{:S(2)}, u32[]{:S(2)}) %all-to-all-start) | async-done | bytes 262176 | tf_op jit(solution)/shard_map/all_to_all | solution.py:373
  21.6 0.8 %group.1 = (bf16[128,512]{1,0:T(8,128)(2,1)}, f32[32,512]{1,0:T(8,128)S(1)}) custom-call(s32[1]{0:T(128)} %bitcast.refs_0_.refs_1_, f32[16,512]{1,0:T(8,128)S(1)} %reshape.20.refs_1_, bf16[256,512]{1,0:T(8,128)(2,1)S(1)} %bitcast.9), custom_call_target="tpu_custom_call" | custom-call | tf_op jit(solution)/shard_map/group/pallas_call | solution.py:447
  22.4 12.7 %all-to-all-start.1 = ((bf16[4,32,512]{2,1,0:T(8,128)(2,1)}), bf16[4,32,512]{2,1,0:T(8,128)(2,1)S(1)}, u32[]{:S(2)}, u32[]{:S(2)}) async-start(bf16[4,32,512]{2,1,0:T(8,128)(2,1)} %bitcast.4), calls=%async_computation.1 | async-start | bytes 262144 | tf_op jit(solution)/shard_map/all_to_all | solution.py:373
  35.0 0.0 collective-permute-done.border_ref
  35.0 0.0 copy-start.7
  35.0 0.7 %copy-done.7 = bf16[288,512]{1,0:T(8,128)(2,1)} copy-done((bf16[288,512]{1,0:T(8,128)(2,1)}, bf16[288,512]{1,0:T(8,128)(2,1)S(1)}, u32[]{:S(2)}) %copy-start.7) | copy-done | bytes 294936
  35.8 0.0 copy-start.1
  35.8 0.0 copy-start.5
  35.8 12.3 %local.1.base_ref = bf16[1152,512]{1,0:T(8,128)(2,1)} custom-call(bf16[288,512]{1,0:T(8,128)(2,1)} %copy-done.7, bf16[2,512,512]{2,1,0:T(8,128)(2,1)} %key_ref.1, bf16[2,512,512]{2,1,0:T(8,128)(2,1)} %value_ref.1, bf16[32,128]{1,0:T(8,128)(2,1)} %filter_ref.1, f32[16,32]{1,0:T(8,128)} %bitcast.14, f32[16,32]{1,0:T(8,128)} %bitcast.16, f32[1,512]{1,0:T(1,128)} %bitcast.17), custom_call_target="tpu_custom_call" | custom-call | flops 12000000000 | bytes 8388608 | tf_op jit(solution)/shard_map/local/pallas_call | solution.py:418
  48.0 0.0 all-to-all-done.1
  48.1 0.0 copy-done.1
  48.1 0.0 copy-start
  48.1 1.3 %copy-done = bf16[1152,512]{1,0:T(8,128)(2,1)S(1)} copy-done((bf16[1152,512]{1,0:T(8,128)(2,1)S(1)}, bf16[1152,512]{1,0:T(8,128)(2,1)}, u32[]{:S(2)}) %copy-start) | copy-done | bytes 1179672
  49.3 0.0 copy-start.2
  49.3 0.0 copy-start.3
  49.3 1.8 %gate.1 = (f32[2,512,512]{2,1,0:T(8,128)S(1)}, f32[16,1,1024]{2,1,0:T(1,128)}) custom-call(bf16[128,512]{1,0:T(8,128)(2,1)S(1)} %bitcast.10, f32[32,512]{1,0:T(8,128)S(1)} %get-tuple-element.13.own_ref, f32[1,512]{1,0:T(1,128)S(1)} %reshape.21.rate_ref, bf16[1152,512]{1,0:T(8,128)(2,1)S(1)} %copy-done, bf16[2,512,512]{2,1,0:T(8,128)(2,1)S(1)} %copy-done.1), custom_call_target="tpu_custom_call" | custom-call | tf_op jit(solution)/shard_map/gate/pallas_call | solution.py:456
  51.2 8.2 %all-to-all-start.2 = ((f32[16,1,1024]{2,1,0:T(1,128)}), f32[16,1,1024]{2,1,0:T(1,128)S(1)}, u32[]{:S(2)}, u32[]{:S(2)}) async-start(f32[16,1,1024]{2,1,0:T(1,128)} %get-tuple-element.15), calls=%async_computation.2 | async-start | bytes 131072 | tf_op jit(solution)/shard_map/all_to_all | solution.py:468
  59.4 0.0 copy-done.5
  59.4 0.0 copy-start.4
  59.4 1.0 %copy-done.4 = bf16[512,512]{1,0:T(8,128)(2,1)S(1)} copy-done((bf16[512,512]{1,0:T(8,128)(2,1)S(1)}, bf16[512,512]{1,0:T(8,128)(2,1)}, u32[]{:S(2)}) %copy-start.4) | copy-done | bytes 524312
  60.4 1.1 %embed.1.refs_4_ = bf16[2,512,512]{2,1,0:T(8,128)(2,1)S(1)} custom-call(s32[2,512]{1,0:T(2,128)S(1)} %copy-done.5, bf16[512,512]{1,0:T(8,128)(2,1)S(1)} %copy-done.4), custom_call_target="tpu_custom_call" | custom-call | flops 536870912 | bytes 4194304 | tf_op jit(solution)/shard_map/embed/pallas_call | solution.py:408
  61.5 3.7 %all-to-all-done.2.refs_2_ = f32[16,1,1024]{2,1,0:T(1,128)S(1)} async-done(((f32[16,1,1024]{2,1,0:T(1,128)}), f32[16,1,1024]{2,1,0:T(1,128)S(1)}, u32[]{:S(2)}, u32[]{:S(2)}) %all-to-all-start.2) | async-done | bytes 65568 | tf_op jit(solution)/shard_map/all_to_all | solution.py:468
  65.2 0.0 copy-done.2
  65.2 0.0 copy-done.3
  65.2 2.0 %norm.1 = bf16[2,512,512]{2,1,0:T(8,128)(2,1)} custom-call(s32[2]{0:T(128)S(1)} %copy-done.3, s32[1]{0:T(128)} %bitcast.refs_0_.refs_1_, f32[16,1,1024]{2,1,0:T(1,128)S(1)} %all-to-all-done.2.refs_2_, f32[2,512,512]{2,1,0:T(8,128)S(1)} %get-tuple-element.16.refs_3_, bf16[2,512,512]{2,1,0:T(8,128)(2,1)S(1)} %embed.1.refs_4_, f32[1,512]{1,0:T(1,128)S(1)} %bitcast.11), custom_call_target="tpu_custom_call" | custom-call | tf_op jit(solution)/shard_map/norm/pallas_call | solution.py:473
Async XLA Ops:
  0.0 17.8 %copy-start.6 = (f32[32,16]{0,1:T(8,128)S(1)}, f32[32,16]{0,1:T(8,128)}, u32[]{:S(2)}) copy-start(f32[32,16]{0,1:T(8,128)} %param.18) | copy-start | bytes 6148
  4.0 17.6 %all-to-all-start = ((bf16[8,32,512]{2,1,0:T(8,128)(2,1)}), bf16[8,32,512]{2,1,0:T(8,128)(2,1)S(1)}, u32[]{:S(2)}, u32[]{:S(2)}) async-start(bf16[8,32,512]{2,1,0:T(8,128)(2,1)} %bitcast.12), calls=%async_computation | async-start | bytes 524288 | tf_op jit(solution)/shard_map/all_to_all | solution.py:373
  12.9 22.1 %collective-permute-start = (bf16[288,512]{1,0:T(8,128)(2,1)}, bf16[288,512]{1,0:T(8,128)(2,1)S(1)}, u32[]{:S(2)}, u32[]{:S(2)}) collective-permute-start(bf16[288,512]{1,0:T(8,128)(2,1)} %get-tuple-element.14), channel_id=1, source_target_pairs={{0,16},{16,32},{32,48},{48,64},{64,80},{80,96},{96,112},{112,128},... | collective-permute-start | bytes 884744 | tf_op jit(solution)/shard_map/ppermute | solution.py:405
  22.4 25.7 %all-to-all-start.1 = ((bf16[4,32,512]{2,1,0:T(8,128)(2,1)}), bf16[4,32,512]{2,1,0:T(8,128)(2,1)S(1)}, u32[]{:S(2)}, u32[]{:S(2)}) async-start(bf16[4,32,512]{2,1,0:T(8,128)(2,1)} %bitcast.4), calls=%async_computation.1 | async-start | bytes 262144 | tf_op jit(solution)/shard_map/all_to_all | solution.py:373
  35.0 0.7 %copy-start.7 = (bf16[288,512]{1,0:T(8,128)(2,1)}, bf16[288,512]{1,0:T(8,128)(2,1)S(1)}, u32[]{:S(2)}) copy-start(bf16[288,512]{1,0:T(8,128)(2,1)S(1)} %collective-permute-done.border_ref) | copy-start | bytes 884740
  35.8 12.3 %copy-start.1 = (bf16[2,512,512]{2,1,0:T(8,128)(2,1)S(1)}, bf16[2,512,512]{2,1,0:T(8,128)(2,1)}, u32[]{:S(2)}) copy-start(bf16[2,512,512]{2,1,0:T(8,128)(2,1)} %query_ref.1) | copy-start | bytes 3145732
  35.8 23.6 %copy-start.5 = (s32[2,512]{1,0:T(2,128)S(1)}, s32[2,512]{1,0:T(2,128)}, u32[]{:S(2)}) copy-start(s32[2,512]{1,0:T(2,128)} %token_ref.1) | copy-start | bytes 12292
  48.1 1.3 %copy-start = (bf16[1152,512]{1,0:T(8,128)(2,1)S(1)}, bf16[1152,512]{1,0:T(8,128)(2,1)}, u32[]{:S(2)}) copy-start(bf16[1152,512]{1,0:T(8,128)(2,1)} %local.1.base_ref) | copy-start | bytes 3538948
  49.3 15.8 %copy-start.2 = (f32[512]{0:T(512)S(1)}, f32[512]{0:T(512)}, u32[]{:S(2)}) copy-start(f32[512]{0:T(512)} %param.21) | copy-start | bytes 6148
  49.3 15.8 %copy-start.3 = (s32[2]{0:T(128)S(1)}, s32[2]{0:T(128)}, u32[]{:S(2)}) copy-start(s32[2]{0:T(128)} %refs_0_.1) | copy-start | bytes 28
  51.2 14.0 %all-to-all-start.2 = ((f32[16,1,1024]{2,1,0:T(1,128)}), f32[16,1,1024]{2,1,0:T(1,128)S(1)}, u32[]{:S(2)}, u32[]{:S(2)}) async-start(f32[16,1,1024]{2,1,0:T(1,128)} %get-tuple-element.15), calls=%async_computation.2 | async-start | bytes 131072 | tf_op jit(solution)/shard_map/all_to_all | solution.py:468
  59.4 1.0 %copy-start.4 = (bf16[512,512]{1,0:T(8,128)(2,1)S(1)}, bf16[512,512]{1,0:T(8,128)(2,1)}, u32[]{:S(2)}) copy-start(bf16[512,512]{1,0:T(8,128)(2,1)} %table_ref.1) | copy-start | bytes 1572868

commit v9 on v5

--- a/solution.py
+++ b/solution.py
@@ -428,7 +428,7 @@
         cost_estimate=pl.CostEstimate(
             flops=12_000_000_000, bytes_accessed=8 << 20, transcendentals=1 << 20
         ),
-        compiler_params=params(60),
+        compiler_params=params(48),
         name="local",
     )(
         before,

time: 67.7 us -> 67.8 us (level)
  Pallas kernels: 22 us -> 20.6 us
  local copies, waits for them, and re-layouts: 3.48 us -> 4.42 us
    pallas_call x1, Pallas kernels: 12.3 us -> 10.9 us  [per_device(): pl.pallas_call(local_kernel, grid=(tiles,), in_specs=[flat(border_rows),...]
    unnamed x17 -> x27, local copies, waits for them, and re-layouts: 3.12 us -> 4.06 us
  transfers between devices with their start and end apart: 4 -> 4, of which waited for: 2 -> 2; matrix products, arithmetic and copies ran while one was open for 1% -> 1% of each run, Pallas kernels for 21% -> 19%
where the time goes in v9:
time: 67.8 us; the launch traced here: 67.3 us
  starting transfers between devices  35 us (52%)
  Pallas kernels  20.6 us (30%)
  waiting for transfers between devices  7.04 us (10%)
  local copies, waits for them, and re-layouts  4.42 us (7%)
    all_to_all x2, starting transfers between devices, exchange(): lax.all_to_all(blocks, 'ctx', split_axis=0, concat_axis=0, axis_index_gro...  21.6 us
    pallas_call x1, Pallas kernels, per_device(): pl.pallas_call(local_kernel, grid=(tiles,), in_specs=[flat(border_rows),...  10.9 us
    all_to_all x1, starting transfers between devices, per_device(): shares = lax.all_to_all(sums, 'tp', split_axis=0, concat_axis=0, tiled=True)  8.55 us
    ppermute x1, starting transfers between devices, per_device(): lax.ppermute(border, 'ctx', [(i, i + 1) for i in range(chunks - 1)])  4.88 us
    pallas_call x1, Pallas kernels, per_device(): pl.pallas_call(states_step, in_specs=[anywhere, anywhere, anywhere], out_...  4.21 us
    unnamed x27, local copies, waits for them, and re-layouts  4.06 us
    all_to_all x1, waiting for transfers between devices, per_device(): shares = lax.all_to_all(sums, 'tp', split_axis=0, concat_axis=0, tiled=True)  3.7 us
    all_to_all x2, waiting for transfers between devices, exchange(): lax.all_to_all(blocks, 'ctx', split_axis=0, concat_axis=0, axis_index_gro...  3.34 us
  transfers between devices with their start and end apart: 4, of which 2 were waited for; matrix products, arithmetic and copies ran while one was open for 1% of the time, Pallas kernels for 19%

profile of v9, /device:TPU:1, one launch (start us, length us, event | category | flops | bytes accessed | tf_op | source)
XLA Modules:
  0.0 67.3 jit_solution(4293084902946430606)
XLA Ops:
  0.0 0.0 copy-start.3
  0.0 0.0 copy-start.1
  0.0 0.0 copy-start
  0.0 0.0 copy-start.12
  0.0 0.0 copy-start.10
  0.0 0.0 copy-start.9
  0.0 4.2 %states.1 = (bf16[256,512]{1,0:T(8,128)(2,1)}, bf16[320,512]{1,0:T(8,128)(2,1)}) custom-call(f32[16,32]{1,0:T(8,128)} %bitcast.11, bf16[2,512,512]{2,1,0:T(8,128)(2,1)} %key_ref.1, bf16[2,512,512]{2,1,0:T(8,128)(2,1)} %value_ref.1), custom_call_target="tpu_custom_call" | custom-call | tf_op jit(solution)/shard_map/states/pallas_call | solution.py:383
  4.3 8.9 %all-to-all-start = ((bf16[8,32,512]{2,1,0:T(8,128)(2,1)}), bf16[8,32,512]{2,1,0:T(8,128)(2,1)S(1)}, u32[]{:S(2)}, u32[]{:S(2)}) async-start(bf16[8,32,512]{2,1,0:T(8,128)(2,1)} %bitcast.17), calls=%async_computation | async-start | bytes 524288 | tf_op jit(solution)/shard_map/all_to_all | solution.py:372
  13.2 4.9 %collective-permute-start = (bf16[320,512]{1,0:T(8,128)(2,1)}, bf16[320,512]{1,0:T(8,128)(2,1)S(1)}, u32[]{:S(2)}, u32[]{:S(2)}) collective-permute-start(bf16[320,512]{1,0:T(8,128)(2,1)} %get-tuple-element.14), channel_id=1, source_target_pairs={{0,16},{16,32},{32,48},{48,64},{64,80},{80,96},{96,112},{112,128},... | collective-permute-start | bytes 983048 | tf_op jit(solution)/shard_map/ppermute | solution.py:404
  18.1 0.0 copy-done.3
  18.1 0.1 copy.13
  18.2 0.1 reshape.21.rate_ref
  18.2 0.1 broadcast_in_dim.3
  18.4 0.2 reshape.20.refs_1_
  18.5 3.3 %all-to-all-done = bf16[8,32,512]{2,1,0:T(8,128)(2,1)S(1)} async-done(((bf16[8,32,512]{2,1,0:T(8,128)(2,1)}), bf16[8,32,512]{2,1,0:T(8,128)(2,1)S(1)}, u32[]{:S(2)}, u32[]{:S(2)}) %all-to-all-start) | async-done | bytes 262176 | tf_op jit(solution)/shard_map/all_to_all | solution.py:372
  21.9 0.8 %group.1 = (bf16[128,512]{1,0:T(8,128)(2,1)}, f32[32,512]{1,0:T(8,128)S(1)}) custom-call(s32[1]{0:T(128)} %bitcast.refs_0_.refs_1_, f32[16,512]{1,0:T(8,128)S(1)} %reshape.20.refs_1_, bf16[256,512]{1,0:T(8,128)(2,1)S(1)} %bitcast.9), custom_call_target="tpu_custom_call" | custom-call | tf_op jit(solution)/shard_map/group/pallas_call | solution.py:446
  22.6 12.7 %all-to-all-start.1 = ((bf16[4,32,512]{2,1,0:T(8,128)(2,1)}), bf16[4,32,512]{2,1,0:T(8,128)(2,1)S(1)}, u32[]{:S(2)}, u32[]{:S(2)}) async-start(bf16[4,32,512]{2,1,0:T(8,128)(2,1)} %bitcast.4), calls=%async_computation.1 | async-start | bytes 262144 | tf_op jit(solution)/shard_map/all_to_all | solution.py:372
  35.3 0.0 collective-permute-done.border_ref
  35.3 0.0 copy-start.7
  35.3 0.7 %copy-done.7 = bf16[320,512]{1,0:T(8,128)(2,1)} copy-done((bf16[320,512]{1,0:T(8,128)(2,1)}, bf16[320,512]{1,0:T(8,128)(2,1)S(1)}, u32[]{:S(2)}) %copy-start.7) | copy-done | bytes 327704
  36.1 0.0 copy-done.1
  36.1 0.0 copy-done
  36.1 0.0 copy-done.12
  36.1 0.0 copy-done.10
  36.1 0.0 copy-done.9
  36.1 0.0 copy-start.8
  36.1 1.0 %copy-done.8 = bf16[320,512]{1,0:T(8,128)(2,1)S(1)} copy-done((bf16[320,512]{1,0:T(8,128)(2,1)S(1)}, bf16[320,512]{1,0:T(8,128)(2,1)}, u32[]{:S(2)}) %copy-start.8) | copy-done | bytes 327704
  37.1 0.0 copy-start.11
  37.1 10.9 %local.1.base_ref = bf16[1152,512]{1,0:T(8,128)(2,1)S(1)} custom-call(bf16[320,512]{1,0:T(8,128)(2,1)S(1)} %copy-done.8, bf16[2,512,512]{2,1,0:T(8,128)(2,1)S(1)} %copy-done, bf16[2,512,512]{2,1,0:T(8,128)(2,1)S(1)} %copy-done.1, bf16[32,128]{1,0:T(8,128)(2,1)S(1)} %copy-done.9, f32[16,32]{1,0:T(8,128)S(1)} %bitcast.13, f32[16,32]{1,0:T(8,128)S(1)} %bitcast.15, ...), custom_call_target="tpu_custom_call" | custom-call | flops 12000000000 | bytes 8388608 | tf_op jit(solution)/shard_map/local/pallas_call | solution.py:417
  47.9 0.0 all-to-all-done.1
  47.9 0.0 copy-start.2
  48.0 1.2 %copy-done.2 = bf16[2,512,512]{2,1,0:T(8,128)(2,1)S(1)} copy-done((bf16[2,512,512]{2,1,0:T(8,128)(2,1)S(1)}, bf16[2,512,512]{2,1,0:T(8,128)(2,1)}, u32[]{:S(2)}) %copy-start.2) | copy-done | bytes 1048600
  49.2 0.0 copy-start.4
  49.2 0.0 copy-start.5
  49.2 1.8 %gate.1 = (f32[2,512,512]{2,1,0:T(8,128)S(1)}, f32[16,1,1024]{2,1,0:T(1,128)}) custom-call(bf16[128,512]{1,0:T(8,128)(2,1)S(1)} %bitcast.10, f32[32,512]{1,0:T(8,128)S(1)} %get-tuple-element.13.own_ref, f32[1,512]{1,0:T(1,128)S(1)} %reshape.21.rate_ref, bf16[1152,512]{1,0:T(8,128)(2,1)S(1)} %local.1.base_ref, bf16[2,512,512]{2,1,0:T(8,128)(2,1)S(1)} %copy-done.2), custom_call_target="tpu_custom_call" | custom-call | tf_op jit(solution)/shard_map/gate/pallas_call | solution.py:455
  51.0 8.6 %all-to-all-start.2 = ((f32[16,1,1024]{2,1,0:T(1,128)}), f32[16,1,1024]{2,1,0:T(1,128)S(1)}, u32[]{:S(2)}, u32[]{:S(2)}) async-start(f32[16,1,1024]{2,1,0:T(1,128)} %get-tuple-element.15), calls=%async_computation.2 | async-start | bytes 131072 | tf_op jit(solution)/shard_map/all_to_all | solution.py:467
  59.5 0.0 copy-done.11
  59.5 0.0 copy-start.6
  59.5 1.0 %copy-done.6 = bf16[512,512]{1,0:T(8,128)(2,1)S(1)} copy-done((bf16[512,512]{1,0:T(8,128)(2,1)S(1)}, bf16[512,512]{1,0:T(8,128)(2,1)}, u32[]{:S(2)}) %copy-start.6) | copy-done | bytes 524312
  60.6 1.1 %embed.1.refs_4_ = bf16[2,512,512]{2,1,0:T(8,128)(2,1)S(1)} custom-call(s32[2,512]{1,0:T(2,128)S(1)} %copy-done.11, bf16[512,512]{1,0:T(8,128)(2,1)S(1)} %copy-done.6), custom_call_target="tpu_custom_call" | custom-call | flops 536870912 | bytes 4194304 | tf_op jit(solution)/shard_map/embed/pallas_call | solution.py:407
  61.6 3.7 %all-to-all-done.2.refs_2_ = f32[16,1,1024]{2,1,0:T(1,128)S(1)} async-done(((f32[16,1,1024]{2,1,0:T(1,128)}), f32[16,1,1024]{2,1,0:T(1,128)S(1)}, u32[]{:S(2)}, u32[]{:S(2)}) %all-to-all-start.2) | async-done | bytes 65568 | tf_op jit(solution)/shard_map/all_to_all | solution.py:467
  65.3 0.0 copy-done.4
  65.3 0.0 copy-done.5
  65.4 1.9 %norm.1 = bf16[2,512,512]{2,1,0:T(8,128)(2,1)} custom-call(s32[2]{0:T(128)S(1)} %copy-done.5, s32[1]{0:T(128)} %bitcast.refs_0_.refs_1_, f32[16,1,1024]{2,1,0:T(1,128)S(1)} %all-to-all-done.2.refs_2_, f32[2,512,512]{2,1,0:T(8,128)S(1)} %get-tuple-element.16.refs_3_, bf16[2,512,512]{2,1,0:T(8,128)(2,1)S(1)} %embed.1.refs_4_, f32[1,512]{1,0:T(1,128)S(1)} %bitcast.14), custom_call_target="tpu_custom_call" | custom-call | tf_op jit(solution)/shard_map/norm/pallas_call | solution.py:472
Async XLA Ops:
  0.0 18.1 %copy-start.3 = (f32[32,16]{0,1:T(8,128)S(1)}, f32[32,16]{0,1:T(8,128)}, u32[]{:S(2)}) copy-start(f32[32,16]{0,1:T(8,128)} %param.18) | copy-start | bytes 6148
  0.0 36.1 %copy-start.1 = (bf16[2,512,512]{2,1,0:T(8,128)(2,1)S(1)}, bf16[2,512,512]{2,1,0:T(8,128)(2,1)}, u32[]{:S(2)}) copy-start(bf16[2,512,512]{2,1,0:T(8,128)(2,1)} %value_ref.1) | copy-start | bytes 3145732
  0.0 36.1 %copy-start = (bf16[2,512,512]{2,1,0:T(8,128)(2,1)S(1)}, bf16[2,512,512]{2,1,0:T(8,128)(2,1)}, u32[]{:S(2)}) copy-start(bf16[2,512,512]{2,1,0:T(8,128)(2,1)} %key_ref.1) | copy-start | bytes 3145732
  0.0 36.1 %copy-start.12 = (f32[512]{0:T(512)S(1)}, f32[512]{0:T(512)}, u32[]{:S(2)}) copy-start(f32[512]{0:T(512)} %param.20) | copy-start | bytes 6148
  0.0 36.0 %copy-start.10 = (f32[32,16]{0,1:T(8,128)S(1)}, f32[32,16]{0,1:T(8,128)}, u32[]{:S(2)}) copy-start(f32[32,16]{0,1:T(8,128)} %param.19) | copy-start | bytes 6148
  0.0 36.0 %copy-start.9 = (bf16[32,128]{1,0:T(8,128)(2,1)S(1)}, bf16[32,128]{1,0:T(8,128)(2,1)}, u32[]{:S(2)}) copy-start(bf16[32,128]{1,0:T(8,128)(2,1)} %filter_ref.1) | copy-start | bytes 24580
  4.3 17.6 %all-to-all-start = ((bf16[8,32,512]{2,1,0:T(8,128)(2,1)}), bf16[8,32,512]{2,1,0:T(8,128)(2,1)S(1)}, u32[]{:S(2)}, u32[]{:S(2)}) async-start(bf16[8,32,512]{2,1,0:T(8,128)(2,1)} %bitcast.17), calls=%async_computation | async-start | bytes 524288 | tf_op jit(solution)/shard_map/all_to_all | solution.py:372
  13.2 22.1 %collective-permute-start = (bf16[320,512]{1,0:T(8,128)(2,1)}, bf16[320,512]{1,0:T(8,128)(2,1)S(1)}, u32[]{:S(2)}, u32[]{:S(2)}) collective-permute-start(bf16[320,512]{1,0:T(8,128)(2,1)} %get-tuple-element.14), channel_id=1, source_target_pairs={{0,16},{16,32},{32,48},{48,64},{64,80},{80,96},{96,112},{112,128},... | collective-permute-start | bytes 983048 | tf_op jit(solution)/shard_map/ppermute | solution.py:404
  22.6 25.3 %all-to-all-start.1 = ((bf16[4,32,512]{2,1,0:T(8,128)(2,1)}), bf16[4,32,512]{2,1,0:T(8,128)(2,1)S(1)}, u32[]{:S(2)}, u32[]{:S(2)}) async-start(bf16[4,32,512]{2,1,0:T(8,128)(2,1)} %bitcast.4), calls=%async_computation.1 | async-start | bytes 262144 | tf_op jit(solution)/shard_map/all_to_all | solution.py:372
  35.3 0.7 %copy-start.7 = (bf16[320,512]{1,0:T(8,128)(2,1)}, bf16[320,512]{1,0:T(8,128)(2,1)S(1)}, u32[]{:S(2)}) copy-start(bf16[320,512]{1,0:T(8,128)(2,1)S(1)} %collective-permute-done.border_ref) | copy-start | bytes 983044
  36.1 1.0 %copy-start.8 = (bf16[320,512]{1,0:T(8,128)(2,1)S(1)}, bf16[320,512]{1,0:T(8,128)(2,1)}, u32[]{:S(2)}) copy-start(bf16[320,512]{1,0:T(8,128)(2,1)} %copy-done.7) | copy-start | bytes 983044
  37.1 22.5 %copy-start.11 = (s32[2,512]{1,0:T(2,128)S(1)}, s32[2,512]{1,0:T(2,128)}, u32[]{:S(2)}) copy-start(s32[2,512]{1,0:T(2,128)} %token_ref.1) | copy-start | bytes 12292
  47.9 1.2 %copy-start.2 = (bf16[2,512,512]{2,1,0:T(8,128)(2,1)S(1)}, bf16[2,512,512]{2,1,0:T(8,128)(2,1)}, u32[]{:S(2)}) copy-start(bf16[2,512,512]{2,1,0:T(8,128)(2,1)} %query_ref.1) | copy-start | bytes 3145732
  49.2 16.2 %copy-start.4 = (f32[512]{0:T(512)S(1)}, f32[512]{0:T(512)}, u32[]{:S(2)}) copy-start(f32[512]{0:T(512)} %param.21) | copy-start | bytes 6148
  49.2 16.2 %copy-start.5 = (s32[2]{0:T(128)S(1)}, s32[2]{0:T(128)}, u32[]{:S(2)}) copy-start(s32[2]{0:T(128)} %refs_0_.1) | copy-start | bytes 28
  51.0 14.4 %all-to-all-start.2 = ((f32[16,1,1024]{2,1,0:T(1,128)}), f32[16,1,1024]{2,1,0:T(1,128)S(1)}, u32[]{:S(2)}, u32[]{:S(2)}) async-start(f32[16,1,1024]{2,1,0:T(1,128)} %get-tuple-element.15), calls=%async_computation.2 | async-start | bytes 131072 | tf_op jit(solution)/shard_map/all_to_all | solution.py:467
  59.5 1.0 %copy-start.6 = (bf16[512,512]{1,0:T(8,128)(2,1)S(1)}, bf16[512,512]{1,0:T(8,128)(2,1)}, u32[]{:S(2)}) copy-start(bf16[512,512]{1,0:T(8,128)(2,1)} %table_ref.1) | copy-start | bytes 1572868

commit v10 on v5

--- a/solution.py
+++ b/solution.py
@@ -283,7 +283,7 @@
             carry = dot(after, jnp.concatenate([upper, upper, lower], axis=0))
             base = base_ref[s * rows : (s + 1) * rows, lanes].astype(F32)
             gated = query_ref[s, :, lanes].astype(F32) * (base + carry)
-            gated_ref[s, :, lanes] = gated
+            gated_ref[s, :, lanes] = gated.astype(BF16)
             if tile == 0:
                 squares[s] = gated * gated
             else:
@@ -309,7 +309,7 @@
             start = index_ref[0] * rows + part * here
             valid = start + iota((here, 1), 0) < length_ref[s]
             first = s * rows + part * here
-            value = gated_ref[s, at, :] * scale[first : first + here] * gain_ref[...]
+            value = gated_ref[s, at, :].astype(F32) * scale[first : first + here] * gain_ref[...]
             value = value + embed_ref[s, at, :].astype(F32)
             out_ref[s, at, :] = jnp.where(valid, value, 0.0).astype(BF16)
             store = pltpu.make_async_copy(
@@ -455,7 +455,7 @@
     gated, sums = pl.pallas_call(
         gate_kernel,
         out_shape=[
-            shape((samples, rows, width), F32),
+            shape((samples, rows, width), BF16),
             shape((columns, 1, samples * rows), F32),
         ],
         scratch_shapes=[

time: 67.7 us -> 67.9 us (level)
  waiting for transfers between devices: 7.05 us -> 8.08 us
  local copies, waits for them, and re-layouts: 3.48 us -> 2.45 us
    all_to_all x1, waiting for transfers between devices: 3.71 us -> 4.74 us  [per_device(): shares = lax.all_to_all(sums, 'tp', split_axis=0, concat_axis=0, tiled=True)]
    unnamed x17, local copies, waits for them, and re-layouts: 3.12 us -> 2.08 us
where the time goes in v10:
time: 67.9 us; the launch traced here: 67.4 us
  starting transfers between devices  34.8 us (51%)
  Pallas kernels  22.1 us (33%)
  waiting for transfers between devices  8.08 us (12%)
  local copies, waits for them, and re-layouts  2.45 us (4%)
    all_to_all x2, starting transfers between devices, exchange(): lax.all_to_all(blocks, 'ctx', split_axis=0, concat_axis=0, axis_index_gro...  21.6 us
    pallas_call x1, Pallas kernels, per_device(): pl.pallas_call(local_kernel, grid=(tiles,), in_specs=[flat(border_rows),...  12.3 us
    all_to_all x1, starting transfers between devices, per_device(): shares = lax.all_to_all(sums, 'tp', split_axis=0, concat_axis=0, tiled=True)  8.29 us
    ppermute x1, starting transfers between devices, per_device(): lax.ppermute(border, 'ctx', [(i, i + 1) for i in range(chunks - 1)])  4.88 us
    all_to_all x1, waiting for transfers between devices, per_device(): shares = lax.all_to_all(sums, 'tp', split_axis=0, concat_axis=0, tiled=True)  4.74 us
    pallas_call x1, Pallas kernels, per_device(): pl.pallas_call(states_step, in_specs=[anywhere, anywhere, anywhere], out_...  4.08 us
    all_to_all x2, waiting for transfers between devices, exchange(): lax.all_to_all(blocks, 'ctx', split_axis=0, concat_axis=0, axis_index_gro...  3.34 us
    unnamed x17, local copies, waits for them, and re-layouts  2.08 us
  transfers between devices with their start and end apart: 4, of which 2 were waited for; matrix products, arithmetic and copies ran while one was open for 1% of the time, Pallas kernels for 21%

profile of v10, /device:TPU:1, one launch (start us, length us, event | category | flops | bytes accessed | tf_op | source)
XLA Modules:
  0.0 67.4 jit_solution(11161627736772582561)
XLA Ops:
  0.0 0.0 copy-start.6
  0.0 4.1 %states.1 = (bf16[256,512]{1,0:T(8,128)(2,1)}, bf16[320,512]{1,0:T(8,128)(2,1)}) custom-call(f32[16,32]{1,0:T(8,128)} %bitcast.13, bf16[2,512,512]{2,1,0:T(8,128)(2,1)} %key_ref.1, bf16[2,512,512]{2,1,0:T(8,128)(2,1)} %value_ref.1), custom_call_target="tpu_custom_call" | custom-call | tf_op jit(solution)/shard_map/states/pallas_call | solution.py:383
  4.1 8.9 %all-to-all-start = ((bf16[8,32,512]{2,1,0:T(8,128)(2,1)}), bf16[8,32,512]{2,1,0:T(8,128)(2,1)S(1)}, u32[]{:S(2)}, u32[]{:S(2)}) async-start(bf16[8,32,512]{2,1,0:T(8,128)(2,1)} %bitcast.12), calls=%async_computation | async-start | bytes 524288 | tf_op jit(solution)/shard_map/all_to_all | solution.py:372
  13.0 4.9 %collective-permute-start = (bf16[320,512]{1,0:T(8,128)(2,1)}, bf16[320,512]{1,0:T(8,128)(2,1)S(1)}, u32[]{:S(2)}, u32[]{:S(2)}) collective-permute-start(bf16[320,512]{1,0:T(8,128)(2,1)} %get-tuple-element.14), channel_id=1, source_target_pairs={{0,16},{16,32},{32,48},{48,64},{64,80},{80,96},{96,112},{112,128},... | collective-permute-start | bytes 983048 | tf_op jit(solution)/shard_map/ppermute | solution.py:404
  17.9 0.0 copy-done.6
  17.9 0.1 copy.13
  18.0 0.1 reshape.21.rate_ref
  18.1 0.1 broadcast_in_dim.3
  18.2 0.2 reshape.20.refs_1_
  18.4 3.3 %all-to-all-done = bf16[8,32,512]{2,1,0:T(8,128)(2,1)S(1)} async-done(((bf16[8,32,512]{2,1,0:T(8,128)(2,1)}), bf16[8,32,512]{2,1,0:T(8,128)(2,1)S(1)}, u32[]{:S(2)}, u32[]{:S(2)}) %all-to-all-start) | async-done | bytes 262176 | tf_op jit(solution)/shard_map/all_to_all | solution.py:372
  21.7 0.8 %group.1 = (bf16[128,512]{1,0:T(8,128)(2,1)}, f32[32,512]{1,0:T(8,128)S(1)}) custom-call(s32[1]{0:T(128)} %bitcast.refs_0_.refs_1_, f32[16,512]{1,0:T(8,128)S(1)} %reshape.20.refs_1_, bf16[256,512]{1,0:T(8,128)(2,1)S(1)} %bitcast.9), custom_call_target="tpu_custom_call" | custom-call | tf_op jit(solution)/shard_map/group/pallas_call | solution.py:446
  22.5 12.7 %all-to-all-start.1 = ((bf16[4,32,512]{2,1,0:T(8,128)(2,1)}), bf16[4,32,512]{2,1,0:T(8,128)(2,1)S(1)}, u32[]{:S(2)}, u32[]{:S(2)}) async-start(bf16[4,32,512]{2,1,0:T(8,128)(2,1)} %bitcast.4), calls=%async_computation.1 | async-start | bytes 262144 | tf_op jit(solution)/shard_map/all_to_all | solution.py:372
  35.2 0.0 collective-permute-done.border_ref
  35.2 0.0 copy-start.7
  35.2 0.7 %copy-done.7 = bf16[320,512]{1,0:T(8,128)(2,1)} copy-done((bf16[320,512]{1,0:T(8,128)(2,1)}, bf16[320,512]{1,0:T(8,128)(2,1)S(1)}, u32[]{:S(2)}) %copy-start.7) | copy-done | bytes 327704
  35.9 0.0 copy-start.1
  35.9 12.3 %local.1.base_ref = bf16[1152,512]{1,0:T(8,128)(2,1)} custom-call(bf16[320,512]{1,0:T(8,128)(2,1)} %copy-done.7, bf16[2,512,512]{2,1,0:T(8,128)(2,1)} %key_ref.1, bf16[2,512,512]{2,1,0:T(8,128)(2,1)} %value_ref.1, bf16[32,128]{1,0:T(8,128)(2,1)} %filter_ref.1, f32[16,32]{1,0:T(8,128)} %bitcast.14, f32[16,32]{1,0:T(8,128)} %bitcast.16, f32[1,512]{1,0:T(1,128)} %bitcast.17), custom_call_target="tpu_custom_call" | custom-call | flops 12000000000 | bytes 8388608 | tf_op jit(solution)/shard_map/local/pallas_call | solution.py:417
  48.2 0.0 all-to-all-done.1
  48.2 0.0 copy-done.1
  48.2 0.0 copy-start
  48.2 1.3 %copy-done = bf16[1152,512]{1,0:T(8,128)(2,1)S(1)} copy-done((bf16[1152,512]{1,0:T(8,128)(2,1)S(1)}, bf16[1152,512]{1,0:T(8,128)(2,1)}, u32[]{:S(2)}) %copy-start) | copy-done | bytes 1179672
  49.5 0.0 copy-start.4
  49.5 0.0 copy-start.5
  49.5 1.9 %gate.1 = (bf16[2,512,512]{2,1,0:T(8,128)(2,1)S(1)}, f32[16,1,1024]{2,1,0:T(1,128)}) custom-call(bf16[128,512]{1,0:T(8,128)(2,1)S(1)} %bitcast.10, f32[32,512]{1,0:T(8,128)S(1)} %get-tuple-element.13.own_ref, f32[1,512]{1,0:T(1,128)S(1)} %reshape.21.rate_ref, bf16[1152,512]{1,0:T(8,128)(2,1)S(1)} %copy-done, bf16[2,512,512]{2,1,0:T(8,128)(2,1)S(1)} %copy-done.1), custom_call_target="tpu_custom_call" | custom-call | tf_op jit(solution)/shard_map/gate/pallas_call | solution.py:455
  51.3 0.0 copy-start.2
  51.3 0.0 copy-start.3
  51.3 8.3 %all-to-all-start.2 = ((f32[16,1,1024]{2,1,0:T(1,128)}), f32[16,1,1024]{2,1,0:T(1,128)S(1)}, u32[]{:S(2)}, u32[]{:S(2)}) async-start(f32[16,1,1024]{2,1,0:T(1,128)} %get-tuple-element.15), calls=%async_computation.2 | async-start | bytes 131072 | tf_op jit(solution)/shard_map/all_to_all | solution.py:467
  59.6 0.0 copy-done.4
  59.6 0.0 copy-done.5
  59.6 1.1 %embed.1.refs_4_ = bf16[2,512,512]{2,1,0:T(8,128)(2,1)S(1)} custom-call(s32[2,512]{1,0:T(2,128)S(1)} %copy-done.5, bf16[512,512]{1,0:T(8,128)(2,1)S(1)} %copy-done.4), custom_call_target="tpu_custom_call" | custom-call | flops 536870912 | bytes 4194304 | tf_op jit(solution)/shard_map/embed/pallas_call | solution.py:407
  60.7 4.7 %all-to-all-done.2.refs_2_ = f32[16,1,1024]{2,1,0:T(1,128)S(1)} async-done(((f32[16,1,1024]{2,1,0:T(1,128)}), f32[16,1,1024]{2,1,0:T(1,128)S(1)}, u32[]{:S(2)}, u32[]{:S(2)}) %all-to-all-start.2) | async-done | bytes 65568 | tf_op jit(solution)/shard_map/all_to_all | solution.py:467
  65.4 0.0 copy-done.2
  65.4 0.0 copy-done.3
  65.4 2.0 %norm.1 = bf16[2,512,512]{2,1,0:T(8,128)(2,1)} custom-call(s32[2]{0:T(128)S(1)} %copy-done.3, s32[1]{0:T(128)} %bitcast.refs_0_.refs_1_, f32[16,1,1024]{2,1,0:T(1,128)S(1)} %all-to-all-done.2.refs_2_, bf16[2,512,512]{2,1,0:T(8,128)(2,1)S(1)} %get-tuple-element.16.refs_3_, bf16[2,512,512]{2,1,0:T(8,128)(2,1)S(1)} %embed.1.refs_4_, f32[1,512]{1,0:T(1,128)S(1)} %bitcast.11), custom_call_target="tpu_custom_call" | custom-call | tf_op jit(solution)/shard_map/norm/pallas_call | solution.py:472
Async XLA Ops:
  0.0 17.9 %copy-start.6 = (f32[32,16]{0,1:T(8,128)S(1)}, f32[32,16]{0,1:T(8,128)}, u32[]{:S(2)}) copy-start(f32[32,16]{0,1:T(8,128)} %param.18) | copy-start | bytes 6148
  4.1 17.6 %all-to-all-start = ((bf16[8,32,512]{2,1,0:T(8,128)(2,1)}), bf16[8,32,512]{2,1,0:T(8,128)(2,1)S(1)}, u32[]{:S(2)}, u32[]{:S(2)}) async-start(bf16[8,32,512]{2,1,0:T(8,128)(2,1)} %bitcast.12), calls=%async_computation | async-start | bytes 524288 | tf_op jit(solution)/shard_map/all_to_all | solution.py:372
  13.0 22.1 %collective-permute-start = (bf16[320,512]{1,0:T(8,128)(2,1)}, bf16[320,512]{1,0:T(8,128)(2,1)S(1)}, u32[]{:S(2)}, u32[]{:S(2)}) collective-permute-start(bf16[320,512]{1,0:T(8,128)(2,1)} %get-tuple-element.14), channel_id=1, source_target_pairs={{0,16},{16,32},{32,48},{48,64},{64,80},{80,96},{96,112},{112,128},... | collective-permute-start | bytes 983048 | tf_op jit(solution)/shard_map/ppermute | solution.py:404
  22.5 25.7 %all-to-all-start.1 = ((bf16[4,32,512]{2,1,0:T(8,128)(2,1)}), bf16[4,32,512]{2,1,0:T(8,128)(2,1)S(1)}, u32[]{:S(2)}, u32[]{:S(2)}) async-start(bf16[4,32,512]{2,1,0:T(8,128)(2,1)} %bitcast.4), calls=%async_computation.1 | async-start | bytes 262144 | tf_op jit(solution)/shard_map/all_to_all | solution.py:372
  35.2 0.7 %copy-start.7 = (bf16[320,512]{1,0:T(8,128)(2,1)}, bf16[320,512]{1,0:T(8,128)(2,1)S(1)}, u32[]{:S(2)}) copy-start(bf16[320,512]{1,0:T(8,128)(2,1)S(1)} %collective-permute-done.border_ref) | copy-start | bytes 983044
  35.9 12.3 %copy-start.1 = (bf16[2,512,512]{2,1,0:T(8,128)(2,1)S(1)}, bf16[2,512,512]{2,1,0:T(8,128)(2,1)}, u32[]{:S(2)}) copy-start(bf16[2,512,512]{2,1,0:T(8,128)(2,1)} %query_ref.1) | copy-start | bytes 3145732
  48.2 1.3 %copy-start = (bf16[1152,512]{1,0:T(8,128)(2,1)S(1)}, bf16[1152,512]{1,0:T(8,128)(2,1)}, u32[]{:S(2)}) copy-start(bf16[1152,512]{1,0:T(8,128)(2,1)} %local.1.base_ref) | copy-start | bytes 3538948
  49.5 10.2 %copy-start.4 = (bf16[512,512]{1,0:T(8,128)(2,1)S(1)}, bf16[512,512]{1,0:T(8,128)(2,1)}, u32[]{:S(2)}) copy-start(bf16[512,512]{1,0:T(8,128)(2,1)} %table_ref.1) | copy-start | bytes 1572868
  49.5 10.2 %copy-start.5 = (s32[2,512]{1,0:T(2,128)S(1)}, s32[2,512]{1,0:T(2,128)}, u32[]{:S(2)}) copy-start(s32[2,512]{1,0:T(2,128)} %token_ref.1) | copy-start | bytes 12292
  51.3 14.1 %copy-start.2 = (f32[512]{0:T(512)S(1)}, f32[512]{0:T(512)}, u32[]{:S(2)}) copy-start(f32[512]{0:T(512)} %param.21) | copy-start | bytes 6148
  51.3 14.1 %copy-start.3 = (s32[2]{0:T(128)S(1)}, s32[2]{0:T(128)}, u32[]{:S(2)}) copy-start(s32[2]{0:T(128)} %refs_0_.1) | copy-start | bytes 28
  51.3 14.1 %all-to-all-start.2 = ((f32[16,1,1024]{2,1,0:T(1,128)}), f32[16,1,1024]{2,1,0:T(1,128)S(1)}, u32[]{:S(2)}, u32[]{:S(2)}) async-start(f32[16,1,1024]{2,1,0:T(1,128)} %get-tuple-element.15), calls=%async_computation.2 | async-start | bytes 131072 | tf_op jit(solution)/shard_map/all_to_all | solution.py:467
